TPU v7x, 32 devices: a whole 2x2x4 slice. The times are simulated.
32 devices in a mesh: dp: 4 (over y, x), expert: 8 (over z, core).
Axes of the slice: x: 2, y: 2, z: 4, core: 2. Of those that a mesh axis runs over, the one named last changes fastest.
Arguments:
- tokens: bfloat16 [4096, 3584], P(('dp', 'expert')), may hold values from -6 to 6
- cotangent: bfloat16 [4096, 3584], P(('dp', 'expert')), may hold values from -6 to 6
- route_weight: float32 [4096, 8], P(('dp', 'expert')), may hold values from 0.05 to 0.5
- expert_ids: int32 [4096, 8], P(('dp', 'expert')), may hold values from 0 to 255, as said below
- live_tokens: int32 [32], P(('dp', 'expert')), may hold values from 1 to 128, 3072 in all
- replica_plan: int32 [32, 1], P(('dp', 'expert')), may hold values 0 or 1
- w_gate: bfloat16 [3584, 2048], P('dp', 'expert'), may hold values from -0.09375 to 0.09375
- w_up: bfloat16 [3584, 2048], P('dp', 'expert'), may hold values from -0.09375 to 0.09375
- w_down: bfloat16 [2048, 3584], P('expert', 'dp'), may hold values from -0.125 to 0.125
- scale_gate: float32 [28, 16], P(None, 'expert'), may hold values from 0.5 to 2
- scale_up: float32 [28, 16], P(None, 'expert'), may hold values from 0.5 to 2
- scale_down: float32 [16, 28], P('expert'), may hold values from 0.5 to 2
Outputs:
- d_tokens: bfloat16 [4096, 3584], P(('dp', 'expert'))
- grad_gate: bfloat16 [3584, 2048], P('dp', 'expert')
- grad_up: bfloat16 [3584, 2048], P('dp', 'expert')
- grad_down: bfloat16 [2048, 3584], P('expert', 'dp')
Inputs may be any that keep to these rules, and one draw needn't show every extreme that they name: `expert_ids`: the 8 ids of one token are distinct.
All inputs are finite; a program needn't handle non-finite values. No bound on the sum of `live_tokens` or of `replica_plan` on one device may be relied on, other than what follows from the above.
Results may differ from a plain program's by a relative error of at most 0.012.
Values may be sent and summed in bfloat16 or wider, within the bound.
No kernel may reach another device: no remote copies, remote signals or barrier semaphores. Data moves between devices by JAX's collectives and lax.ppermute only.
A program may use at most 64 MiB of HBM per device.

v0:
```python
import jax
import jax.numpy as jnp
from jax import lax
from jax.sharding import PartitionSpec as P

HSH = 8
CAP = 4


def dequantize(values, scale):
    block_rows = values.shape[0] // scale.shape[0]
    block_cols = values.shape[1] // scale.shape[1]
    spread = jnp.repeat(jnp.repeat(scale, block_rows, axis=0), block_cols, axis=1)
    return (values.astype(jnp.float32) * spread).astype(jnp.bfloat16)


def route_rows(tokens, cotangent, route_weight, expert_ids, live_count, plan, experts, capacity):
    count = tokens.shape[0]
    token_index = jnp.arange(count, dtype=jnp.int32)
    expert_index = jnp.arange(experts, dtype=jnp.int32)
    matches = expert_ids[:, None, :] == expert_index[None, :, None]
    routed = jnp.any(matches, axis=2) & (token_index < live_count)[:, None]
    to_replica = (token_index % 2 == 1)[:, None] & (plan[None, :] == 1)
    in_lists = jnp.stack([routed & ~to_replica, routed & to_replica], axis=2).astype(jnp.int32)
    position = jnp.cumsum(in_lists, axis=0) - 1
    capacity_index = jnp.arange(capacity, dtype=jnp.int32)
    selected = ((in_lists[..., None] == 1) & (position[..., None] == capacity_index)).astype(
        jnp.float32
    )
    weight_sum = jnp.sum(jnp.where(matches, route_weight[:, None, :], jnp.float32(0.0)), axis=2)
    row_weight = jnp.sum(selected * weight_sum[:, :, None, None], axis=0)
    flat = selected.reshape(count, -1)
    picker = flat.T.astype(jnp.bfloat16)
    token_rows = jnp.dot(picker, tokens, preferred_element_type=jnp.float32).astype(jnp.bfloat16)
    cot_picked = jnp.dot(picker, cotangent, preferred_element_type=jnp.float32)
    cot_rows = (row_weight.reshape(-1, 1) * cot_picked).astype(jnp.bfloat16)
    shape = (experts, 2, capacity, tokens.shape[1])
    return (flat, token_rows.reshape(shape), cot_rows.reshape(shape))


def expert_terms(token_rows, cot_rows, gate_w, up_w, down_w):
    by_hidden = (((1,), (1,)), ((), ()))
    by_rows = (((0,), (0,)), ((), ()))
    gate_pre = jnp.dot(token_rows, gate_w, preferred_element_type=jnp.float32)
    up_pre = jnp.dot(token_rows, up_w, preferred_element_type=jnp.float32)
    gate_sig = jax.nn.sigmoid(gate_pre)
    swish = gate_pre * gate_sig
    d_hidden = lax.dot_general(cot_rows, down_w, by_hidden, preferred_element_type=jnp.float32)
    hidden = (swish * up_pre).astype(jnp.bfloat16)
    d_up = (d_hidden * swish).astype(jnp.bfloat16)
    d_gate = (d_hidden * up_pre * gate_sig * (1.0 + gate_pre * (1.0 - gate_sig))).astype(
        jnp.bfloat16
    )
    grad_g = lax.dot_general(
        token_rows, d_gate, by_rows, preferred_element_type=jnp.float32
    ).astype(jnp.bfloat16)
    grad_u = lax.dot_general(token_rows, d_up, by_rows, preferred_element_type=jnp.float32).astype(
        jnp.bfloat16
    )
    grad_d = lax.dot_general(cot_rows, hidden, by_rows, preferred_element_type=jnp.float32).astype(
        jnp.bfloat16
    )
    dx_part = lax.dot_general(d_gate, gate_w, by_hidden, preferred_element_type=jnp.float32)
    dx_part = dx_part + lax.dot_general(d_up, up_w, by_hidden, preferred_element_type=jnp.float32)
    return (grad_g, grad_u, grad_d, dx_part.astype(jnp.bfloat16))


def fan_out(rows, members):
    slot_count = rows.shape[0]
    spread = jnp.broadcast_to(rows[:, None], (slot_count, members // slot_count) + rows.shape[1:])
    return spread.reshape((members,) + rows.shape[1:])


def send_rows(token_rows, cot_rows, members):
    return (
        lax.all_to_all(
            fan_out(token_rows, members), "expert", split_axis=0, concat_axis=0, tiled=True
        ),
        lax.all_to_all(
            fan_out(cot_rows, members), "expert", split_axis=0, concat_axis=0, tiled=True
        ),
    )


def on_device(
    tokens,
    cotangent,
    route_weight,
    expert_ids,
    live_tokens,
    replica_plan,
    w_gate,
    w_up,
    w_down,
    scale_gate,
    scale_up,
    scale_down,
):
    members = lax.axis_size("expert")
    groups = lax.axis_size("dp")
    slot_count = members // HSH
    width = tokens.shape[1]
    flat, token_rows, cot_rows = route_rows(
        tokens,
        cotangent,
        route_weight,
        expert_ids,
        live_tokens[0],
        replica_plan[0],
        slot_count,
        CAP,
    )
    gathered = (
        lax.all_gather(w_gate, "dp", axis=0, tiled=True),
        lax.all_gather(w_up, "dp", axis=0, tiled=True),
        lax.all_gather(w_down, "dp", axis=1, tiled=True),
    )
    full_gate, full_up, full_down = gathered
    recv_tokens, recv_cots = send_rows(token_rows, cot_rows, members)
    own_gate = dequantize(full_gate, scale_gate)
    own_up = dequantize(full_up, scale_up)
    own_down = dequantize(full_down, scale_down)
    leading = expert_terms(
        recv_tokens[:, 0].reshape(-1, width),
        recv_cots[:, 0].reshape(-1, width),
        own_gate,
        own_up,
        own_down,
    )
    trailing = expert_terms(
        recv_tokens[:, 1].reshape(-1, width),
        recv_cots[:, 1].reshape(-1, width),
        own_gate,
        own_up,
        own_down,
    )
    dx_parts = jnp.stack(
        [leading[3].reshape(members, CAP, width), trailing[3].reshape(members, CAP, width)], axis=1
    )
    returned = lax.all_to_all(dx_parts, "expert", split_axis=0, concat_axis=0, tiled=True)
    summed = jnp.sum(returned.astype(jnp.float32).reshape(slot_count, HSH, 2, CAP, width), axis=1)
    sum_gate = (leading[0].astype(jnp.float32) + trailing[0].astype(jnp.float32)).astype(
        jnp.bfloat16
    )
    sum_up = (leading[1].astype(jnp.float32) + trailing[1].astype(jnp.float32)).astype(jnp.bfloat16)
    sum_down = (leading[2].astype(jnp.float32) + trailing[2].astype(jnp.float32)).astype(
        jnp.bfloat16
    )
    stacked = jnp.stack([sum_gate, sum_up, sum_down], axis=0)
    received = lax.all_to_all(stacked, "dp", split_axis=1, concat_axis=0, tiled=True)
    rows_here = received.shape[1]
    totals = jnp.sum(received.astype(jnp.float32).reshape(groups, 3, rows_here, -1), axis=0)
    totals = totals.astype(jnp.bfloat16)
    d_tokens = jnp.dot(flat, summed.reshape(-1, width), precision=lax.Precision.HIGHEST).astype(
        jnp.bfloat16
    )
    return (d_tokens, totals[0], totals[1], totals[2].T)


def solution(mesh):
    return jax.shard_map(
        on_device,
        mesh=mesh,
        in_specs=(
            P(("dp", "expert"), None),
            P(("dp", "expert"), None),
            P(("dp", "expert"), None),
            P(("dp", "expert"), None),
            P(("dp", "expert")),
            P(("dp", "expert"), None),
            P("dp", "expert"),
            P("dp", "expert"),
            P("expert", "dp"),
            P(None, "expert"),
            P(None, "expert"),
            P("expert", None),
        ),
        out_specs=(
            P(("dp", "expert"), None),
            P("dp", "expert"),
            P("dp", "expert"),
            P("expert", "dp"),
        ),
        check_vma=False,
    )
```

profile of v0, /device:TPU:0, one launch (start us, length us, event | category | flops | bytes accessed | tf_op | source)
XLA Modules:
  0.0 279.2 jit_solution(3513891874383219620)
XLA Ops:
  7.2 0.7 all-gather.8.cloned.1.call-update
  8.0 0.7 all-gather.6.cloned.1.call-update
  10.1 0.7 select_reduce_fusion.1
  11.3 0.3 convolution_convert_fusion.6
  11.6 0.9 reshape.222
  12.5 6.3 %all-to-all-start.1 = ((bf16[8,2,4,3584]{3,2,1,0:T(4,128)(2,1)}), bf16[8,2,4,3584]{3,2,1,0:T(4,128)(2,1)S(1)}, u32[]{:S(2)}, u32[]{:S(2)}) async-start(bf16[8,2,4,3584]{3,2,1,0:T(4,128)(2,1)} %reshape.222), calls=%async_computation.1 | async-start | bytes 917504 | tf_op jit(solution)/shard_map/all_to_all | solution.py:76
  18.8 1.0 copy.65
  20.5 0.3 fusion.18
  20.8 12.0 %all-to-all-done.1 = bf16[8,2,4,3584]{3,2,1,0:T(4,128)(2,1)S(1)} async-done(((bf16[8,2,4,3584]{3,2,1,0:T(4,128)(2,1)}), bf16[8,2,4,3584]{3,2,1,0:T(4,128)(2,1)S(1)}, u32[]{:S(2)}, u32[]{:S(2)}) %all-to-all-start.1) | async-done | bytes 458784 | tf_op jit(solution)/shard_map/all_to_all | solution.py:76
  32.8 0.9 reshape.219
  33.6 3.5 %all-to-all-start = ((bf16[8,2,4,3584]{3,2,1,0:T(4,128)(2,1)}), bf16[8,2,4,3584]{3,2,1,0:T(4,128)(2,1)S(1)}, u32[]{:S(2)}, u32[]{:S(2)}) async-start(bf16[8,2,4,3584]{3,2,1,0:T(4,128)(2,1)} %reshape.219), calls=%async_computation | async-start | bytes 917504 | tf_op jit(solution)/shard_map/all_to_all | solution.py:79
  37.4 13.6 %all-to-all-done = bf16[8,2,4,3584]{3,2,1,0:T(4,128)(2,1)S(1)} async-done(((bf16[8,2,4,3584]{3,2,1,0:T(4,128)(2,1)}), bf16[8,2,4,3584]{3,2,1,0:T(4,128)(2,1)S(1)}, u32[]{:S(2)}, u32[]{:S(2)}) %all-to-all-start) | async-done | bytes 458784 | tf_op jit(solution)/shard_map/all_to_all | solution.py:79
  51.5 8.2 %broadcast_in_dim.48 = f32[3584,2,128]{2,1,0:T(2,128)S(1)} broadcast(f32[3584,2]{1,0:T(8,128)S(1)} %bitcast.89), dimensions={0,1} | broadcast | bytes 3698688 | tf_op jit(solution)/shard_map/broadcast_in_dim | solution.py:13
  59.7 0.4 fusion.19
  60.1 0.4 fusion.41
  60.5 0.4 fusion.38
  60.9 19.9 %all-gather.6.cloned.1.call-done = bf16[3584,256]{1,0:T(8,128)(2,1)} async-done(((bf16[896,256]{1,0:T(8,128)(2,1)}), bf16[3584,256]{1,0:T(8,128)(2,1)}) %all-gather.6.cloned.1.call-update) | async-done | bytes 1835024 | tf_op jit(solution)/shard_map/all_gather | solution.py:115
  81.0 8.2 %broadcast_in_dim.46 = f32[3584,2,128]{2,1,0:T(2,128)S(1)} broadcast(f32[3584,2]{1,0:T(8,128)S(1)} %bitcast.90), dimensions={0,1} | broadcast | bytes 3698688 | tf_op jit(solution)/shard_map/broadcast_in_dim | solution.py:13
  89.2 0.4 fusion.20
  89.6 0.4 fusion.40
  90.0 0.4 fusion.37
  90.5 0.4 copy-done.2
  90.9 2.5 fusion.3
  93.3 23.1 %all-gather.4.cloned.1.call-done = bf16[256,3584]{0,1:T(8,128)(2,1)} async-done(((bf16[256,896]{0,1:T(8,128)(2,1)}), bf16[256,3584]{0,1:T(8,128)(2,1)}) %all-gather.4.cloned.1.call-update) | async-done | bytes 1835024 | tf_op jit(solution)/shard_map/all_gather | solution.py:116
  116.4 1.9 fusion.21
  118.3 0.4 multiply_convert_fusion.4
  118.7 0.6 fusion.39
  119.3 2.5 fusion.11
  121.9 0.4 multiply_convert_fusion.2
  122.3 0.6 fusion.42
  122.9 2.6 fusion.7
  125.6 0.6 fusion.16
  126.3 0.6 fusion.17
  127.0 1.1 pad_maximum_fusion.1
  128.1 4.6 %all-to-all-start.2 = ((bf16[8,2,4,3584]{3,2,1,0:T(4,128)(2,1)}), bf16[8,2,4,3584]{3,2,1,0:T(4,128)(2,1)S(1)}, u32[]{:S(2)}, u32[]{:S(2)}) async-start(bf16[8,2,4,3584]{3,2,1,0:T(4,128)(2,1)} %pad_maximum_fusion.1), calls=%async_computation.2 | async-start | bytes 917504 | tf_op jit(solution)/shard_map/all_to_all | solution.py:140
  132.7 2.9 %fusion.14 = bf16[1,3584,256]{2,1,0:T(8,128)(2,1)S(1)} fusion(f32[3584,256]{1,0:T(8,128)} %fusion.3, bf16[32,3584]{1,0:T(8,128)(2,1)S(1)} %reshape_squeeze.14, f32[32,256]{1,0:T(8,128)S(1)} %fusion.40, f32[32,256]{1,0:T(8,128)S(1)} %fusion.41), kind=kOutput, calls=%fused_computation.21 | convolution fusion | flops 62439424 | bytes 5799936 | tf_op jit(solution)/shard_map/dot_general | solution.py:60
  135.8 0.7 fusion.13
  136.5 1.4 copy-done.4
  137.9 0.7 fusion.12
  138.5 0.7 pad_maximum_fusion
  139.2 29.3 %copy.71 = bf16[3,3584,256]{2,0,1:T(4,128)(2,1)} copy(bf16[3,3584,256]{2,1,0:T(8,128)(2,1)S(1)} %pad_maximum_fusion) | data formatting | bytes 11010048 | tf_op jit(solution)/shard_map/stack | solution.py:149
  168.5 5.7 %all-to-all-start.3 = ((bf16[3,3584,256]{2,0,1:T(4,128)(2,1)}), bf16[3,3584,256]{2,0,1:T(4,128)(2,1)}, u32[]{:S(2)}, u32[]{:S(2)}) async-start(bf16[3,3584,256]{2,0,1:T(4,128)(2,1)} %copy.71), calls=%async_computation.3 | async-start | bytes 14680064 | tf_op jit(solution)/shard_map/all_to_all | solution.py:150
  174.4 1.9 fusion.15
  176.3 79.7 %all-to-all-done.3 = bf16[3,3584,256]{2,0,1:T(4,128)(2,1)} async-done(((bf16[3,3584,256]{2,0,1:T(4,128)(2,1)}), bf16[3,3584,256]{2,0,1:T(4,128)(2,1)}, u32[]{:S(2)}, u32[]{:S(2)}) %all-to-all-start.3) | async-done | bytes 5505056 | tf_op jit(solution)/shard_map/all_to_all | solution.py:150
  256.0 7.5 %reduce_sum.42 = bf16[3,896,256]{2,0,1:T(4,128)(2,1)S(1)} reduce(bf16[3,4,896,256]{3,0,2,1:T(4,128)(2,1)} %bitcast.14, bf16[]{:T(256)} %constant.35.clone.1), dimensions={1}, to_apply=%region_5.6 | reduce | flops 2064384 | bytes 6881282 | tf_op jit(solution)/shard_map/reduce_sum | solution.py:152
  263.5 3.3 %fusion.34 = (bf16[1,896,256]{2,0,1:T(2,128)(2,1)}, bf16[1,896,256]{2,0,1:T(2,128)(2,1)}, bf16[1,896,256]{2,0,1:T(2,128)(2,1)}) fusion(bf16[3,896,256]{2,0,1:T(4,128)(2,1)S(1)} %reduce_sum.42), kind=kLoop, calls=%fused_computation.72 | loop fusion | bytes 2752512 | tf_op jit(solution)/shard_map/slice | solution.py:157
  266.8 3.6 %copy.76 = bf16[1,896,256]{1,2,0:T(8,128)(2,1)} copy(bf16[1,896,256]{2,0,1:T(2,128)(2,1)} %get-tuple-element.26) | data formatting | bytes 917504 | tf_op jit(solution)/shard_map/transpose | solution.py:157
  270.4 2.2 copy_bitcast_fusion
  (64 shorter events, 2.8 us)
Async XLA Ops:
  7.2 4.0 %copy-start = (bf16[128,3584]{1,0:T(8,128)(2,1)S(1)}, bf16[128,3584]{1,0:T(8,128)(2,1)}, u32[]{:S(2)}) copy-start(bf16[128,3584]{1,0:T(8,128)(2,1)} %param.12) | copy-start | bytes 2752516
  7.2 11.7 %copy-start.10 = (bf16[256,896]{1,0:T(8,128)(2,1)S(1)}, bf16[256,896]{1,0:T(8,128)(2,1)}, u32[]{:S(2)}) copy-start(bf16[256,896]{1,0:T(8,128)(2,1)} %param.20) | copy-start | bytes 1376260
  7.2 44.1 %all-gather.8.cloned.1.call-start = ((), (), s32[]{:S(2)}) async-start(), calls=%async_computation.6 | async-start | bytes 2293760 | tf_op jit(solution)/shard_map/all_gather | solution.py:114
  7.9 72.9 %all-gather.6.cloned.1.call-start = ((), (), s32[]{:S(2)}) async-start(), calls=%async_computation.5 | async-start | bytes 2293760 | tf_op jit(solution)/shard_map/all_gather | solution.py:115
  11.2 8.6 %copy-start.11 = (f32[28,2]{0,1:T(2,128)S(1)}, f32[28,2]{0,1:T(2,128)}, u32[]{:S(2)}) copy-start(f32[28,2]{0,1:T(2,128)} %param.21) | copy-start | bytes 676
  11.2 8.7 %copy-start.12 = (f32[28,2]{0,1:T(2,128)S(1)}, f32[28,2]{0,1:T(2,128)}, u32[]{:S(2)}) copy-start(f32[28,2]{0,1:T(2,128)} %param.22) | copy-start | bytes 676
  11.2 8.8 %copy-start.13 = (f32[2,28]{1,0:T(2,128)S(1)}, f32[2,28]{1,0:T(2,128)}, u32[]{:S(2)}) copy-start(f32[2,28]{1,0:T(2,128)} %param.23) | copy-start | bytes 676
  11.3 9.2 %copy-start.9 = (bf16[128,3584]{1,0:T(8,128)(2,1)S(1)}, bf16[128,3584]{1,0:T(8,128)(2,1)}, u32[]{:S(2)}) copy-start(bf16[128,3584]{1,0:T(8,128)(2,1)} %param.13) | copy-start | bytes 2752516
  12.5 20.3 %all-to-all-start.1 = ((bf16[8,2,4,3584]{3,2,1,0:T(4,128)(2,1)}), bf16[8,2,4,3584]{3,2,1,0:T(4,128)(2,1)S(1)}, u32[]{:S(2)}, u32[]{:S(2)}) async-start(bf16[8,2,4,3584]{3,2,1,0:T(4,128)(2,1)} %reshape.222), calls=%async_computation.1 | async-start | bytes 917504 | tf_op jit(solution)/shard_map/all_to_all | solution.py:76
  18.8 97.6 %all-gather.4.cloned.1.call-start = ((), (), s32[]{:S(2)}) async-start(), calls=%async_computation.4 | async-start | bytes 2293760 | tf_op jit(solution)/shard_map/all_gather | solution.py:116
  33.6 17.4 %all-to-all-start = ((bf16[8,2,4,3584]{3,2,1,0:T(4,128)(2,1)}), bf16[8,2,4,3584]{3,2,1,0:T(4,128)(2,1)S(1)}, u32[]{:S(2)}, u32[]{:S(2)}) async-start(bf16[8,2,4,3584]{3,2,1,0:T(4,128)(2,1)} %reshape.219), calls=%async_computation | async-start | bytes 917504 | tf_op jit(solution)/shard_map/all_to_all | solution.py:79
  51.4 8.2 %copy-start.8 = (bf16[3584,256]{1,0:T(8,128)(2,1)S(1)}, bf16[3584,256]{1,0:T(8,128)(2,1)}, u32[]{:S(2)}) copy-start(bf16[3584,256]{1,0:T(8,128)(2,1)} %all-gather.8.cloned.1.call-done) | copy-start | bytes 5505028
  80.9 8.2 %copy-start.7 = (bf16[3584,256]{1,0:T(8,128)(2,1)S(1)}, bf16[3584,256]{1,0:T(8,128)(2,1)}, u32[]{:S(2)}) copy-start(bf16[3584,256]{1,0:T(8,128)(2,1)} %all-gather.6.cloned.1.call-done) | copy-start | bytes 5505028
  89.6 1.3 copy-start.2
  122.9 2.6 copy-start.3
  128.1 40.4 %all-to-all-start.2 = ((bf16[8,2,4,3584]{3,2,1,0:T(4,128)(2,1)}), bf16[8,2,4,3584]{3,2,1,0:T(4,128)(2,1)S(1)}, u32[]{:S(2)}, u32[]{:S(2)}) async-start(bf16[8,2,4,3584]{3,2,1,0:T(4,128)(2,1)} %pad_maximum_fusion.1), calls=%async_computation.2 | async-start | bytes 917504 | tf_op jit(solution)/shard_map/all_to_all | solution.py:140
  132.7 3.1 %copy-start.5 = (f32[3584,256]{1,0:T(8,128)S(1)}, f32[3584,256]{1,0:T(8,128)}, u32[]{:S(2)}) copy-start(f32[3584,256]{1,0:T(8,128)} %fusion.7) | copy-start | bytes 11010052
  135.8 2.0 copy-start.4
  168.5 87.5 %all-to-all-start.3 = ((bf16[3,3584,256]{2,0,1:T(4,128)(2,1)}), bf16[3,3584,256]{2,0,1:T(4,128)(2,1)}, u32[]{:S(2)}, u32[]{:S(2)}) async-start(bf16[3,3584,256]{2,0,1:T(4,128)(2,1)} %copy.71), calls=%async_computation.3 | async-start | bytes 14680064 | tf_op jit(solution)/shard_map/all_to_all | solution.py:150
  266.8 3.6 %copy-start.6 = (bf16[1,896,256]{2,0,1:T(2,128)(2,1)S(1)}, bf16[1,896,256]{2,0,1:T(2,128)(2,1)}, u32[]{:S(2)}) copy-start(bf16[1,896,256]{2,0,1:T(2,128)(2,1)} %get-tuple-element.27) | copy-start | bytes 1376260
  266.8 5.8 %copy-start.1 = (bf16[128,3584]{1,0:T(8,128)(2,1)S(1)}, bf16[128,3584]{1,0:T(8,128)(2,1)}, u32[]{:S(2)}) copy-start(bf16[128,3584]{1,0:T(8,128)(2,1)} %param.12) | copy-start | bytes 2752516
Sparse Core Ops, SparseCore 0:
  9.9 35.8 all-gather.7
  47.6 33.1 all-gather.5
  83.2 33.1 all-gather.3
where the time goes:
time: 280 us; the launch traced here: 279 us
  waiting for transfers between devices  150 us (54%)
  local copies, waits for them, and re-layouts  61.4 us (22%)
  starting transfers between devices  20.2 us (7%)
  matrix products  19.3 us (7%)
  between operations  15.4 us (6%)
  other arithmetic  13.2 us (5%)
    all_to_all x1, waiting for transfers between devices, on_device(): lax.all_to_all(stacked, 'dp', split_axis=1, concat_axis=0, tiled=True)  79.7 us
    another operation x1, local copies, waits for them, and re-layouts, on_device(): stacked = jnp.stack([sum_gate, sum_up, sum_down], axis=0)  29.3 us
    all_gather x1, waiting for transfers between devices, on_device(): lax.all_gather(w_down, 'dp', axis=1, tiled=True)  23.1 us
    all_gather x1, waiting for transfers between devices, on_device(): lax.all_gather(w_up, 'dp', axis=0, tiled=True)  19.9 us
    broadcast_in_dim x2, local copies, waits for them, and re-layouts, dequantize(): jnp.repeat(jnp.repeat(scale, block_rows, axis=0), block_cols, axis=1)  16.4 us
    all_to_all x1, waiting for transfers between devices, send_rows(): lax.all_to_all(fan_out(cot_rows, members), 'expert', split_axis=0, concat...  13.6 us
    all_to_all x1, waiting for transfers between devices, send_rows(): lax.all_to_all(fan_out(token_rows, members), 'expert', split_axis=0, conc...  12 us
    reduce_sum x1, other arithmetic, on_device(): jnp.sum(received.astype(jnp.float32).reshape(groups, 3, rows_here, -1), a...  7.48 us
  transfers between devices with their start and end apart: 7, of which 5 were waited for; matrix products, arithmetic and copies ran while one was open for 23% of the time, Pallas kernels for 0%

commit v1 on v0

v1 whole, which is shorter than its diff:
```python
import functools
import math

import jax
import jax.numpy as jnp
from jax import lax
from jax.experimental import pallas as pl
from jax.experimental.pallas import tpu as pltpu
from jax.sharding import PartitionSpec as P

HSH = 8
CAP = 4
ROWS = 2 * CAP
BLOCK = 128
CHIPS = HSH // 2
BF16 = jnp.bfloat16
F32 = jnp.float32
VMEM_BYTES = 48 * 1024 * 1024

NN = (((1,), (0,)), ((), ()))
NT = (((1,), (1,)), ((), ()))
TN = (((0,), (0,)), ((), ()))


def mm(a, b, dims):
    return lax.dot_general(a, b, dims, preferred_element_type=F32)


def call(kernel, outs, scalars, arrays, scratch=(), flops=0, name=None):
    moved = sum(math.prod(x.shape) * x.dtype.itemsize for x in (*arrays, *outs))
    return pl.pallas_call(
        kernel,
        out_shape=outs,
        in_specs=[pl.BlockSpec(memory_space=pltpu.SMEM)] * len(scalars)
        + [pl.BlockSpec(memory_space=pltpu.VMEM)] * len(arrays),
        out_specs=[pl.BlockSpec(memory_space=pltpu.VMEM)] * len(outs),
        scratch_shapes=list(scratch),
        compiler_params=pltpu.CompilerParams(vmem_limit_bytes=VMEM_BYTES),
        cost_estimate=pl.CostEstimate(flops=flops, bytes_accessed=moved, transcendentals=0),
        name=name,
    )(*scalars, *arrays)


def shape(dims, dtype=BF16):
    return jax.ShapeDtypeStruct(dims, dtype)


def swap(x, axis, k):
    return lax.ppermute(x, axis, [(i, i ^ k) for i in range(lax.axis_size(axis))])


def rows_of(value, first, count=ROWS):
    return value[first : first + count]


def route_kernel(groups, experts, live, plan, me, ids, weight, tokens, cots, *rest):
    outs, picks, slices = rest[:groups], rest[groups], rest[groups + 1]
    count, width = tokens.shape
    depth = width // groups
    lists = experts * ROWS
    slot = lax.broadcasted_iota(jnp.int32, (count, 1), 0)
    lane = lax.broadcasted_iota(jnp.int32, (count, lists), 1)
    alive = slot < live[0]
    odd = slot % 2 == 1
    listed = jnp.zeros((count, lists), F32)
    weights = jnp.zeros((count, lists), F32)
    for e in range(experts):
        match = ids[...] == e
        routed = (jnp.sum(jnp.where(match, 1.0, 0.0), axis=1, keepdims=True) > 0.0) & alive
        total = jnp.sum(jnp.where(match, weight[...], 0.0), axis=1, keepdims=True)
        second = odd & (plan[0, e] == 1)
        in_first = jnp.where(routed & ~second, 1.0, 0.0)
        in_second = jnp.where(routed & second, 1.0, 0.0)
        is_first = (lane >= e * ROWS) & (lane < e * ROWS + CAP)
        is_second = (lane >= e * ROWS + CAP) & (lane < (e + 1) * ROWS)
        listed = jnp.where(is_first, in_first, jnp.where(is_second, in_second, listed))
        weights = jnp.where(is_first | is_second, total, weights)
    before = lax.broadcasted_iota(jnp.int32, (count, count), 1)
    here = lax.broadcasted_iota(jnp.int32, (count, count), 0)
    upto = jnp.where(before <= here, 1.0, 0.0).astype(BF16)
    place = mm(upto, listed.astype(BF16), NN)
    wanted = (lane % CAP + 1).astype(F32)
    picked = jnp.where((listed > 0.0) & (place == wanted), 1.0, 0.0)
    row_weight = jnp.sum(picked * weights, axis=0, keepdims=True)
    square = (lists, lists)
    eye = lax.broadcasted_iota(jnp.int32, square, 0) == lax.broadcasted_iota(jnp.int32, square, 1)
    column = jnp.sum(jnp.where(eye, row_weight, 0.0), axis=1, keepdims=True)
    picked = picked.astype(BF16)
    for e in range(experts):
        picks[e] = picked[:, e * ROWS : (e + 1) * ROWS]
    for s in range(groups):
        cut = slice(s * depth, (s + 1) * depth)
        token_rows = mm(picked, tokens[:, cut], TN)
        cot_rows = mm(picked, cots[:, cut], TN) * column
        parts = []
        for e in range(experts):
            parts += [rows_of(token_rows, e * ROWS), rows_of(cot_rows, e * ROWS)]
        slices[s] = jnp.concatenate(parts, axis=0).astype(BF16)
    for k in range(groups):
        outs[k][...] = slices[me[0] ^ k]


def weights_kernel(first, scale_gate, scale_up, scale_down, gate, up, down, gate_up, down_out):
    depth, hid = gate.shape
    step = math.gcd(depth, BLOCK)
    for i in range(depth // step):
        block = (first[0] + i * step) // BLOCK
        for h in range(hid // BLOCK):
            at = (slice(i * step, (i + 1) * step), slice(h * BLOCK, (h + 1) * BLOCK))
            to = slice(hid + h * BLOCK, hid + (h + 1) * BLOCK)
            gate_up[at] = (gate[at].astype(F32) * scale_gate[block, h]).astype(BF16)
            gate_up[at[0], to] = (up[at].astype(F32) * scale_up[block, h]).astype(BF16)
    lane = lax.broadcasted_iota(jnp.int32, (1, depth), 1)
    start = first[0] // BLOCK
    last = scale_down.shape[1] - 1
    for h in range(hid // BLOCK):
        spread = jnp.zeros((1, depth), F32) + scale_down[h, start]
        for j in range(1, depth // BLOCK + 2):
            block = jnp.minimum(start + j, last)
            spread = jnp.where(lane >= (start + j) * BLOCK - first[0], scale_down[h, block], spread)
        at = slice(h * BLOCK, (h + 1) * BLOCK)
        down_out[at, :] = (down[at, :].astype(F32) * spread).astype(BF16)


def token_part(chunks):
    return jnp.concatenate([c[: c.shape[0] // 2, :] for c in chunks], axis=0)


def cot_part(chunks):
    return jnp.concatenate([c[c.shape[0] // 2 :, :] for c in chunks], axis=0)


def partial_kernel(groups, chips, *refs):
    chunks, weights, outs = refs[:chips], refs[chips : chips + 4], refs[chips + 4 :]
    tokens, cots = token_part(chunks), cot_part(chunks)
    hid = weights[1].shape[0]
    for half in range(2):
        gate_up, down = weights[2 * half], weights[2 * half + 1]
        for product, at in (
            (mm(tokens, gate_up[...], NN), 0),
            (mm(cots, down[...], NT), 2 * hid),
        ):
            cut = slice(3 * hid * half + at, 3 * hid * half + at + product.shape[1])
            for k in range(groups):
                rows = [rows_of(product, (c * groups + k) * ROWS) for c in range(chips)]
                outs[k][:, cut] = jnp.concatenate(rows, axis=0).astype(outs[k].dtype)


def act_kernel(groups, *refs):
    parts, out = refs[:groups], refs[groups]
    hid = out.shape[1] // 6
    for half in range(2):
        values = []
        for i in range(3):
            cut = slice((3 * half + i) * hid, (3 * half + i + 1) * hid)
            total = parts[0][:, cut]
            for part in parts[1:]:
                total = total + part[:, cut].astype(F32)
            values.append(total)
        a, b, dh = values
        sig = jax.nn.sigmoid(a)
        swish = a * sig
        results = (dh * b * sig * (1.0 + a * (1.0 - sig)), dh * swish, swish * b)
        for i, result in enumerate(results):
            cut = slice((3 * half + i) * hid, (3 * half + i + 1) * hid)
            out[:, cut] = result.astype(BF16)


def dx_kernel(groups, chips, *refs):
    acts, (own, other), outs = refs[:groups], refs[groups : groups + 2], refs[groups + 2 :]
    hid = own.shape[1] // 2
    act = jnp.concatenate([a[...] for a in acts], axis=0)
    outs[chips][...] = act[:, 3 * hid :]
    dx = mm(act[:, : 2 * hid], own[...], NT) + mm(act[:, 3 * hid : 5 * hid], other[...], NT)
    for c in range(chips):
        rows = [rows_of(dx, (k * chips + c) * ROWS) for k in range(groups)]
        outs[c][...] = jnp.concatenate(rows, axis=0).astype(outs[c].dtype)


def collect_kernel(groups, chips, *refs):
    parts, outs = refs[:chips], refs[chips:]
    sums = []
    for first in range(0, chips, CHIPS):
        total = parts[first][...].astype(F32)
        for part in parts[first + 1 : first + CHIPS]:
            total = total + part[...].astype(F32)
        sums.append(total)
    for k in range(groups):
        rows = [rows_of(total, k * ROWS) for total in sums]
        outs[k][...] = jnp.concatenate(rows, axis=0).astype(BF16)


def place_kernel(groups, experts, me, home, *refs):
    parts, picks, out, slices = refs[:groups], refs[groups], refs[groups + 1], refs[groups + 2]
    depth = parts[0].shape[1]
    for k in range(groups):
        slices[me[0] ^ k] = parts[k][...].astype(F32)
    for s in range(groups):
        total = jnp.zeros((out.shape[0], depth), F32)
        for x in range(experts):
            rows = slices[s, x * ROWS : (x + 1) * ROWS, :].astype(BF16)
            total = total + mm(picks[home[0] ^ x], rows, NN)
        out[:, s * depth : (s + 1) * depth] = total.astype(BF16)


def regroup(act, groups, chips):
    wide = act.astype(F32)
    rows = [rows_of(wide, (k * chips + c) * ROWS) for c in range(chips) for k in range(groups)]
    return jnp.concatenate(rows, axis=0).astype(BF16)


def grads_kernel(groups, chips, *refs):
    own, other = refs[:chips], refs[chips : 2 * chips]
    acts, act_other = refs[2 * chips : 2 * chips + groups], refs[2 * chips + groups]
    grad_gate, grad_up, grad_down = refs[2 * chips + groups + 1 :]
    hid = grad_gate.shape[1]
    act = jnp.concatenate([a[:, : 3 * hid] for a in acts], axis=0)
    tokens = jnp.concatenate([token_part(own), token_part(other)], axis=0)
    cots = jnp.concatenate([cot_part(own), cot_part(other)], axis=0)
    both = jnp.concatenate(
        [regroup(act, groups, chips), regroup(act_other[...], groups, chips)], axis=0
    )
    grad_gate[...] = mm(tokens, both[:, :hid], TN).astype(BF16)
    grad_up[...] = mm(tokens, both[:, hid : 2 * hid], TN).astype(BF16)
    grad_down[...] = mm(both[:, 2 * hid :], cots, TN).astype(BF16)


def chunk_of(parts, experts, slot):
    blocks = [p.reshape(experts, 2, ROWS, p.shape[1]) for p in parts]
    if experts == 1:
        blocks = [b[0] for b in blocks]
    else:
        blocks = [lax.dynamic_index_in_dim(b, slot, 0, keepdims=False) for b in blocks]
    return jnp.concatenate([b[0] for b in blocks] + [b[1] for b in blocks], axis=0)


def on_device(
    tokens,
    cotangent,
    route_weight,
    expert_ids,
    live_tokens,
    replica_plan,
    w_gate,
    w_up,
    w_down,
    scale_gate,
    scale_up,
    scale_down,
):
    members, groups = lax.axis_size("expert"), lax.axis_size("dp")
    experts, chips = members // HSH, members // 2
    count, width = tokens.shape
    depth, hid = w_gate.shape
    group, member = lax.axis_index("dp"), lax.axis_index("expert")
    me = jnp.reshape(group, (1,))
    home = jnp.reshape(member // HSH, (1,))
    rows = groups * chips * ROWS

    *sent, picks = call(
        functools.partial(route_kernel, groups, experts),
        [shape((2 * ROWS * experts, depth))] * groups + [shape((experts, count, ROWS))],
        (live_tokens, replica_plan, me),
        (expert_ids, route_weight, tokens, cotangent),
        scratch=[pltpu.VMEM((groups, 2 * ROWS * experts, depth), BF16)],
        flops=4 * count * experts * ROWS * width,
        name="route",
    )
    parts = [sent[0]] + [swap(sent[k], "dp", k) for k in range(1, groups)]

    gate_up, down = call(
        weights_kernel,
        [shape((depth, 2 * hid)), shape((hid, depth))],
        (me * depth, scale_gate, scale_up, scale_down),
        (w_gate, w_up, w_down),
        flops=6 * depth * hid,
        name="weights",
    )
    other_gate_up, other_down = swap(gate_up, "expert", 1), swap(down, "expert", 1)

    chunks = [chunk_of(parts, experts, member // HSH)]
    for c in range(1, chips):
        out = chunks[0] if experts == 1 else chunk_of(parts, experts, (member ^ (2 * c)) // HSH)
        chunks.append(swap(out, "expert", 2 * c))

    partial = call(
        functools.partial(partial_kernel, groups, chips),
        [shape((chips * ROWS, 6 * hid), F32 if k == 0 else BF16) for k in range(groups)],
        (),
        (*chunks, gate_up, down, other_gate_up, other_down),
        flops=12 * rows * depth * hid,
        name="partial",
    )
    summands = [partial[0]] + [swap(partial[k], "dp", k) for k in range(1, groups)]
    (act,) = call(
        functools.partial(act_kernel, groups),
        [shape((chips * ROWS, 6 * hid))],
        (),
        summands,
        flops=40 * chips * ROWS * hid,
        name="activations",
    )
    acts = [act] + [swap(act, "dp", k) for k in range(1, groups)]
    *dx, act_out = call(
        functools.partial(dx_kernel, groups, chips),
        [shape((groups * ROWS, depth), F32 if c == 0 else BF16) for c in range(chips)]
        + [shape((rows, 3 * hid))],
        (),
        (*acts, gate_up, other_gate_up),
        flops=8 * rows * depth * hid,
        name="dx",
    )
    returned = [dx[0]] + [swap(dx[c], "expert", 2 * c) for c in range(1, chips)]

    other_chunks = [swap(c, "expert", 1) for c in chunks]
    act_other = swap(act_out, "expert", 1)

    home_rows = call(
        functools.partial(collect_kernel, groups, chips),
        [shape((experts * ROWS, depth))] * groups,
        (),
        returned,
        flops=rows * depth,
        name="collect",
    )
    placed = [home_rows[0]] + [swap(home_rows[k], "dp", k) for k in range(1, groups)]

    grad_gate, grad_up, grad_down = call(
        functools.partial(grads_kernel, groups, chips),
        [shape((depth, hid)), shape((depth, hid)), shape((hid, depth))],
        (),
        (*chunks, *other_chunks, *acts, act_other),
        flops=12 * rows * depth * hid,
        name="gradients",
    )
    (d_tokens,) = call(
        functools.partial(place_kernel, groups, experts),
        [shape((count, width))],
        (me, home),
        (*placed, picks),
        scratch=[pltpu.VMEM((groups, experts * ROWS, depth), F32)],
        flops=2 * count * experts * ROWS * width,
        name="place",
    )
    return (d_tokens, grad_gate, grad_up, grad_down)


def solution(mesh):
    return jax.shard_map(
        on_device,
        mesh=mesh,
        in_specs=(
            P(("dp", "expert"), None),
            P(("dp", "expert"), None),
            P(("dp", "expert"), None),
            P(("dp", "expert"), None),
            P(("dp", "expert")),
            P(("dp", "expert"), None),
            P("dp", "expert"),
            P("dp", "expert"),
            P("expert", "dp"),
            P(None, "expert"),
            P(None, "expert"),
            P("expert", None),
        ),
        out_specs=(
            P(("dp", "expert"), None),
            P("dp", "expert"),
            P("dp", "expert"),
            P("expert", "dp"),
        ),
        check_vma=False,
    )
```

time: 280 us -> 65 us (0.23)
  waiting for transfers between devices: 150 us -> 24.9 us
  local copies, waits for them, and re-layouts: 61.4 us -> 5.89 us
  matrix products: 19.3 us -> 0 us
  between operations: 15.4 us -> 2.07 us
  other arithmetic: 13.2 us -> 0 us
  Pallas kernels: 0 us -> 6.36 us
  starting transfers between devices: 20.2 us -> 25.3 us
    all_to_all x4 -> x0, waiting for transfers between devices: 105 us -> none  [the longest x1 79.7 us: on_device(): lax.all_to_all(stacked, 'dp', split_axis=1, concat_axis=0, tiled=True)]
    all_gather x3 -> x0, waiting for transfers between devices: 43 us -> none  [the longest x1 23.1 us: on_device(): lax.all_gather(w_down, 'dp', axis=1, tiled=True)]
    another operation x7 -> x0, local copies, waits for them, and re-layouts: 29.6 us -> none  [the longest x1 29.3 us: on_device(): stacked = jnp.stack([sum_gate, sum_up, sum_down], axis=0)]
    ppermute x0 -> x25, starting transfers between devices: none -> 25.3 us  [swap(): lax.ppermute(x, axis, [(i, i ^ k) for i in range(lax.axis_size(axis))])]
    ppermute x0 -> x25, waiting for transfers between devices: none -> 24.9 us  [swap(): lax.ppermute(x, axis, [(i, i ^ k) for i in range(lax.axis_size(axis))])]
    all_to_all x4 -> x0, starting transfers between devices: 20.1 us -> none  [the longest x1 6.33 us: send_rows(): lax.all_to_all(fan_out(token_rows, members), 'expert', split_axis=0, conc...]
    dot_general x19 -> x0, matrix products: 19.3 us -> none  [the longest x2 5.34 us: expert_terms(): lax.dot_general(cot_rows, hidden, by_rows, preferred_element_type=jnp.flo...]
    broadcast_in_dim x6 -> x0, local copies, waits for them, and re-layouts: 16.7 us -> none  [the longest x2 16.4 us: dequantize(): jnp.repeat(jnp.repeat(scale, block_rows, axis=0), block_cols, axis=1)]
  transfers between devices with their start and end apart: 7 -> 25, of which waited for: 5 -> 11; matrix products, arithmetic and copies ran while one was open for 23% -> 0% of each run, Pallas kernels for 0% -> 4%
where the time goes in v1:
time: 65 us; the launch traced here: 64.6 us
  starting transfers between devices  25.3 us (39%)
  waiting for transfers between devices  24.9 us (38%)
  Pallas kernels  6.36 us (10%)
  local copies, waits for them, and re-layouts  5.89 us (9%)
  between operations  2.07 us (3%)
    ppermute x25, starting transfers between devices, swap(): lax.ppermute(x, axis, [(i, i ^ k) for i in range(lax.axis_size(axis))])  25.3 us
    ppermute x25, waiting for transfers between devices, swap(): lax.ppermute(x, axis, [(i, i ^ k) for i in range(lax.axis_size(axis))])  24.9 us
    pallas_call x8, Pallas kernels, call(): pl.pallas_call(kernel, out_shape=outs, in_specs=[pl.BlockSpec(memory_spac...  6.36 us
    unnamed x31, local copies, waits for them, and re-layouts  5.88 us
  transfers between devices with their start and end apart: 25, of which 11 were waited for; matrix products, arithmetic and copies ran while one was open for 0% of the time, Pallas kernels for 4%

profile of v1, /device:TPU:0, one launch (start us, length us, event | category | flops | bytes accessed | tf_op | source)
XLA Modules:
  0.0 64.6 jit_solution(7580306581362396579)
XLA Ops:
  0.6 0.7 %copy-done.6 = s32[128,8]{0,1:T(8,128)S(1)} copy-done((s32[128,8]{0,1:T(8,128)S(1)}, s32[128,8]{0,1:T(8,128)}, u32[]{:S(2)}) %copy-start.6) | copy-done | bytes 4120
  1.3 0.1 copy.16.ids
  1.4 0.6 copy-done.7
  2.0 0.1 copy.17.weight
  3.4 1.2 %copy-done = bf16[128,3584]{1,0:T(8,128)(2,1)S(1)} copy-done((bf16[128,3584]{1,0:T(8,128)(2,1)S(1)}, bf16[128,3584]{1,0:T(8,128)(2,1)}, u32[]{:S(2)}) %copy-start) | copy-done | bytes 917528
  4.6 1.2 %copy-done.1 = bf16[128,3584]{1,0:T(8,128)(2,1)S(1)} copy-done((bf16[128,3584]{1,0:T(8,128)(2,1)S(1)}, bf16[128,3584]{1,0:T(8,128)(2,1)}, u32[]{:S(2)}) %copy-start.1) | copy-done | bytes 917528
  5.8 0.7 %route.1 = (bf16[16,896]{1,0:T(8,128)(2,1)S(1)}, bf16[16,896]{1,0:T(8,128)(2,1)S(1)}, bf16[16,896]{1,0:T(8,128)(2,1)S(1)}, bf16[16,896]{1,0:T(8,128)(2,1)S(1)}, bf16[1,128,8]{2,1,0:T(8,128)(2,1)S(1)}) custom-call(s32[1]{0:T(128)S(6)} %copy.27.live, s32[1,1]{1,0:T(1,128)S(6)} %copy.28.plan, s32[1]{0:T(128)} %bitcast.me, s32[128,8]{1,0:T(8,128)S(1)} %copy.16.ids, ...), custom_call_target="tpu_custom_call" | custom-call | flops 14680064 | bytes 1959936 | tf_op jit(solution)/shard_map/route/pallas_call | solution.py:31
  6.4 3.0 %collective-permute-start = (bf16[16,896]{1,0:T(8,128)(2,1)S(1)}, bf16[16,896]{1,0:T(8,128)(2,1)S(1)}, u32[]{:S(2)}, u32[]{:S(2)}) collective-permute-start(bf16[16,896]{1,0:T(8,128)(2,1)S(1)} %get-tuple-element.28), channel_id=1, source_target_pairs={{0,8},{8,0},{16,24},{24,16},{1,9},{9,1},{17,25},{25,17},{2,10},{10... | collective-permute-start | bytes 86024 | tf_op jit(solution)/shard_map/ppermute | solution.py:49
  9.4 1.5 %collective-permute-start.1 = (bf16[16,896]{1,0:T(8,128)(2,1)S(1)}, bf16[16,896]{1,0:T(8,128)(2,1)S(1)}, u32[]{:S(2)}, u32[]{:S(2)}) collective-permute-start(bf16[16,896]{1,0:T(8,128)(2,1)S(1)} %get-tuple-element.29), channel_id=1, source_target_pairs={{0,16},{8,24},{16,0},{24,8},{1,17},{9,25},{17,1},{25,9},{2,18},{10... | collective-permute-start | bytes 86024 | tf_op jit(solution)/shard_map/ppermute | solution.py:49
  11.0 0.7 %copy-done.8 = f32[28,2]{0,1:T(2,128)S(1)} copy-done((f32[28,2]{0,1:T(2,128)S(1)}, f32[28,2]{0,1:T(2,128)}, u32[]{:S(2)}) %copy-start.8) | copy-done | bytes 248
  11.6 0.1 copy.18.scale_gate
  11.7 0.6 copy-done.9
  12.3 0.1 copy.19.scale_up
  12.4 0.6 copy-done.5
  13.0 1.4 %weights.1 = (bf16[896,512]{1,0:T(8,128)(2,1)S(1)}, bf16[256,896]{1,0:T(8,128)(2,1)S(1)}) custom-call(s32[1]{0:T(128)S(6)} %mul.3.first, f32[28,2]{1,0:T(8,128)S(1)} %copy.18.scale_gate, f32[28,2]{1,0:T(8,128)S(1)} %copy.19.scale_up, f32[2,28]{1,0:T(2,128)S(1)} %copy-done.5, bf16[896,256]{1,0:T(8,128)(2,1)S(1)} %copy-done.2, bf16[896,256]{1,0:T(8,128)(2,1)S(1)} %copy-done.3, ...), custom_call_target="tpu_custom_call" | custom-call | flops 1376256 | bytes 2752512 | tf_op jit(solution)/shard_map/weights/pallas_call | solution.py:31
  14.4 0.1 collective-permute-start.6
  14.5 0.5 collective-permute-start.7
  15.0 0.7 %collective-permute-done.2 = bf16[16,896]{1,0:T(8,128)(2,1)S(1)} collective-permute-done((bf16[16,896]{1,0:T(8,128)(2,1)S(1)}, bf16[16,896]{1,0:T(8,128)(2,1)S(1)}, u32[]{:S(2)}, u32[]{:S(2)}) %collective-permute-start.2) | collective-permute-done | bytes 28704 | tf_op jit(solution)/shard_map/ppermute | solution.py:49
  15.8 1.6 %collective-permute-start.3 = (bf16[64,896]{1,0:T(8,128)(2,1)S(1)}, bf16[64,896]{1,0:T(8,128)(2,1)S(1)}, u32[]{:S(2)}, u32[]{:S(2)}) collective-permute-start(bf16[64,896]{1,0:T(8,128)(2,1)S(1)} %constant_dynamic-update-slice_fusion.refs_0_), channel_id=1, source_target_pairs={{0,2},{1,3},{2,0},{3,1},{4,6},{5,7},{6,4},{7,5},{8,10},{9,11},{10,... | collective-permute-start | bytes 344072 | tf_op jit(solution)/shard_map/ppermute | solution.py:49
  17.4 2.6 %collective-permute-start.4 = (bf16[64,896]{1,0:T(8,128)(2,1)S(1)}, bf16[64,896]{1,0:T(8,128)(2,1)S(1)}, u32[]{:S(2)}, u32[]{:S(2)}) collective-permute-start(bf16[64,896]{1,0:T(8,128)(2,1)S(1)} %constant_dynamic-update-slice_fusion.refs_0_), channel_id=1, source_target_pairs={{0,4},{1,5},{2,6},{3,7},{4,0},{5,1},{6,2},{7,3},{8,12},{9,13},{10,... | collective-permute-start | bytes 344072 | tf_op jit(solution)/shard_map/ppermute | solution.py:49
  20.0 0.2 collective-permute-start.5
  20.2 1.6 %collective-permute-done.3.refs_1_ = bf16[64,896]{1,0:T(8,128)(2,1)S(1)} collective-permute-done((bf16[64,896]{1,0:T(8,128)(2,1)S(1)}, bf16[64,896]{1,0:T(8,128)(2,1)S(1)}, u32[]{:S(2)}, u32[]{:S(2)}) %collective-permute-start.3) | collective-permute-done | bytes 114720 | tf_op jit(solution)/shard_map/ppermute | solution.py:49
  21.8 6.9 %collective-permute-done.4.refs_2_ = bf16[64,896]{1,0:T(8,128)(2,1)S(1)} collective-permute-done((bf16[64,896]{1,0:T(8,128)(2,1)S(1)}, bf16[64,896]{1,0:T(8,128)(2,1)S(1)}, u32[]{:S(2)}, u32[]{:S(2)}) %collective-permute-start.4) | collective-permute-done | bytes 114720 | tf_op jit(solution)/shard_map/ppermute | solution.py:49
  28.7 0.7 %partial.1 = (f32[32,1536]{1,0:T(8,128)S(1)}, bf16[32,1536]{1,0:T(8,128)(2,1)S(1)}, bf16[32,1536]{1,0:T(8,128)(2,1)S(1)}, bf16[32,1536]{1,0:T(8,128)(2,1)S(1)}) custom-call(bf16[64,896]{1,0:T(8,128)(2,1)S(1)} %constant_dynamic-update-slice_fusion.refs_0_, bf16[64,896]{1,0:T(8,128)(2,1)S(1)} %collective-permute-done.3.refs_1_, ...), custom_call_target="tpu_custom_call" | custom-call | flops 352321536 | bytes 3702784 | tf_op jit(solution)/shard_map/partial/pallas_call | solution.py:31
  29.4 2.2 %collective-permute-start.10 = (bf16[32,1536]{1,0:T(8,128)(2,1)S(1)}, bf16[32,1536]{1,0:T(8,128)(2,1)S(1)}, u32[]{:S(2)}, u32[]{:S(2)}) collective-permute-start(bf16[32,1536]{1,0:T(8,128)(2,1)S(1)} %get-tuple-element.36), channel_id=1, source_target_pairs={{0,24},{8,16},{16,8},{24,0},{1,25},{9,17},{17,9},{25,1},{2,26},{10... | collective-permute-start | bytes 294920 | tf_op jit(solution)/shard_map/ppermute | solution.py:49
  31.6 0.5 collective-permute-start.8
  32.2 0.8 %collective-permute-start.9 = (bf16[32,1536]{1,0:T(8,128)(2,1)S(1)}, bf16[32,1536]{1,0:T(8,128)(2,1)S(1)}, u32[]{:S(2)}, u32[]{:S(2)}) collective-permute-start(bf16[32,1536]{1,0:T(8,128)(2,1)S(1)} %get-tuple-element.35), channel_id=1, source_target_pairs={{0,16},{8,24},{16,0},{24,8},{1,17},{9,25},{17,1},{25,9},{2,18},{10... | collective-permute-start | bytes 294920 | tf_op jit(solution)/shard_map/ppermute | solution.py:49
  33.0 2.0 %collective-permute-done.10.refs_3_ = bf16[32,1536]{1,0:T(8,128)(2,1)S(1)} collective-permute-done((bf16[32,1536]{1,0:T(8,128)(2,1)S(1)}, bf16[32,1536]{1,0:T(8,128)(2,1)S(1)}, u32[]{:S(2)}, u32[]{:S(2)}) %collective-permute-start.10) | collective-permute-done | bytes 98336 | tf_op jit(solution)/shard_map/ppermute | solution.py:49
  35.0 1.9 %collective-permute-done.8.refs_1_ = bf16[32,1536]{1,0:T(8,128)(2,1)S(1)} collective-permute-done((bf16[32,1536]{1,0:T(8,128)(2,1)S(1)}, bf16[32,1536]{1,0:T(8,128)(2,1)S(1)}, u32[]{:S(2)}, u32[]{:S(2)}) %collective-permute-start.8) | collective-permute-done | bytes 98336 | tf_op jit(solution)/shard_map/ppermute | solution.py:49
  36.9 2.3 %collective-permute-start.11 = (bf16[32,1536]{1,0:T(8,128)(2,1)S(1)}, bf16[32,1536]{1,0:T(8,128)(2,1)S(1)}, u32[]{:S(2)}, u32[]{:S(2)}) collective-permute-start(bf16[32,1536]{1,0:T(8,128)(2,1)S(1)} %activations.1.refs_0_.refs_8_), channel_id=1, source_target_pairs={{0,8},{8,0},{16,24},{24,16},{1,9},{9,1},{17,25},{25,17},{2,10},{10... | collective-permute-start | bytes 294920 | tf_op jit(solution)/shard_map/ppermute | solution.py:49
  39.2 1.5 %collective-permute-start.13 = (bf16[32,1536]{1,0:T(8,128)(2,1)S(1)}, bf16[32,1536]{1,0:T(8,128)(2,1)S(1)}, u32[]{:S(2)}, u32[]{:S(2)}) collective-permute-start(bf16[32,1536]{1,0:T(8,128)(2,1)S(1)} %activations.1.refs_0_.refs_8_), channel_id=1, source_target_pairs={{0,24},{8,16},{16,8},{24,0},{1,25},{9,17},{17,9},{25,1},{2,26},{10... | collective-permute-start | bytes 294920 | tf_op jit(solution)/shard_map/ppermute | solution.py:49
  40.8 1.1 %collective-permute-done.11.refs_1_.refs_9_ = bf16[32,1536]{1,0:T(8,128)(2,1)S(1)} collective-permute-done((bf16[32,1536]{1,0:T(8,128)(2,1)S(1)}, bf16[32,1536]{1,0:T(8,128)(2,1)S(1)}, u32[]{:S(2)}, u32[]{:S(2)}) %collective-permute-start.11) | collective-permute-done | bytes 98336 | tf_op jit(solution)/shard_map/ppermute | solution.py:49
  41.8 3.1 %collective-permute-done.12.refs_2_.refs_10_ = bf16[32,1536]{1,0:T(8,128)(2,1)S(1)} collective-permute-done((bf16[32,1536]{1,0:T(8,128)(2,1)S(1)}, bf16[32,1536]{1,0:T(8,128)(2,1)S(1)}, u32[]{:S(2)}, u32[]{:S(2)}) %collective-permute-start.12) | collective-permute-done | bytes 98336 | tf_op jit(solution)/shard_map/ppermute | solution.py:49
  44.9 0.7 %dx.1 = (f32[32,896]{1,0:T(8,128)S(1)}, bf16[32,896]{1,0:T(8,128)(2,1)S(1)}, bf16[32,896]{1,0:T(8,128)(2,1)S(1)}, bf16[32,896]{1,0:T(8,128)(2,1)S(1)}, bf16[128,768]{1,0:T(8,128)(2,1)S(1)}) custom-call(bf16[32,1536]{1,0:T(8,128)(2,1)S(1)} %activations.1.refs_0_.refs_8_, bf16[32,1536]{1,0:T(8,128)(2,1)S(1)} %collective-permute-done.11.refs_1_.refs_9_, ...), custom_call_target="tpu_custom_call" | custom-call | flops 234881024 | bytes 2711552 | tf_op jit(solution)/shard_map/dx/pallas_call | solution.py:31
  45.6 0.1 collective-permute-start.24
  45.7 1.6 %collective-permute-start.14 = (bf16[32,896]{1,0:T(8,128)(2,1)S(1)}, bf16[32,896]{1,0:T(8,128)(2,1)S(1)}, u32[]{:S(2)}, u32[]{:S(2)}) collective-permute-start(bf16[32,896]{1,0:T(8,128)(2,1)S(1)} %get-tuple-element.38), channel_id=1, source_target_pairs={{0,2},{1,3},{2,0},{3,1},{4,6},{5,7},{6,4},{7,5},{8,10},{9,11},{10,... | collective-permute-start | bytes 172040 | tf_op jit(solution)/shard_map/ppermute | solution.py:49
  47.2 1.5 %collective-permute-start.15 = (bf16[32,896]{1,0:T(8,128)(2,1)S(1)}, bf16[32,896]{1,0:T(8,128)(2,1)S(1)}, u32[]{:S(2)}, u32[]{:S(2)}) collective-permute-start(bf16[32,896]{1,0:T(8,128)(2,1)S(1)} %get-tuple-element.39), channel_id=1, source_target_pairs={{0,4},{1,5},{2,6},{3,7},{4,0},{5,1},{6,2},{7,3},{8,12},{9,13},{10,... | collective-permute-start | bytes 172040 | tf_op jit(solution)/shard_map/ppermute | solution.py:49
  48.7 1.4 %collective-permute-start.16 = (bf16[32,896]{1,0:T(8,128)(2,1)S(1)}, bf16[32,896]{1,0:T(8,128)(2,1)S(1)}, u32[]{:S(2)}, u32[]{:S(2)}) collective-permute-start(bf16[32,896]{1,0:T(8,128)(2,1)S(1)} %get-tuple-element.40), channel_id=1, source_target_pairs={{0,6},{1,7},{2,4},{3,5},{4,2},{5,3},{6,0},{7,1},{8,14},{9,15},{10,... | collective-permute-start | bytes 172040 | tf_op jit(solution)/shard_map/ppermute | solution.py:49
  50.1 4.9 %collective-permute-done.15.refs_2_ = bf16[32,896]{1,0:T(8,128)(2,1)S(1)} collective-permute-done((bf16[32,896]{1,0:T(8,128)(2,1)S(1)}, bf16[32,896]{1,0:T(8,128)(2,1)S(1)}, u32[]{:S(2)}, u32[]{:S(2)}) %collective-permute-start.15) | collective-permute-done | bytes 57376 | tf_op jit(solution)/shard_map/ppermute | solution.py:49
  55.1 0.8 %collective-permute-start.17 = (bf16[8,896]{1,0:T(8,128)(2,1)S(1)}, bf16[8,896]{1,0:T(8,128)(2,1)S(1)}, u32[]{:S(2)}, u32[]{:S(2)}) collective-permute-start(bf16[8,896]{1,0:T(8,128)(2,1)S(1)} %get-tuple-element.42), channel_id=1, source_target_pairs={{0,8},{8,0},{16,24},{24,16},{1,9},{9,1},{17,25},{25,17},{2,10},{10... | collective-permute-start | bytes 43016 | tf_op jit(solution)/shard_map/ppermute | solution.py:49
  55.8 1.3 %collective-permute-start.18 = (bf16[8,896]{1,0:T(8,128)(2,1)S(1)}, bf16[8,896]{1,0:T(8,128)(2,1)S(1)}, u32[]{:S(2)}, u32[]{:S(2)}) collective-permute-start(bf16[8,896]{1,0:T(8,128)(2,1)S(1)} %get-tuple-element.43), channel_id=1, source_target_pairs={{0,16},{8,24},{16,0},{24,8},{1,17},{9,25},{17,1},{25,9},{2,18},{10... | collective-permute-start | bytes 43016 | tf_op jit(solution)/shard_map/ppermute | solution.py:49
  57.1 1.5 %collective-permute-start.19 = (bf16[8,896]{1,0:T(8,128)(2,1)S(1)}, bf16[8,896]{1,0:T(8,128)(2,1)S(1)}, u32[]{:S(2)}, u32[]{:S(2)}) collective-permute-start(bf16[8,896]{1,0:T(8,128)(2,1)S(1)} %get-tuple-element.44), channel_id=1, source_target_pairs={{0,24},{8,16},{16,8},{24,0},{1,25},{9,17},{17,9},{25,1},{2,26},{10... | collective-permute-start | bytes 43016 | tf_op jit(solution)/shard_map/ppermute | solution.py:49
  58.6 0.2 collective-permute-done.17.refs_1_
  58.9 0.3 collective-permute-start.21
  59.2 0.4 collective-permute-done.18.refs_2_
  59.6 2.2 %collective-permute-done.19.refs_3_ = bf16[8,896]{1,0:T(8,128)(2,1)S(1)} collective-permute-done((bf16[8,896]{1,0:T(8,128)(2,1)S(1)}, bf16[8,896]{1,0:T(8,128)(2,1)S(1)}, u32[]{:S(2)}, u32[]{:S(2)}) %collective-permute-start.19) | collective-permute-done | bytes 14368 | tf_op jit(solution)/shard_map/ppermute | solution.py:49
  61.7 1.3 %place.1 = bf16[128,3584]{1,0:T(8,128)(2,1)} custom-call(s32[1]{0:T(128)} %bitcast.me, s32[1]{0:T(128)} %bitcast.1.home, bf16[8,896]{1,0:T(8,128)(2,1)S(1)} %get-tuple-element.41.refs_0_, bf16[8,896]{1,0:T(8,128)(2,1)S(1)} %collective-permute-done.17.refs_1_, bf16[8,896]{1,0:T(8,128)(2,1)S(1)} %collective-permute-done.18.refs_2_, ...), custom_call_target="tpu_custom_call" | custom-call | flops 7340032 | bytes 976896 | tf_op jit(solution)/shard_map/place/pallas_call | solution.py:31
  63.1 1.5 %gradients.1 = (bf16[896,256]{1,0:T(8,128)(2,1)}, bf16[896,256]{1,0:T(8,128)(2,1)}, bf16[256,896]{1,0:T(8,128)(2,1)}) custom-call(bf16[64,896]{1,0:T(8,128)(2,1)S(1)} %constant_dynamic-update-slice_fusion.refs_0_, bf16[64,896]{1,0:T(8,128)(2,1)S(1)} %collective-permute-done.3.refs_1_, bf16[64,896]{1,0:T(8,128)(2,1)S(1)} %collective-permute-done.4.refs_2_, ...), custom_call_target="tpu_custom_call" | custom-call | flops 352321536 | bytes 2883584 | tf_op jit(solution)/shard_map/gradients/pallas_call | solution.py:31
  (42 shorter events, 0.3 us)
Async XLA Ops:
  0.6 0.7 %copy-start.6 = (s32[128,8]{0,1:T(8,128)S(1)}, s32[128,8]{0,1:T(8,128)}, u32[]{:S(2)}) copy-start(s32[128,8]{0,1:T(8,128)} %param.15) | copy-start | bytes 12292
  1.3 0.7 %copy-start.7 = (f32[128,8]{0,1:T(8,128)S(1)}, f32[128,8]{0,1:T(8,128)}, u32[]{:S(2)}) copy-start(f32[128,8]{0,1:T(8,128)} %param.14) | copy-start | bytes 12292
  3.4 1.2 %copy-start = (bf16[128,3584]{1,0:T(8,128)(2,1)S(1)}, bf16[128,3584]{1,0:T(8,128)(2,1)}, u32[]{:S(2)}) copy-start(bf16[128,3584]{1,0:T(8,128)(2,1)} %tokens.1) | copy-start | bytes 2752516
  4.6 1.2 %copy-start.1 = (bf16[128,3584]{1,0:T(8,128)(2,1)S(1)}, bf16[128,3584]{1,0:T(8,128)(2,1)}, u32[]{:S(2)}) copy-start(bf16[128,3584]{1,0:T(8,128)(2,1)} %cots.1) | copy-start | bytes 2752516
  5.8 6.7 %copy-start.2 = (bf16[896,256]{1,0:T(8,128)(2,1)S(1)}, bf16[896,256]{1,0:T(8,128)(2,1)}, u32[]{:S(2)}) copy-start(bf16[896,256]{1,0:T(8,128)(2,1)} %gate.1) | copy-start | bytes 1376260
  5.8 6.7 %copy-start.3 = (bf16[896,256]{1,0:T(8,128)(2,1)S(1)}, bf16[896,256]{1,0:T(8,128)(2,1)}, u32[]{:S(2)}) copy-start(bf16[896,256]{1,0:T(8,128)(2,1)} %up.1) | copy-start | bytes 1376260
  5.8 6.7 %copy-start.4 = (bf16[256,896]{1,0:T(8,128)(2,1)S(1)}, bf16[256,896]{1,0:T(8,128)(2,1)}, u32[]{:S(2)}) copy-start(bf16[256,896]{1,0:T(8,128)(2,1)} %down.1) | copy-start | bytes 1376260
  6.4 8.5 %collective-permute-start = (bf16[16,896]{1,0:T(8,128)(2,1)S(1)}, bf16[16,896]{1,0:T(8,128)(2,1)S(1)}, u32[]{:S(2)}, u32[]{:S(2)}) collective-permute-start(bf16[16,896]{1,0:T(8,128)(2,1)S(1)} %get-tuple-element.28), channel_id=1, source_target_pairs={{0,8},{8,0},{16,24},{24,16},{1,9},{9,1},{17,25},{25,17},{2,10},{10... | collective-permute-start | bytes 86024 | tf_op jit(solution)/shard_map/ppermute | solution.py:49
  9.4 5.5 %collective-permute-start.1 = (bf16[16,896]{1,0:T(8,128)(2,1)S(1)}, bf16[16,896]{1,0:T(8,128)(2,1)S(1)}, u32[]{:S(2)}, u32[]{:S(2)}) collective-permute-start(bf16[16,896]{1,0:T(8,128)(2,1)S(1)} %get-tuple-element.29), channel_id=1, source_target_pairs={{0,16},{8,24},{16,0},{24,8},{1,17},{9,25},{17,1},{25,9},{2,18},{10... | collective-permute-start | bytes 86024 | tf_op jit(solution)/shard_map/ppermute | solution.py:49
  11.0 0.7 %copy-start.8 = (f32[28,2]{0,1:T(2,128)S(1)}, f32[28,2]{0,1:T(2,128)}, u32[]{:S(2)}) copy-start(f32[28,2]{0,1:T(2,128)} %param.21) | copy-start | bytes 676
  11.0 4.8 %collective-permute-start.2 = (bf16[16,896]{1,0:T(8,128)(2,1)S(1)}, bf16[16,896]{1,0:T(8,128)(2,1)S(1)}, u32[]{:S(2)}, u32[]{:S(2)}) collective-permute-start(bf16[16,896]{1,0:T(8,128)(2,1)S(1)} %get-tuple-element.30), channel_id=1, source_target_pairs={{0,24},{8,16},{16,8},{24,0},{1,25},{9,17},{17,9},{25,1},{2,26},{10... | collective-permute-start | bytes 86024 | tf_op jit(solution)/shard_map/ppermute | solution.py:49
  11.6 0.7 %copy-start.9 = (f32[28,2]{0,1:T(2,128)S(1)}, f32[28,2]{0,1:T(2,128)}, u32[]{:S(2)}) copy-start(f32[28,2]{0,1:T(2,128)} %param.22) | copy-start | bytes 676
  12.3 0.7 %copy-start.5 = (f32[2,28]{1,0:T(2,128)S(1)}, f32[2,28]{1,0:T(2,128)}, u32[]{:S(2)}) copy-start(f32[2,28]{1,0:T(2,128)} %scale_down.1) | copy-start | bytes 676
  14.4 14.3 %collective-permute-start.6 = (bf16[896,512]{1,0:T(8,128)(2,1)S(1)}, bf16[896,512]{1,0:T(8,128)(2,1)S(1)}, u32[]{:S(2)}, u32[]{:S(2)}) collective-permute-start(bf16[896,512]{1,0:T(8,128)(2,1)S(1)} %get-tuple-element.31.refs_4_), channel_id=1, source_target_pairs={{0,1},{1,0},{2,3},{3,2},{4,5},{5,4},{6,7},{7,6},{8,9},{9,8},{10,11... | collective-permute-start | bytes 2752520 | tf_op jit(solution)/shard_map/ppermute | solution.py:49
  14.5 14.2 %collective-permute-start.7 = (bf16[256,896]{1,0:T(8,128)(2,1)S(1)}, bf16[256,896]{1,0:T(8,128)(2,1)S(1)}, u32[]{:S(2)}, u32[]{:S(2)}) collective-permute-start(bf16[256,896]{1,0:T(8,128)(2,1)S(1)} %get-tuple-element.32.refs_5_), channel_id=1, source_target_pairs={{0,1},{1,0},{2,3},{3,2},{4,5},{5,4},{6,7},{7,6},{8,9},{9,8},{10,11... | collective-permute-start | bytes 1376264 | tf_op jit(solution)/shard_map/ppermute | solution.py:49
  15.8 6.0 %collective-permute-start.3 = (bf16[64,896]{1,0:T(8,128)(2,1)S(1)}, bf16[64,896]{1,0:T(8,128)(2,1)S(1)}, u32[]{:S(2)}, u32[]{:S(2)}) collective-permute-start(bf16[64,896]{1,0:T(8,128)(2,1)S(1)} %constant_dynamic-update-slice_fusion.refs_0_), channel_id=1, source_target_pairs={{0,2},{1,3},{2,0},{3,1},{4,6},{5,7},{6,4},{7,5},{8,10},{9,11},{10,... | collective-permute-start | bytes 344072 | tf_op jit(solution)/shard_map/ppermute | solution.py:49
  17.4 11.2 %collective-permute-start.4 = (bf16[64,896]{1,0:T(8,128)(2,1)S(1)}, bf16[64,896]{1,0:T(8,128)(2,1)S(1)}, u32[]{:S(2)}, u32[]{:S(2)}) collective-permute-start(bf16[64,896]{1,0:T(8,128)(2,1)S(1)} %constant_dynamic-update-slice_fusion.refs_0_), channel_id=1, source_target_pairs={{0,4},{1,5},{2,6},{3,7},{4,0},{5,1},{6,2},{7,3},{8,12},{9,13},{10,... | collective-permute-start | bytes 344072 | tf_op jit(solution)/shard_map/ppermute | solution.py:49
  20.0 8.7 %collective-permute-start.5 = (bf16[64,896]{1,0:T(8,128)(2,1)S(1)}, bf16[64,896]{1,0:T(8,128)(2,1)S(1)}, u32[]{:S(2)}, u32[]{:S(2)}) collective-permute-start(bf16[64,896]{1,0:T(8,128)(2,1)S(1)} %constant_dynamic-update-slice_fusion.refs_0_), channel_id=1, source_target_pairs={{0,6},{1,7},{2,4},{3,5},{4,2},{5,3},{6,0},{7,1},{8,14},{9,15},{10,... | collective-permute-start | bytes 344072 | tf_op jit(solution)/shard_map/ppermute | solution.py:49
  29.4 5.6 %collective-permute-start.10 = (bf16[32,1536]{1,0:T(8,128)(2,1)S(1)}, bf16[32,1536]{1,0:T(8,128)(2,1)S(1)}, u32[]{:S(2)}, u32[]{:S(2)}) collective-permute-start(bf16[32,1536]{1,0:T(8,128)(2,1)S(1)} %get-tuple-element.36), channel_id=1, source_target_pairs={{0,24},{8,16},{16,8},{24,0},{1,25},{9,17},{17,9},{25,1},{2,26},{10... | collective-permute-start | bytes 294920 | tf_op jit(solution)/shard_map/ppermute | solution.py:49
  31.6 5.2 %collective-permute-start.8 = (bf16[32,1536]{1,0:T(8,128)(2,1)S(1)}, bf16[32,1536]{1,0:T(8,128)(2,1)S(1)}, u32[]{:S(2)}, u32[]{:S(2)}) collective-permute-start(bf16[32,1536]{1,0:T(8,128)(2,1)S(1)} %get-tuple-element.34), channel_id=1, source_target_pairs={{0,8},{8,0},{16,24},{24,16},{1,9},{9,1},{17,25},{25,17},{2,10},{10... | collective-permute-start | bytes 294920 | tf_op jit(solution)/shard_map/ppermute | solution.py:49
  32.2 4.7 %collective-permute-start.9 = (bf16[32,1536]{1,0:T(8,128)(2,1)S(1)}, bf16[32,1536]{1,0:T(8,128)(2,1)S(1)}, u32[]{:S(2)}, u32[]{:S(2)}) collective-permute-start(bf16[32,1536]{1,0:T(8,128)(2,1)S(1)} %get-tuple-element.35), channel_id=1, source_target_pairs={{0,16},{8,24},{16,0},{24,8},{1,17},{9,25},{17,1},{25,9},{2,18},{10... | collective-permute-start | bytes 294920 | tf_op jit(solution)/shard_map/ppermute | solution.py:49
  36.9 4.9 %collective-permute-start.11 = (bf16[32,1536]{1,0:T(8,128)(2,1)S(1)}, bf16[32,1536]{1,0:T(8,128)(2,1)S(1)}, u32[]{:S(2)}, u32[]{:S(2)}) collective-permute-start(bf16[32,1536]{1,0:T(8,128)(2,1)S(1)} %activations.1.refs_0_.refs_8_), channel_id=1, source_target_pairs={{0,8},{8,0},{16,24},{24,16},{1,9},{9,1},{17,25},{25,17},{2,10},{10... | collective-permute-start | bytes 294920 | tf_op jit(solution)/shard_map/ppermute | solution.py:49
  39.2 5.7 %collective-permute-start.12 = (bf16[32,1536]{1,0:T(8,128)(2,1)S(1)}, bf16[32,1536]{1,0:T(8,128)(2,1)S(1)}, u32[]{:S(2)}, u32[]{:S(2)}) collective-permute-start(bf16[32,1536]{1,0:T(8,128)(2,1)S(1)} %activations.1.refs_0_.refs_8_), channel_id=1, source_target_pairs={{0,16},{8,24},{16,0},{24,8},{1,17},{9,25},{17,1},{25,9},{2,18},{10... | collective-permute-start | bytes 294920 | tf_op jit(solution)/shard_map/ppermute | solution.py:49
  39.2 5.7 %collective-permute-start.13 = (bf16[32,1536]{1,0:T(8,128)(2,1)S(1)}, bf16[32,1536]{1,0:T(8,128)(2,1)S(1)}, u32[]{:S(2)}, u32[]{:S(2)}) collective-permute-start(bf16[32,1536]{1,0:T(8,128)(2,1)S(1)} %activations.1.refs_0_.refs_8_), channel_id=1, source_target_pairs={{0,24},{8,16},{16,8},{24,0},{1,25},{9,17},{17,9},{25,1},{2,26},{10... | collective-permute-start | bytes 294920 | tf_op jit(solution)/shard_map/ppermute | solution.py:49
  45.6 17.5 %collective-permute-start.24 = (bf16[128,768]{1,0:T(8,128)(2,1)S(1)}, bf16[128,768]{1,0:T(8,128)(2,1)S(1)}, u32[]{:S(2)}, u32[]{:S(2)}) collective-permute-start(bf16[128,768]{1,0:T(8,128)(2,1)S(1)} %get-tuple-element.46), channel_id=1, source_target_pairs={{0,1},{1,0},{2,3},{3,2},{4,5},{5,4},{6,7},{7,6},{8,9},{9,8},{10,11... | collective-permute-start | bytes 589832 | tf_op jit(solution)/shard_map/ppermute | solution.py:49
  45.7 4.5 %collective-permute-start.14 = (bf16[32,896]{1,0:T(8,128)(2,1)S(1)}, bf16[32,896]{1,0:T(8,128)(2,1)S(1)}, u32[]{:S(2)}, u32[]{:S(2)}) collective-permute-start(bf16[32,896]{1,0:T(8,128)(2,1)S(1)} %get-tuple-element.38), channel_id=1, source_target_pairs={{0,2},{1,3},{2,0},{3,1},{4,6},{5,7},{6,4},{7,5},{8,10},{9,11},{10,... | collective-permute-start | bytes 172040 | tf_op jit(solution)/shard_map/ppermute | solution.py:49
  47.2 7.8 %collective-permute-start.15 = (bf16[32,896]{1,0:T(8,128)(2,1)S(1)}, bf16[32,896]{1,0:T(8,128)(2,1)S(1)}, u32[]{:S(2)}, u32[]{:S(2)}) collective-permute-start(bf16[32,896]{1,0:T(8,128)(2,1)S(1)} %get-tuple-element.39), channel_id=1, source_target_pairs={{0,4},{1,5},{2,6},{3,7},{4,0},{5,1},{6,2},{7,3},{8,12},{9,13},{10,... | collective-permute-start | bytes 172040 | tf_op jit(solution)/shard_map/ppermute | solution.py:49
  48.7 6.3 %collective-permute-start.16 = (bf16[32,896]{1,0:T(8,128)(2,1)S(1)}, bf16[32,896]{1,0:T(8,128)(2,1)S(1)}, u32[]{:S(2)}, u32[]{:S(2)}) collective-permute-start(bf16[32,896]{1,0:T(8,128)(2,1)S(1)} %get-tuple-element.40), channel_id=1, source_target_pairs={{0,6},{1,7},{2,4},{3,5},{4,2},{5,3},{6,0},{7,1},{8,14},{9,15},{10,... | collective-permute-start | bytes 172040 | tf_op jit(solution)/shard_map/ppermute | solution.py:49
  55.1 3.8 %collective-permute-start.17 = (bf16[8,896]{1,0:T(8,128)(2,1)S(1)}, bf16[8,896]{1,0:T(8,128)(2,1)S(1)}, u32[]{:S(2)}, u32[]{:S(2)}) collective-permute-start(bf16[8,896]{1,0:T(8,128)(2,1)S(1)} %get-tuple-element.42), channel_id=1, source_target_pairs={{0,8},{8,0},{16,24},{24,16},{1,9},{9,1},{17,25},{25,17},{2,10},{10... | collective-permute-start | bytes 43016 | tf_op jit(solution)/shard_map/ppermute | solution.py:49
  55.8 3.7 %collective-permute-start.18 = (bf16[8,896]{1,0:T(8,128)(2,1)S(1)}, bf16[8,896]{1,0:T(8,128)(2,1)S(1)}, u32[]{:S(2)}, u32[]{:S(2)}) collective-permute-start(bf16[8,896]{1,0:T(8,128)(2,1)S(1)} %get-tuple-element.43), channel_id=1, source_target_pairs={{0,16},{8,24},{16,0},{24,8},{1,17},{9,25},{17,1},{25,9},{2,18},{10... | collective-permute-start | bytes 43016 | tf_op jit(solution)/shard_map/ppermute | solution.py:49
  57.1 4.6 %collective-permute-start.19 = (bf16[8,896]{1,0:T(8,128)(2,1)S(1)}, bf16[8,896]{1,0:T(8,128)(2,1)S(1)}, u32[]{:S(2)}, u32[]{:S(2)}) collective-permute-start(bf16[8,896]{1,0:T(8,128)(2,1)S(1)} %get-tuple-element.44), channel_id=1, source_target_pairs={{0,24},{8,16},{16,8},{24,0},{1,25},{9,17},{17,9},{25,1},{2,26},{10... | collective-permute-start | bytes 43016 | tf_op jit(solution)/shard_map/ppermute | solution.py:49
  58.6 4.4 %collective-permute-start.20 = (bf16[64,896]{1,0:T(8,128)(2,1)S(1)}, bf16[64,896]{1,0:T(8,128)(2,1)S(1)}, u32[]{:S(2)}, u32[]{:S(2)}) collective-permute-start(bf16[64,896]{1,0:T(8,128)(2,1)S(1)} %constant_dynamic-update-slice_fusion.refs_0_), channel_id=1, source_target_pairs={{0,1},{1,0},{2,3},{3,2},{4,5},{5,4},{6,7},{7,6},{8,9},{9,8},{10,11... | collective-permute-start | bytes 344072 | tf_op jit(solution)/shard_map/ppermute | solution.py:49
  58.9 4.2 %collective-permute-start.21 = (bf16[64,896]{1,0:T(8,128)(2,1)S(1)}, bf16[64,896]{1,0:T(8,128)(2,1)S(1)}, u32[]{:S(2)}, u32[]{:S(2)}) collective-permute-start(bf16[64,896]{1,0:T(8,128)(2,1)S(1)} %collective-permute-done.3.refs_1_), channel_id=1, source_target_pairs={{0,1},{1,0},{2,3},{3,2},{4,5},{5,4},{6,7},{7,6},{8,9},{9,8},{10,11... | collective-permute-start | bytes 344072 | tf_op jit(solution)/shard_map/ppermute | solution.py:49
  59.6 3.5 %collective-permute-start.22 = (bf16[64,896]{1,0:T(8,128)(2,1)S(1)}, bf16[64,896]{1,0:T(8,128)(2,1)S(1)}, u32[]{:S(2)}, u32[]{:S(2)}) collective-permute-start(bf16[64,896]{1,0:T(8,128)(2,1)S(1)} %collective-permute-done.4.refs_2_), channel_id=1, source_target_pairs={{0,1},{1,0},{2,3},{3,2},{4,5},{5,4},{6,7},{7,6},{8,9},{9,8},{10,11... | collective-permute-start | bytes 344072 | tf_op jit(solution)/shard_map/ppermute | solution.py:49
  61.7 1.3 %collective-permute-start.23 = (bf16[64,896]{1,0:T(8,128)(2,1)S(1)}, bf16[64,896]{1,0:T(8,128)(2,1)S(1)}, u32[]{:S(2)}, u32[]{:S(2)}) collective-permute-start(bf16[64,896]{1,0:T(8,128)(2,1)S(1)} %collective-permute-done.5.refs_3_), channel_id=1, source_target_pairs={{0,1},{1,0},{2,3},{3,2},{4,5},{5,4},{6,7},{7,6},{8,9},{9,8},{10,11... | collective-permute-start | bytes 344072 | tf_op jit(solution)/shard_map/ppermute | solution.py:49

commit v2 on v1

v2 whole, which is shorter than its diff:
```python
import functools
import math

import jax
import jax.numpy as jnp
from jax import lax
from jax.experimental import pallas as pl
from jax.experimental.pallas import tpu as pltpu
from jax.sharding import PartitionSpec as P

HSH = 8
CAP = 4
ROWS = 2 * CAP
BLOCK = 128
CHIPS = HSH // 2
BF16 = jnp.bfloat16
F32 = jnp.float32
VMEM_BYTES = 48 * 1024 * 1024

NN = (((1,), (0,)), ((), ()))
NT = (((1,), (1,)), ((), ()))
TN = (((0,), (0,)), ((), ()))


def mm(a, b, dims):
    return lax.dot_general(a, b, dims, preferred_element_type=F32)


def call(kernel, outs, scalars, arrays, far=(), scratch=(), flops=0, name=None):
    moved = sum(math.prod(x.shape) * x.dtype.itemsize for x in (*arrays, *outs))
    return pl.pallas_call(
        kernel,
        out_shape=outs,
        in_specs=[pl.BlockSpec(memory_space=pltpu.SMEM)] * len(scalars)
        + [pl.BlockSpec(memory_space=pl.ANY)] * len(far)
        + [pl.BlockSpec(memory_space=pltpu.VMEM)] * len(arrays),
        out_specs=[pl.BlockSpec(memory_space=pltpu.VMEM)] * len(outs),
        scratch_shapes=list(scratch),
        compiler_params=pltpu.CompilerParams(vmem_limit_bytes=VMEM_BYTES),
        cost_estimate=pl.CostEstimate(flops=flops, bytes_accessed=moved, transcendentals=0),
        name=name,
    )(*scalars, *far, *arrays)


def shape(dims, dtype=BF16):
    return jax.ShapeDtypeStruct(dims, dtype)


def swap(x, axis, k):
    return lax.ppermute(x, axis, [(i, i ^ k) for i in range(lax.axis_size(axis))])


def rows_of(value, first, count=ROWS):
    return value[first : first + count]


def route_kernel(groups, experts, me, live_in, plan_in, ids_in, weight_in, tokens_in, cots_in, *rest):
    outs, picks, scratch = rest[:groups], rest[groups], rest[groups + 1 :]
    live, plan, ids, weight, tokens, cots, slices, sems = scratch
    sources = (live_in, plan_in, ids_in, weight_in, tokens_in, cots_in)
    targets = (live, plan, ids, weight, tokens, cots)
    copies = [pltpu.make_async_copy(s, t, sems.at[i]) for i, (s, t) in enumerate(zip(sources, targets))]
    for copy in copies:
        copy.start()
    for copy in copies[:4]:
        copy.wait()
    count, width = tokens.shape
    depth = width // groups
    lists = experts * ROWS
    slot = lax.broadcasted_iota(jnp.int32, (1, count), 1)
    line = lax.broadcasted_iota(jnp.int32, (lists, count), 0)
    alive = slot < live[0]
    odd = slot % 2 == 1
    listed = jnp.zeros((lists, count), F32)
    weights = jnp.zeros((lists, count), F32)
    for e in range(experts):
        match = ids[...] == e
        routed = (jnp.sum(jnp.where(match, 1.0, 0.0), axis=0, keepdims=True) > 0.0) & alive
        total = jnp.sum(jnp.where(match, weight[...], 0.0), axis=0, keepdims=True)
        second = odd & (plan[0, e] == 1)
        in_first = jnp.where(routed & ~second, 1.0, 0.0)
        in_second = jnp.where(routed & second, 1.0, 0.0)
        is_first = (line >= e * ROWS) & (line < e * ROWS + CAP)
        is_second = (line >= e * ROWS + CAP) & (line < (e + 1) * ROWS)
        listed = jnp.where(is_first, in_first, jnp.where(is_second, in_second, listed))
        weights = jnp.where(is_first | is_second, total, weights)
    before = lax.broadcasted_iota(jnp.int32, (count, count), 0)
    here = lax.broadcasted_iota(jnp.int32, (count, count), 1)
    upto = jnp.where(before <= here, 1.0, 0.0).astype(BF16)
    place = mm(listed.astype(BF16), upto, NN)
    wanted = (line % CAP + 1).astype(F32)
    picked = jnp.where((listed > 0.0) & (place == wanted), 1.0, 0.0)
    column = jnp.sum(picked * weights, axis=1, keepdims=True)
    for e in range(experts):
        picks[e] = rows_of(picked, e * ROWS)
    picked = picked.astype(BF16)
    for copy in copies[4:]:
        copy.wait()
    for s in range(groups):
        cut = slice(s * depth, (s + 1) * depth)
        token_rows = mm(picked, tokens[:, cut], NN)
        cot_rows = mm(picked, cots[:, cut], NN) * column
        parts = []
        for e in range(experts):
            parts += [rows_of(token_rows, e * ROWS), rows_of(cot_rows, e * ROWS)]
        slices[s] = jnp.concatenate(parts, axis=0).astype(BF16)
    for k in range(groups):
        outs[k][...] = slices[me[0] ^ k]


def weights_kernel(first, scale_gate, scale_up, scale_down, after, gate, up, down, gate_up, down_out):
    del after
    depth, hid = gate.shape
    step = math.gcd(depth, BLOCK)
    for i in range(depth // step):
        block = (first[0] + i * step) // BLOCK
        for h in range(hid // BLOCK):
            at = (slice(i * step, (i + 1) * step), slice(h * BLOCK, (h + 1) * BLOCK))
            to = slice(hid + h * BLOCK, hid + (h + 1) * BLOCK)
            gate_up[at] = (gate[at].astype(F32) * scale_gate[h, block]).astype(BF16)
            gate_up[at[0], to] = (up[at].astype(F32) * scale_up[h, block]).astype(BF16)
    lane = lax.broadcasted_iota(jnp.int32, (1, depth), 1)
    start = first[0] // BLOCK
    last = scale_down.shape[1] - 1
    for h in range(hid // BLOCK):
        spread = jnp.zeros((1, depth), F32) + scale_down[h, start]
        for j in range(1, depth // BLOCK + 2):
            block = jnp.minimum(start + j, last)
            spread = jnp.where(lane >= (start + j) * BLOCK - first[0], scale_down[h, block], spread)
        at = slice(h * BLOCK, (h + 1) * BLOCK)
        down_out[at, :] = (down[at, :].astype(F32) * spread).astype(BF16)


def token_part(chunks):
    return jnp.concatenate([c[: c.shape[0] // 2, :] for c in chunks], axis=0)


def cot_part(chunks):
    return jnp.concatenate([c[c.shape[0] // 2 :, :] for c in chunks], axis=0)


def partial_kernel(groups, chips, *refs):
    chunks, weights, outs = refs[:chips], refs[chips : chips + 4], refs[chips + 4 :]
    tokens, cots = token_part(chunks), cot_part(chunks)
    hid = weights[1].shape[0]
    for half in range(2):
        gate_up, down = weights[2 * half], weights[2 * half + 1]
        for product, at in (
            (mm(tokens, gate_up[...], NN), 0),
            (mm(cots, down[...], NT), 2 * hid),
        ):
            cut = slice(3 * hid * half + at, 3 * hid * half + at + product.shape[1])
            for k in range(groups):
                rows = [rows_of(product, (c * groups + k) * ROWS) for c in range(chips)]
                outs[k][:, cut] = jnp.concatenate(rows, axis=0).astype(outs[k].dtype)


def act_kernel(groups, *refs):
    parts, out = refs[:groups], refs[groups]
    hid = out.shape[1] // 6
    for half in range(2):
        values = []
        for i in range(3):
            cut = slice((3 * half + i) * hid, (3 * half + i + 1) * hid)
            total = parts[0][:, cut]
            for part in parts[1:]:
                total = total + part[:, cut].astype(F32)
            values.append(total)
        a, b, dh = values
        sig = jax.nn.sigmoid(a)
        swish = a * sig
        results = (dh * b * sig * (1.0 + a * (1.0 - sig)), dh * swish, swish * b)
        for i, result in enumerate(results):
            cut = slice((3 * half + i) * hid, (3 * half + i + 1) * hid)
            out[:, cut] = result.astype(BF16)


def dx_kernel(near, chips, *refs):
    acts, weights, outs = refs[:near], refs[near : near + 4], refs[near + 4 :]
    own, other, own_pair, other_pair = weights
    depth, hid = own.shape[0], own.shape[1] // 2
    act = jnp.concatenate([a[...] for a in acts], axis=0)
    first, second = act[:, : 2 * hid], act[:, 3 * hid : 5 * hid]
    for half, (left, right) in enumerate(((own, other), (own_pair, other_pair))):
        dx = mm(first, left[...], NT) + mm(second, right[...], NT)
        for c in range(chips):
            rows = [rows_of(dx, (k * chips + c) * ROWS) for k in range(near)]
            cut = slice(half * depth, (half + 1) * depth)
            outs[c][:, cut] = jnp.concatenate(rows, axis=0).astype(outs[c].dtype)


def share_kernel(groups, chips, *refs):
    acts, own, other = refs[:groups], refs[groups], refs[groups + 1]
    hid = own.shape[1] // 3
    act = jnp.concatenate([a[...] for a in acts], axis=0)
    own[...] = regroup(act[:, : 3 * hid], groups, chips)
    other[...] = regroup(act[:, 3 * hid :], groups, chips)


def collect_kernel(near, chips, *refs):
    parts, outs = refs[len(refs) - chips - near : len(refs) - near], refs[len(refs) - near :]
    sums = []
    for first in range(0, chips, CHIPS):
        total = parts[first][...].astype(F32)
        for part in parts[first + 1 : first + CHIPS]:
            total = total + part[...].astype(F32)
        sums.append(total)
    for k in range(near):
        rows = [rows_of(total, k * ROWS) for total in sums]
        outs[k][...] = jnp.concatenate(rows, axis=0).astype(BF16)


def place_kernel(groups, experts, me, home, *refs):
    near = groups // 2
    parts, picks, out, slices = refs[:near], refs[near], refs[near + 1], refs[near + 2]
    depth = parts[0].shape[1] // 2
    for k in range(near):
        for half in range(2):
            slices[me[0] ^ (2 * k + half)] = parts[k][:, half * depth : (half + 1) * depth].astype(F32)
    for s in range(groups):
        total = jnp.zeros((out.shape[0], depth), F32)
        for x in range(experts):
            rows = slices[s, x * ROWS : (x + 1) * ROWS, :].astype(BF16)
            total = total + mm(picks[home[0] ^ x].astype(BF16), rows, TN)
        out[:, s * depth : (s + 1) * depth] = total.astype(BF16)


def regroup(act, groups, chips):
    wide = act.astype(F32)
    rows = [rows_of(wide, (k * chips + c) * ROWS) for c in range(chips) for k in range(groups)]
    return jnp.concatenate(rows, axis=0).astype(BF16)


def grads_kernel(chips, *refs):
    own, other, acts = refs[:chips], refs[chips : 2 * chips], refs[2 * chips : 2 * chips + 2]
    grad_gate, grad_up, grad_down = refs[2 * chips + 2 :]
    hid = grad_gate.shape[1]
    tokens = jnp.concatenate([token_part(own), token_part(other)], axis=0)
    cots = jnp.concatenate([cot_part(own), cot_part(other)], axis=0)
    act = jnp.concatenate([a[...] for a in acts], axis=0)
    grad_gate[...] = mm(tokens, act[:, :hid], TN).astype(BF16)
    grad_up[...] = mm(tokens, act[:, hid : 2 * hid], TN).astype(BF16)
    grad_down[...] = mm(act[:, 2 * hid :], cots, TN).astype(BF16)


def chunk_of(parts, experts, slot):
    blocks = [p.reshape(experts, 2, ROWS, p.shape[1]) for p in parts]
    if experts == 1:
        blocks = [b[0] for b in blocks]
    else:
        blocks = [lax.dynamic_index_in_dim(b, slot, 0, keepdims=False) for b in blocks]
    return jnp.concatenate([b[0] for b in blocks] + [b[1] for b in blocks], axis=0)


def on_device(
    tokens,
    cotangent,
    route_weight,
    expert_ids,
    live_tokens,
    replica_plan,
    w_gate,
    w_up,
    w_down,
    scale_gate,
    scale_up,
    scale_down,
):
    members, groups = lax.axis_size("expert"), lax.axis_size("dp")
    experts, chips, near = members // HSH, members // 2, groups // 2
    count, width = tokens.shape
    depth, hid = w_gate.shape
    group, member = lax.axis_index("dp"), lax.axis_index("expert")
    me = jnp.reshape(group, (1,))
    home = jnp.reshape(member // HSH, (1,))
    rows = groups * chips * ROWS

    *sent, picks = call(
        functools.partial(route_kernel, groups, experts),
        [shape((2 * ROWS * experts, depth))] * groups + [shape((experts, ROWS, count), F32)],
        (me,),
        (),
        far=(live_tokens, replica_plan, expert_ids.T, route_weight.T, tokens, cotangent),
        scratch=[
            pltpu.SMEM(live_tokens.shape, jnp.int32),
            pltpu.SMEM(replica_plan.shape, jnp.int32),
            pltpu.VMEM(expert_ids.shape[::-1], jnp.int32),
            pltpu.VMEM(route_weight.shape[::-1], F32),
            pltpu.VMEM(tokens.shape, BF16),
            pltpu.VMEM(cotangent.shape, BF16),
            pltpu.VMEM((groups, 2 * ROWS * experts, depth), BF16),
            pltpu.SemaphoreType.DMA((6,)),
        ],
        flops=4 * count * experts * ROWS * width,
        name="route",
    )
    parts = [sent[0]] + [swap(sent[k], "dp", k) for k in range(1, groups)]
    chunks = [chunk_of(parts, experts, member // HSH)]
    for c in range(1, chips):
        out = chunks[0] if experts == 1 else chunk_of(parts, experts, (member ^ (2 * c)) // HSH)
        chunks.append(swap(out, "expert", 2 * c))

    gate_up, down = call(
        weights_kernel,
        [shape((depth, 2 * hid)), shape((hid, depth))],
        (me * depth, scale_gate.T, scale_up.T, scale_down),
        (w_gate, w_up, w_down),
        far=(chunks[0],),
        flops=6 * depth * hid,
        name="weights",
    )
    other_gate_up, other_down = swap(gate_up, "expert", 1), swap(down, "expert", 1)
    gate_up_pair = swap(gate_up, "dp", 1)

    partial = call(
        functools.partial(partial_kernel, groups, chips),
        [shape((chips * ROWS, 6 * hid), F32 if k == 0 else BF16) for k in range(groups)],
        (),
        (*chunks, gate_up, down, other_gate_up, other_down),
        flops=12 * rows * depth * hid,
        name="partial",
    )
    summands = [partial[0]] + [swap(partial[k], "dp", k) for k in range(1, groups)]
    other_chunks = [swap(c, "expert", 1) for c in chunks]
    other_gate_up_pair = swap(gate_up_pair, "expert", 1)

    (act,) = call(
        functools.partial(act_kernel, groups),
        [shape((chips * ROWS, 6 * hid))],
        (),
        summands,
        flops=40 * chips * ROWS * hid,
        name="activations",
    )
    acts = [act] + [swap(act, "dp", k) for k in range(1, groups)]
    dx = call(
        functools.partial(dx_kernel, near, chips),
        [shape((near * ROWS, 2 * depth), F32 if c == 0 else BF16) for c in range(chips)],
        (),
        (*acts[::2], gate_up, other_gate_up, gate_up_pair, other_gate_up_pair),
        flops=8 * rows * depth * hid,
        name="dx",
    )
    returned = [dx[0]] + [swap(dx[c], "expert", 2 * c) for c in range(1, chips)]

    act_own, act_out = call(
        functools.partial(share_kernel, groups, chips),
        [shape((rows, 3 * hid))] * 2,
        (),
        acts,
        name="share",
    )
    act_other = swap(act_out, "expert", 1)
    grads = call(
        functools.partial(grads_kernel, chips),
        [shape((depth, hid)), shape((depth, hid)), shape((hid, depth))],
        (),
        (*chunks, *other_chunks, act_own, act_other),
        flops=12 * rows * depth * hid,
        name="gradients",
    )
    home_rows = call(
        functools.partial(collect_kernel, near, chips),
        [shape((experts * ROWS, 2 * depth))] * near,
        (),
        returned,
        far=(grads[0],),
        flops=rows * depth,
        name="collect",
    )
    placed = [home_rows[0]] + [swap(home_rows[k], "dp", 2 * k) for k in range(1, near)]
    (d_tokens,) = call(
        functools.partial(place_kernel, groups, experts),
        [shape((count, width))],
        (me, home),
        (*placed, picks),
        scratch=[pltpu.VMEM((groups, experts * ROWS, depth), F32)],
        flops=2 * count * experts * ROWS * width,
        name="place",
    )
    return (d_tokens, *grads)


def solution(mesh):
    return jax.shard_map(
        on_device,
        mesh=mesh,
        in_specs=(
            P(("dp", "expert"), None),
            P(("dp", "expert"), None),
            P(("dp", "expert"), None),
            P(("dp", "expert"), None),
            P(("dp", "expert")),
            P(("dp", "expert"), None),
            P("dp", "expert"),
            P("dp", "expert"),
            P("expert", "dp"),
            P(None, "expert"),
            P(None, "expert"),
            P("expert", None),
        ),
        out_specs=(
            P(("dp", "expert"), None),
            P("dp", "expert"),
            P("dp", "expert"),
            P("expert", "dp"),
        ),
        check_vma=False,
    )
```

time: 65 us -> 85.9 us (1.32)
  waiting for transfers between devices: 24.9 us -> 45.6 us
  local copies, waits for them, and re-layouts: 5.89 us -> 4.1 us
  starting transfers between devices: 25.3 us -> 26.8 us
    ppermute x25, waiting for transfers between devices: 24.9 us -> 45.6 us  [swap(): lax.ppermute(x, axis, [(i, i ^ k) for i in range(lax.axis_size(axis))])]
    unnamed x31 -> x29, local copies, waits for them, and re-layouts: 5.88 us -> 4.09 us
    ppermute x25, starting transfers between devices: 25.3 us -> 26.8 us  [swap(): lax.ppermute(x, axis, [(i, i ^ k) for i in range(lax.axis_size(axis))])]
    pallas_call x8 -> x9, Pallas kernels: 6.36 us -> 7.01 us  [call(): pl.pallas_call(kernel, out_shape=outs, in_specs=[pl.BlockSpec(memory_spac...]
  transfers between devices with their start and end apart: 25 -> 25, of which waited for: 11 -> 16; matrix products, arithmetic and copies ran while one was open for 0% -> 0% of each run, Pallas kernels for 4% -> 4%
where the time goes in v2:
time: 85.9 us; the launch traced here: 85.6 us
  waiting for transfers between devices  45.6 us (53%)
  starting transfers between devices  26.8 us (31%)
  Pallas kernels  7.01 us (8%)
  local copies, waits for them, and re-layouts  4.1 us (5%)
  between operations  2.13 us (2%)
    ppermute x25, waiting for transfers between devices, swap(): lax.ppermute(x, axis, [(i, i ^ k) for i in range(lax.axis_size(axis))])  45.6 us
    ppermute x25, starting transfers between devices, swap(): lax.ppermute(x, axis, [(i, i ^ k) for i in range(lax.axis_size(axis))])  26.8 us
    pallas_call x9, Pallas kernels, call(): pl.pallas_call(kernel, out_shape=outs, in_specs=[pl.BlockSpec(memory_spac...  7.01 us
    unnamed x29, local copies, waits for them, and re-layouts  4.09 us
  transfers between devices with their start and end apart: 25, of which 16 were waited for; matrix products, arithmetic and copies ran while one was open for 0% of the time, Pallas kernels for 4%

profile of v2, /device:TPU:0, one launch (start us, length us, event | category | flops | bytes accessed | tf_op | source)
XLA Modules:
  0.0 85.6 jit_solution(13170527968301021982)
XLA Ops:
  2.0 1.2 %copy-done = bf16[128,3584]{1,0:T(8,128)(2,1)S(1)} copy-done((bf16[128,3584]{1,0:T(8,128)(2,1)S(1)}, bf16[128,3584]{1,0:T(8,128)(2,1)}, u32[]{:S(2)}) %copy-start) | copy-done | bytes 917528
  3.2 1.2 %copy-done.1 = bf16[128,3584]{1,0:T(8,128)(2,1)S(1)} copy-done((bf16[128,3584]{1,0:T(8,128)(2,1)S(1)}, bf16[128,3584]{1,0:T(8,128)(2,1)}, u32[]{:S(2)}) %copy-start.1) | copy-done | bytes 917528
  4.4 1.2 %route.1 = (bf16[16,896]{1,0:T(8,128)(2,1)S(1)}, bf16[16,896]{1,0:T(8,128)(2,1)S(1)}, bf16[16,896]{1,0:T(8,128)(2,1)S(1)}, bf16[16,896]{1,0:T(8,128)(2,1)S(1)}, f32[1,8,128]{2,1,0:T(8,128)S(1)}) custom-call(s32[1]{0:T(128)} %bitcast.me, s32[1]{0:T(128)S(6)} %copy.23.live_in, s32[1,1]{1,0:T(1,128)S(6)} %copy.24.plan_in, s32[8,128]{1,0:T(8,128)S(1)} %bitcast.6, ...), custom_call_target="tpu_custom_call" | custom-call | flops 14680064 | bytes 118784 | tf_op jit(solution)/shard_map/route/pallas_call | solution.py:31
  5.6 3.0 %collective-permute-start = (bf16[16,896]{1,0:T(8,128)(2,1)S(1)}, bf16[16,896]{1,0:T(8,128)(2,1)S(1)}, u32[]{:S(2)}, u32[]{:S(2)}) collective-permute-start(bf16[16,896]{1,0:T(8,128)(2,1)S(1)} %get-tuple-element.27), channel_id=1, source_target_pairs={{0,8},{8,0},{16,24},{24,16},{1,9},{9,1},{17,25},{25,17},{2,10},{10... | collective-permute-start | bytes 86024 | tf_op jit(solution)/shard_map/ppermute | solution.py:50
  8.6 1.5 %collective-permute-start.1 = (bf16[16,896]{1,0:T(8,128)(2,1)S(1)}, bf16[16,896]{1,0:T(8,128)(2,1)S(1)}, u32[]{:S(2)}, u32[]{:S(2)}) collective-permute-start(bf16[16,896]{1,0:T(8,128)(2,1)S(1)} %get-tuple-element.28), channel_id=1, source_target_pairs={{0,16},{8,24},{16,0},{24,8},{1,17},{9,25},{17,1},{25,9},{2,18},{10... | collective-permute-start | bytes 86024 | tf_op jit(solution)/shard_map/ppermute | solution.py:50
  10.1 0.3 collective-permute-done
  10.5 2.0 %collective-permute-done.1 = bf16[16,896]{1,0:T(8,128)(2,1)S(1)} collective-permute-done((bf16[16,896]{1,0:T(8,128)(2,1)S(1)}, bf16[16,896]{1,0:T(8,128)(2,1)S(1)}, u32[]{:S(2)}, u32[]{:S(2)}) %collective-permute-start.1) | collective-permute-done | bytes 28704 | tf_op jit(solution)/shard_map/ppermute | solution.py:50
  12.5 2.4 %collective-permute-done.2 = bf16[16,896]{1,0:T(8,128)(2,1)S(1)} collective-permute-done((bf16[16,896]{1,0:T(8,128)(2,1)S(1)}, bf16[16,896]{1,0:T(8,128)(2,1)S(1)}, u32[]{:S(2)}, u32[]{:S(2)}) %collective-permute-start.2) | collective-permute-done | bytes 28704 | tf_op jit(solution)/shard_map/ppermute | solution.py:50
  15.0 0.6 copy-done.9
  15.6 0.9 %weights.1 = (bf16[896,512]{1,0:T(8,128)(2,1)S(1)}, bf16[256,896]{1,0:T(8,128)(2,1)S(1)}) custom-call(s32[1]{0:T(128)S(6)} %mul.3.first, f32[2,28]{1,0:T(2,128)S(1)} %bitcast.8, f32[2,28]{1,0:T(2,128)S(1)} %bitcast.9, f32[2,28]{1,0:T(2,128)S(1)} %copy-done.10, bf16[64,896]{1,0:T(8,128)(2,1)S(1)} %constant_dynamic-update-slice_fusion.after.refs_0_, ...), custom_call_target="tpu_custom_call" | custom-call | flops 1376256 | bytes 2752512 | tf_op jit(solution)/shard_map/weights/pallas_call | solution.py:31
  16.5 0.6 collective-permute-start.19
  17.1 19.8 %collective-permute-done.19.refs_4_ = bf16[896,512]{1,0:T(8,128)(2,1)S(1)} collective-permute-done((bf16[896,512]{1,0:T(8,128)(2,1)S(1)}, bf16[896,512]{1,0:T(8,128)(2,1)S(1)}, u32[]{:S(2)}, u32[]{:S(2)}) %collective-permute-start.19) | collective-permute-done | bytes 917536 | tf_op jit(solution)/shard_map/ppermute | solution.py:50
  37.0 0.5 collective-permute-start.11
  37.5 1.6 %collective-permute-start.3 = (bf16[64,896]{1,0:T(8,128)(2,1)S(1)}, bf16[64,896]{1,0:T(8,128)(2,1)S(1)}, u32[]{:S(2)}, u32[]{:S(2)}) collective-permute-start(bf16[64,896]{1,0:T(8,128)(2,1)S(1)} %constant_dynamic-update-slice_fusion.after.refs_0_), channel_id=1, source_target_pairs={{0,2},{1,3},{2,0},{3,1},{4,6},{5,7},{6,4},{7,5},{8,10},{9,11},{10,... | collective-permute-start | bytes 344072 | tf_op jit(solution)/shard_map/ppermute | solution.py:50
  39.1 2.6 %collective-permute-start.4 = (bf16[64,896]{1,0:T(8,128)(2,1)S(1)}, bf16[64,896]{1,0:T(8,128)(2,1)S(1)}, u32[]{:S(2)}, u32[]{:S(2)}) collective-permute-start(bf16[64,896]{1,0:T(8,128)(2,1)S(1)} %constant_dynamic-update-slice_fusion.after.refs_0_), channel_id=1, source_target_pairs={{0,4},{1,5},{2,6},{3,7},{4,0},{5,1},{6,2},{7,3},{8,12},{9,13},{10,... | collective-permute-start | bytes 344072 | tf_op jit(solution)/shard_map/ppermute | solution.py:50
  41.6 2.4 %collective-permute-done.3.refs_1_ = bf16[64,896]{1,0:T(8,128)(2,1)S(1)} collective-permute-done((bf16[64,896]{1,0:T(8,128)(2,1)S(1)}, bf16[64,896]{1,0:T(8,128)(2,1)S(1)}, u32[]{:S(2)}, u32[]{:S(2)}) %collective-permute-start.3) | collective-permute-done | bytes 114720 | tf_op jit(solution)/shard_map/ppermute | solution.py:50
  44.0 3.3 %collective-permute-start.5 = (bf16[64,896]{1,0:T(8,128)(2,1)S(1)}, bf16[64,896]{1,0:T(8,128)(2,1)S(1)}, u32[]{:S(2)}, u32[]{:S(2)}) collective-permute-start(bf16[64,896]{1,0:T(8,128)(2,1)S(1)} %constant_dynamic-update-slice_fusion.after.refs_0_), channel_id=1, source_target_pairs={{0,6},{1,7},{2,4},{3,5},{4,2},{5,3},{6,0},{7,1},{8,14},{9,15},{10,... | collective-permute-start | bytes 344072 | tf_op jit(solution)/shard_map/ppermute | solution.py:50
  47.4 1.4 %collective-permute-done.4.refs_2_ = bf16[64,896]{1,0:T(8,128)(2,1)S(1)} collective-permute-done((bf16[64,896]{1,0:T(8,128)(2,1)S(1)}, bf16[64,896]{1,0:T(8,128)(2,1)S(1)}, u32[]{:S(2)}, u32[]{:S(2)}) %collective-permute-start.4) | collective-permute-done | bytes 114720 | tf_op jit(solution)/shard_map/ppermute | solution.py:50
  48.7 2.0 %collective-permute-done.5.refs_3_ = bf16[64,896]{1,0:T(8,128)(2,1)S(1)} collective-permute-done((bf16[64,896]{1,0:T(8,128)(2,1)S(1)}, bf16[64,896]{1,0:T(8,128)(2,1)S(1)}, u32[]{:S(2)}, u32[]{:S(2)}) %collective-permute-start.5) | collective-permute-done | bytes 114720 | tf_op jit(solution)/shard_map/ppermute | solution.py:50
  50.7 0.7 partial.1
  51.5 0.6 collective-permute-start.12
  52.1 0.5 collective-permute-start.13
  52.6 2.4 %collective-permute-start.14 = (bf16[32,1536]{1,0:T(8,128)(2,1)S(1)}, bf16[32,1536]{1,0:T(8,128)(2,1)S(1)}, u32[]{:S(2)}, u32[]{:S(2)}) collective-permute-start(bf16[32,1536]{1,0:T(8,128)(2,1)S(1)} %get-tuple-element.35), channel_id=1, source_target_pairs={{0,24},{8,16},{16,8},{24,0},{1,25},{9,17},{17,9},{25,1},{2,26},{10... | collective-permute-start | bytes 294920 | tf_op jit(solution)/shard_map/ppermute | solution.py:50
  55.0 1.1 %collective-permute-done.12.refs_1_ = bf16[32,1536]{1,0:T(8,128)(2,1)S(1)} collective-permute-done((bf16[32,1536]{1,0:T(8,128)(2,1)S(1)}, bf16[32,1536]{1,0:T(8,128)(2,1)S(1)}, u32[]{:S(2)}, u32[]{:S(2)}) %collective-permute-start.12) | collective-permute-done | bytes 98336 | tf_op jit(solution)/shard_map/ppermute | solution.py:50
  56.1 0.5 collective-permute-done.13.refs_2_
  56.7 1.5 %collective-permute-done.14.refs_3_ = bf16[32,1536]{1,0:T(8,128)(2,1)S(1)} collective-permute-done((bf16[32,1536]{1,0:T(8,128)(2,1)S(1)}, bf16[32,1536]{1,0:T(8,128)(2,1)S(1)}, u32[]{:S(2)}, u32[]{:S(2)}) %collective-permute-start.14) | collective-permute-done | bytes 98336 | tf_op jit(solution)/shard_map/ppermute | solution.py:50
  58.3 1.6 %collective-permute-start.16 = (bf16[32,1536]{1,0:T(8,128)(2,1)S(1)}, bf16[32,1536]{1,0:T(8,128)(2,1)S(1)}, u32[]{:S(2)}, u32[]{:S(2)}) collective-permute-start(bf16[32,1536]{1,0:T(8,128)(2,1)S(1)} %activations.1.refs_0_), channel_id=1, source_target_pairs={{0,16},{8,24},{16,0},{24,8},{1,17},{9,25},{17,1},{25,9},{2,18},{10... | collective-permute-start | bytes 294920 | tf_op jit(solution)/shard_map/ppermute | solution.py:50
  59.9 1.5 %collective-permute-start.15 = (bf16[32,1536]{1,0:T(8,128)(2,1)S(1)}, bf16[32,1536]{1,0:T(8,128)(2,1)S(1)}, u32[]{:S(2)}, u32[]{:S(2)}) collective-permute-start(bf16[32,1536]{1,0:T(8,128)(2,1)S(1)} %activations.1.refs_0_), channel_id=1, source_target_pairs={{0,8},{8,0},{16,24},{24,16},{1,9},{9,1},{17,25},{25,17},{2,10},{10... | collective-permute-start | bytes 294920 | tf_op jit(solution)/shard_map/ppermute | solution.py:50
  61.3 0.5 collective-permute-start.17
  61.8 1.1 %collective-permute-done.16.refs_2_.refs_1_ = bf16[32,1536]{1,0:T(8,128)(2,1)S(1)} collective-permute-done((bf16[32,1536]{1,0:T(8,128)(2,1)S(1)}, bf16[32,1536]{1,0:T(8,128)(2,1)S(1)}, u32[]{:S(2)}, u32[]{:S(2)}) %collective-permute-start.16) | collective-permute-done | bytes 98336 | tf_op jit(solution)/shard_map/ppermute | solution.py:50
  63.0 1.5 %collective-permute-done.15.refs_1_ = bf16[32,1536]{1,0:T(8,128)(2,1)S(1)} collective-permute-done((bf16[32,1536]{1,0:T(8,128)(2,1)S(1)}, bf16[32,1536]{1,0:T(8,128)(2,1)S(1)}, u32[]{:S(2)}, u32[]{:S(2)}) %collective-permute-start.15) | collective-permute-done | bytes 98336 | tf_op jit(solution)/shard_map/ppermute | solution.py:50
  64.5 2.4 %collective-permute-done.17.refs_3_ = bf16[32,1536]{1,0:T(8,128)(2,1)S(1)} collective-permute-done((bf16[32,1536]{1,0:T(8,128)(2,1)S(1)}, bf16[32,1536]{1,0:T(8,128)(2,1)S(1)}, u32[]{:S(2)}, u32[]{:S(2)}) %collective-permute-start.17) | collective-permute-done | bytes 98336 | tf_op jit(solution)/shard_map/ppermute | solution.py:50
  66.9 0.1 collective-permute-start.18
  67.0 0.5 collective-permute-start.6
  67.5 0.1 collective-permute-start.7
  67.5 0.4 collective-permute-start.8
  68.0 0.1 collective-permute-start.9
  68.1 1.2 %dx.1 = (f32[16,1792]{1,0:T(8,128)S(1)}, bf16[16,1792]{1,0:T(8,128)(2,1)S(1)}, bf16[16,1792]{1,0:T(8,128)(2,1)S(1)}, bf16[16,1792]{1,0:T(8,128)(2,1)S(1)}) custom-call(bf16[32,1536]{1,0:T(8,128)(2,1)S(1)} %activations.1.refs_0_, bf16[32,1536]{1,0:T(8,128)(2,1)S(1)} %collective-permute-done.16.refs_2_.refs_1_, ...), custom_call_target="tpu_custom_call" | custom-call | flops 234881024 | bytes 4153344 | tf_op jit(solution)/shard_map/dx/pallas_call | solution.py:31
  69.3 2.0 %collective-permute-start.21 = (bf16[16,1792]{1,0:T(8,128)(2,1)S(1)}, bf16[16,1792]{1,0:T(8,128)(2,1)S(1)}, u32[]{:S(2)}, u32[]{:S(2)}) collective-permute-start(bf16[16,1792]{1,0:T(8,128)(2,1)S(1)} %get-tuple-element.40), channel_id=1, source_target_pairs={{0,2},{1,3},{2,0},{3,1},{4,6},{5,7},{6,4},{7,5},{8,10},{9,11},{10,... | collective-permute-start | bytes 172040 | tf_op jit(solution)/shard_map/ppermute | solution.py:50
  71.2 1.9 %collective-permute-start.22 = (bf16[16,1792]{1,0:T(8,128)(2,1)S(1)}, bf16[16,1792]{1,0:T(8,128)(2,1)S(1)}, u32[]{:S(2)}, u32[]{:S(2)}) collective-permute-start(bf16[16,1792]{1,0:T(8,128)(2,1)S(1)} %get-tuple-element.41), channel_id=1, source_target_pairs={{0,4},{1,5},{2,6},{3,7},{4,0},{5,1},{6,2},{7,3},{8,12},{9,13},{10,... | collective-permute-start | bytes 172040 | tf_op jit(solution)/shard_map/ppermute | solution.py:50
  73.2 0.7 collective-permute-start.23
  73.9 1.5 %gradients.1 = (bf16[896,256]{1,0:T(8,128)(2,1)}, bf16[896,256]{1,0:T(8,128)(2,1)}, bf16[256,896]{1,0:T(8,128)(2,1)}) custom-call(bf16[64,896]{1,0:T(8,128)(2,1)S(1)} %constant_dynamic-update-slice_fusion.after.refs_0_, bf16[64,896]{1,0:T(8,128)(2,1)S(1)} %collective-permute-done.3.refs_1_, bf16[64,896]{1,0:T(8,128)(2,1)S(1)} %collective-permute-done.4.refs_2_, ...), custom_call_target="tpu_custom_call" | custom-call | flops 352321536 | bytes 2686976 | tf_op jit(solution)/shard_map/gradients/pallas_call | solution.py:31
  75.4 3.0 %collective-permute-done.22.refs_3_ = bf16[16,1792]{1,0:T(8,128)(2,1)S(1)} collective-permute-done((bf16[16,1792]{1,0:T(8,128)(2,1)S(1)}, bf16[16,1792]{1,0:T(8,128)(2,1)S(1)}, u32[]{:S(2)}, u32[]{:S(2)}) %collective-permute-start.22) | collective-permute-done | bytes 57376 | tf_op jit(solution)/shard_map/ppermute | solution.py:50
  78.4 0.8 collective-permute-done.23.refs_4_
  79.3 1.0 %copy-done.5 = bf16[896,256]{1,0:T(8,128)(2,1)S(1)} copy-done((bf16[896,256]{1,0:T(8,128)(2,1)S(1)}, bf16[896,256]{1,0:T(8,128)(2,1)}, u32[]{:S(2)}) %copy-start.5) | copy-done | bytes 458776
  80.3 0.8 collective-permute-start.24
  81.1 3.1 %collective-permute-done.24.refs_1_ = bf16[8,1792]{1,0:T(8,128)(2,1)S(1)} collective-permute-done((bf16[8,1792]{1,0:T(8,128)(2,1)S(1)}, bf16[8,1792]{1,0:T(8,128)(2,1)S(1)}, u32[]{:S(2)}, u32[]{:S(2)}) %collective-permute-start.24) | collective-permute-done | bytes 28704 | tf_op jit(solution)/shard_map/ppermute | solution.py:50
  84.3 1.3 %place.1 = bf16[128,3584]{1,0:T(8,128)(2,1)} custom-call(s32[1]{0:T(128)} %bitcast.me, s32[1]{0:T(128)} %bitcast.1.home, bf16[8,1792]{1,0:T(8,128)(2,1)S(1)} %get-tuple-element.43.refs_0_, bf16[8,1792]{1,0:T(8,128)(2,1)S(1)} %collective-permute-done.24.refs_1_, f32[1,8,128]{2,1,0:T(8,128)S(1)} %get-tuple-element.45.refs_2_), custom_call_target="tpu_custom_call" | custom-call | flops 7340032 | bytes 978944 | tf_op jit(solution)/shard_map/place/pallas_call | solution.py:31
  (41 shorter events, 0.3 us)
Async XLA Ops:
  0.6 1.3 %copy-start.7 = (f32[128,8]{0,1:T(8,128)S(1)}, f32[128,8]{0,1:T(8,128)}, u32[]{:S(2)}) copy-start(f32[128,8]{0,1:T(8,128)} %param.14) | copy-start | bytes 12292
  1.3 0.7 copy-start.6
  2.0 1.2 %copy-start = (bf16[128,3584]{1,0:T(8,128)(2,1)S(1)}, bf16[128,3584]{1,0:T(8,128)(2,1)}, u32[]{:S(2)}) copy-start(bf16[128,3584]{1,0:T(8,128)(2,1)} %tokens_in.1) | copy-start | bytes 2752516
  3.2 1.2 %copy-start.1 = (bf16[128,3584]{1,0:T(8,128)(2,1)S(1)}, bf16[128,3584]{1,0:T(8,128)(2,1)}, u32[]{:S(2)}) copy-start(bf16[128,3584]{1,0:T(8,128)(2,1)} %cots_in.1) | copy-start | bytes 2752516
  4.4 10.6 %copy-start.2 = (bf16[896,256]{1,0:T(8,128)(2,1)S(1)}, bf16[896,256]{1,0:T(8,128)(2,1)}, u32[]{:S(2)}) copy-start(bf16[896,256]{1,0:T(8,128)(2,1)} %gate.1) | copy-start | bytes 1376260
  4.4 10.6 %copy-start.3 = (bf16[896,256]{1,0:T(8,128)(2,1)S(1)}, bf16[896,256]{1,0:T(8,128)(2,1)}, u32[]{:S(2)}) copy-start(bf16[896,256]{1,0:T(8,128)(2,1)} %up.1) | copy-start | bytes 1376260
  4.4 10.6 %copy-start.4 = (bf16[256,896]{1,0:T(8,128)(2,1)S(1)}, bf16[256,896]{1,0:T(8,128)(2,1)}, u32[]{:S(2)}) copy-start(bf16[256,896]{1,0:T(8,128)(2,1)} %down.1) | copy-start | bytes 1376260
  5.6 4.9 %collective-permute-start = (bf16[16,896]{1,0:T(8,128)(2,1)S(1)}, bf16[16,896]{1,0:T(8,128)(2,1)S(1)}, u32[]{:S(2)}, u32[]{:S(2)}) collective-permute-start(bf16[16,896]{1,0:T(8,128)(2,1)S(1)} %get-tuple-element.27), channel_id=1, source_target_pairs={{0,8},{8,0},{16,24},{24,16},{1,9},{9,1},{17,25},{25,17},{2,10},{10... | collective-permute-start | bytes 86024 | tf_op jit(solution)/shard_map/ppermute | solution.py:50
  8.6 3.9 %collective-permute-start.1 = (bf16[16,896]{1,0:T(8,128)(2,1)S(1)}, bf16[16,896]{1,0:T(8,128)(2,1)S(1)}, u32[]{:S(2)}, u32[]{:S(2)}) collective-permute-start(bf16[16,896]{1,0:T(8,128)(2,1)S(1)} %get-tuple-element.28), channel_id=1, source_target_pairs={{0,16},{8,24},{16,0},{24,8},{1,17},{9,25},{17,1},{25,9},{2,18},{10... | collective-permute-start | bytes 86024 | tf_op jit(solution)/shard_map/ppermute | solution.py:50
  10.1 4.8 %collective-permute-start.2 = (bf16[16,896]{1,0:T(8,128)(2,1)S(1)}, bf16[16,896]{1,0:T(8,128)(2,1)S(1)}, u32[]{:S(2)}, u32[]{:S(2)}) collective-permute-start(bf16[16,896]{1,0:T(8,128)(2,1)S(1)} %get-tuple-element.29), channel_id=1, source_target_pairs={{0,24},{8,16},{16,8},{24,0},{1,25},{9,17},{17,9},{25,1},{2,26},{10... | collective-permute-start | bytes 86024 | tf_op jit(solution)/shard_map/ppermute | solution.py:50
  14.9 0.7 copy-start.9
  14.9 0.7 copy-start.10
  15.0 0.7 copy-start.8
  16.5 20.4 %collective-permute-start.19 = (bf16[896,512]{1,0:T(8,128)(2,1)S(1)}, bf16[896,512]{1,0:T(8,128)(2,1)S(1)}, u32[]{:S(2)}, u32[]{:S(2)}) collective-permute-start(bf16[896,512]{1,0:T(8,128)(2,1)S(1)} %get-tuple-element.30.refs_4_.refs_2_), channel_id=1, source_target_pairs={{0,8},{8,0},{16,24},{24,16},{1,9},{9,1},{17,25},{25,17},{2,10},{10... | collective-permute-start | bytes 2752520 | tf_op jit(solution)/shard_map/ppermute | solution.py:50
  17.1 33.6 %collective-permute-start.10 = (bf16[896,512]{1,0:T(8,128)(2,1)S(1)}, bf16[896,512]{1,0:T(8,128)(2,1)S(1)}, u32[]{:S(2)}, u32[]{:S(2)}) collective-permute-start(bf16[896,512]{1,0:T(8,128)(2,1)S(1)} %get-tuple-element.30.refs_4_.refs_2_), channel_id=1, source_target_pairs={{0,1},{1,0},{2,3},{3,2},{4,5},{5,4},{6,7},{7,6},{8,9},{9,8},{10,11... | collective-permute-start | bytes 2752520 | tf_op jit(solution)/shard_map/ppermute | solution.py:50
  37.0 31.0 %collective-permute-start.20 = (bf16[896,512]{1,0:T(8,128)(2,1)S(1)}, bf16[896,512]{1,0:T(8,128)(2,1)S(1)}, u32[]{:S(2)}, u32[]{:S(2)}) collective-permute-start(bf16[896,512]{1,0:T(8,128)(2,1)S(1)} %collective-permute-done.19.refs_4_), channel_id=1, source_target_pairs={{0,1},{1,0},{2,3},{3,2},{4,5},{5,4},{6,7},{7,6},{8,9},{9,8},{10,11... | collective-permute-start | bytes 2752520 | tf_op jit(solution)/shard_map/ppermute | solution.py:50
  37.0 13.8 %collective-permute-start.11 = (bf16[256,896]{1,0:T(8,128)(2,1)S(1)}, bf16[256,896]{1,0:T(8,128)(2,1)S(1)}, u32[]{:S(2)}, u32[]{:S(2)}) collective-permute-start(bf16[256,896]{1,0:T(8,128)(2,1)S(1)} %get-tuple-element.31.refs_5_), channel_id=1, source_target_pairs={{0,1},{1,0},{2,3},{3,2},{4,5},{5,4},{6,7},{7,6},{8,9},{9,8},{10,11... | collective-permute-start | bytes 1376264 | tf_op jit(solution)/shard_map/ppermute | solution.py:50
  37.5 6.5 %collective-permute-start.3 = (bf16[64,896]{1,0:T(8,128)(2,1)S(1)}, bf16[64,896]{1,0:T(8,128)(2,1)S(1)}, u32[]{:S(2)}, u32[]{:S(2)}) collective-permute-start(bf16[64,896]{1,0:T(8,128)(2,1)S(1)} %constant_dynamic-update-slice_fusion.after.refs_0_), channel_id=1, source_target_pairs={{0,2},{1,3},{2,0},{3,1},{4,6},{5,7},{6,4},{7,5},{8,10},{9,11},{10,... | collective-permute-start | bytes 344072 | tf_op jit(solution)/shard_map/ppermute | solution.py:50
  39.1 9.7 %collective-permute-start.4 = (bf16[64,896]{1,0:T(8,128)(2,1)S(1)}, bf16[64,896]{1,0:T(8,128)(2,1)S(1)}, u32[]{:S(2)}, u32[]{:S(2)}) collective-permute-start(bf16[64,896]{1,0:T(8,128)(2,1)S(1)} %constant_dynamic-update-slice_fusion.after.refs_0_), channel_id=1, source_target_pairs={{0,4},{1,5},{2,6},{3,7},{4,0},{5,1},{6,2},{7,3},{8,12},{9,13},{10,... | collective-permute-start | bytes 344072 | tf_op jit(solution)/shard_map/ppermute | solution.py:50
  44.0 6.7 %collective-permute-start.5 = (bf16[64,896]{1,0:T(8,128)(2,1)S(1)}, bf16[64,896]{1,0:T(8,128)(2,1)S(1)}, u32[]{:S(2)}, u32[]{:S(2)}) collective-permute-start(bf16[64,896]{1,0:T(8,128)(2,1)S(1)} %constant_dynamic-update-slice_fusion.after.refs_0_), channel_id=1, source_target_pairs={{0,6},{1,7},{2,4},{3,5},{4,2},{5,3},{6,0},{7,1},{8,14},{9,15},{10,... | collective-permute-start | bytes 344072 | tf_op jit(solution)/shard_map/ppermute | solution.py:50
  51.5 4.7 %collective-permute-start.12 = (bf16[32,1536]{1,0:T(8,128)(2,1)S(1)}, bf16[32,1536]{1,0:T(8,128)(2,1)S(1)}, u32[]{:S(2)}, u32[]{:S(2)}) collective-permute-start(bf16[32,1536]{1,0:T(8,128)(2,1)S(1)} %get-tuple-element.33), channel_id=1, source_target_pairs={{0,8},{8,0},{16,24},{24,16},{1,9},{9,1},{17,25},{25,17},{2,10},{10... | collective-permute-start | bytes 294920 | tf_op jit(solution)/shard_map/ppermute | solution.py:50
  52.1 4.6 %collective-permute-start.13 = (bf16[32,1536]{1,0:T(8,128)(2,1)S(1)}, bf16[32,1536]{1,0:T(8,128)(2,1)S(1)}, u32[]{:S(2)}, u32[]{:S(2)}) collective-permute-start(bf16[32,1536]{1,0:T(8,128)(2,1)S(1)} %get-tuple-element.34), channel_id=1, source_target_pairs={{0,16},{8,24},{16,0},{24,8},{1,17},{9,25},{17,1},{25,9},{2,18},{10... | collective-permute-start | bytes 294920 | tf_op jit(solution)/shard_map/ppermute | solution.py:50
  52.6 5.6 %collective-permute-start.14 = (bf16[32,1536]{1,0:T(8,128)(2,1)S(1)}, bf16[32,1536]{1,0:T(8,128)(2,1)S(1)}, u32[]{:S(2)}, u32[]{:S(2)}) collective-permute-start(bf16[32,1536]{1,0:T(8,128)(2,1)S(1)} %get-tuple-element.35), channel_id=1, source_target_pairs={{0,24},{8,16},{16,8},{24,0},{1,25},{9,17},{17,9},{25,1},{2,26},{10... | collective-permute-start | bytes 294920 | tf_op jit(solution)/shard_map/ppermute | solution.py:50
  58.3 4.7 %collective-permute-start.16 = (bf16[32,1536]{1,0:T(8,128)(2,1)S(1)}, bf16[32,1536]{1,0:T(8,128)(2,1)S(1)}, u32[]{:S(2)}, u32[]{:S(2)}) collective-permute-start(bf16[32,1536]{1,0:T(8,128)(2,1)S(1)} %activations.1.refs_0_), channel_id=1, source_target_pairs={{0,16},{8,24},{16,0},{24,8},{1,17},{9,25},{17,1},{25,9},{2,18},{10... | collective-permute-start | bytes 294920 | tf_op jit(solution)/shard_map/ppermute | solution.py:50
  59.9 4.6 %collective-permute-start.15 = (bf16[32,1536]{1,0:T(8,128)(2,1)S(1)}, bf16[32,1536]{1,0:T(8,128)(2,1)S(1)}, u32[]{:S(2)}, u32[]{:S(2)}) collective-permute-start(bf16[32,1536]{1,0:T(8,128)(2,1)S(1)} %activations.1.refs_0_), channel_id=1, source_target_pairs={{0,8},{8,0},{16,24},{24,16},{1,9},{9,1},{17,25},{25,17},{2,10},{10... | collective-permute-start | bytes 294920 | tf_op jit(solution)/shard_map/ppermute | solution.py:50
  61.3 5.5 %collective-permute-start.17 = (bf16[32,1536]{1,0:T(8,128)(2,1)S(1)}, bf16[32,1536]{1,0:T(8,128)(2,1)S(1)}, u32[]{:S(2)}, u32[]{:S(2)}) collective-permute-start(bf16[32,1536]{1,0:T(8,128)(2,1)S(1)} %activations.1.refs_0_), channel_id=1, source_target_pairs={{0,24},{8,16},{16,8},{24,0},{1,25},{9,17},{17,9},{25,1},{2,26},{10... | collective-permute-start | bytes 294920 | tf_op jit(solution)/shard_map/ppermute | solution.py:50
  66.9 7.0 %collective-permute-start.18 = (bf16[128,768]{1,0:T(8,128)(2,1)S(1)}, bf16[128,768]{1,0:T(8,128)(2,1)S(1)}, u32[]{:S(2)}, u32[]{:S(2)}) collective-permute-start(bf16[128,768]{1,0:T(8,128)(2,1)S(1)} %get-tuple-element.37), channel_id=1, source_target_pairs={{0,1},{1,0},{2,3},{3,2},{4,5},{5,4},{6,7},{7,6},{8,9},{9,8},{10,11... | collective-permute-start | bytes 589832 | tf_op jit(solution)/shard_map/ppermute | solution.py:50
  67.0 2.3 %collective-permute-start.6 = (bf16[64,896]{1,0:T(8,128)(2,1)S(1)}, bf16[64,896]{1,0:T(8,128)(2,1)S(1)}, u32[]{:S(2)}, u32[]{:S(2)}) collective-permute-start(bf16[64,896]{1,0:T(8,128)(2,1)S(1)} %constant_dynamic-update-slice_fusion.after.refs_0_), channel_id=1, source_target_pairs={{0,1},{1,0},{2,3},{3,2},{4,5},{5,4},{6,7},{7,6},{8,9},{9,8},{10,11... | collective-permute-start | bytes 344072 | tf_op jit(solution)/shard_map/ppermute | solution.py:50
  67.5 3.8 %collective-permute-start.7 = (bf16[64,896]{1,0:T(8,128)(2,1)S(1)}, bf16[64,896]{1,0:T(8,128)(2,1)S(1)}, u32[]{:S(2)}, u32[]{:S(2)}) collective-permute-start(bf16[64,896]{1,0:T(8,128)(2,1)S(1)} %collective-permute-done.3.refs_1_), channel_id=1, source_target_pairs={{0,1},{1,0},{2,3},{3,2},{4,5},{5,4},{6,7},{7,6},{8,9},{9,8},{10,11... | collective-permute-start | bytes 344072 | tf_op jit(solution)/shard_map/ppermute | solution.py:50
  67.5 5.6 %collective-permute-start.8 = (bf16[64,896]{1,0:T(8,128)(2,1)S(1)}, bf16[64,896]{1,0:T(8,128)(2,1)S(1)}, u32[]{:S(2)}, u32[]{:S(2)}) collective-permute-start(bf16[64,896]{1,0:T(8,128)(2,1)S(1)} %collective-permute-done.4.refs_2_), channel_id=1, source_target_pairs={{0,1},{1,0},{2,3},{3,2},{4,5},{5,4},{6,7},{7,6},{8,9},{9,8},{10,11... | collective-permute-start | bytes 344072 | tf_op jit(solution)/shard_map/ppermute | solution.py:50
  68.0 5.9 %collective-permute-start.9 = (bf16[64,896]{1,0:T(8,128)(2,1)S(1)}, bf16[64,896]{1,0:T(8,128)(2,1)S(1)}, u32[]{:S(2)}, u32[]{:S(2)}) collective-permute-start(bf16[64,896]{1,0:T(8,128)(2,1)S(1)} %collective-permute-done.5.refs_3_), channel_id=1, source_target_pairs={{0,1},{1,0},{2,3},{3,2},{4,5},{5,4},{6,7},{7,6},{8,9},{9,8},{10,11... | collective-permute-start | bytes 344072 | tf_op jit(solution)/shard_map/ppermute | solution.py:50
  69.3 6.1 %collective-permute-start.21 = (bf16[16,1792]{1,0:T(8,128)(2,1)S(1)}, bf16[16,1792]{1,0:T(8,128)(2,1)S(1)}, u32[]{:S(2)}, u32[]{:S(2)}) collective-permute-start(bf16[16,1792]{1,0:T(8,128)(2,1)S(1)} %get-tuple-element.40), channel_id=1, source_target_pairs={{0,2},{1,3},{2,0},{3,1},{4,6},{5,7},{6,4},{7,5},{8,10},{9,11},{10,... | collective-permute-start | bytes 172040 | tf_op jit(solution)/shard_map/ppermute | solution.py:50
  71.2 7.2 %collective-permute-start.22 = (bf16[16,1792]{1,0:T(8,128)(2,1)S(1)}, bf16[16,1792]{1,0:T(8,128)(2,1)S(1)}, u32[]{:S(2)}, u32[]{:S(2)}) collective-permute-start(bf16[16,1792]{1,0:T(8,128)(2,1)S(1)} %get-tuple-element.41), channel_id=1, source_target_pairs={{0,4},{1,5},{2,6},{3,7},{4,0},{5,1},{6,2},{7,3},{8,12},{9,13},{10,... | collective-permute-start | bytes 172040 | tf_op jit(solution)/shard_map/ppermute | solution.py:50
  73.2 6.1 %collective-permute-start.23 = (bf16[16,1792]{1,0:T(8,128)(2,1)S(1)}, bf16[16,1792]{1,0:T(8,128)(2,1)S(1)}, u32[]{:S(2)}, u32[]{:S(2)}) collective-permute-start(bf16[16,1792]{1,0:T(8,128)(2,1)S(1)} %get-tuple-element.42), channel_id=1, source_target_pairs={{0,6},{1,7},{2,4},{3,5},{4,2},{5,3},{6,0},{7,1},{8,14},{9,15},{10,... | collective-permute-start | bytes 172040 | tf_op jit(solution)/shard_map/ppermute | solution.py:50
  79.3 1.0 %copy-start.5 = (bf16[896,256]{1,0:T(8,128)(2,1)S(1)}, bf16[896,256]{1,0:T(8,128)(2,1)}, u32[]{:S(2)}) copy-start(bf16[896,256]{1,0:T(8,128)(2,1)} %get-tuple-element.23.refs_0_) | copy-start | bytes 1376260
  80.3 3.9 %collective-permute-start.24 = (bf16[8,1792]{1,0:T(8,128)(2,1)S(1)}, bf16[8,1792]{1,0:T(8,128)(2,1)S(1)}, u32[]{:S(2)}, u32[]{:S(2)}) collective-permute-start(bf16[8,1792]{1,0:T(8,128)(2,1)S(1)} %get-tuple-element.44), channel_id=1, source_target_pairs={{0,16},{8,24},{16,0},{24,8},{1,17},{9,25},{17,1},{25,9},{2,18},{10... | collective-permute-start | bytes 86024 | tf_op jit(solution)/shard_map/ppermute | solution.py:50

commit v3 on v2

v3 whole, which is shorter than its diff:
```python
import functools
import math

import jax
import jax.numpy as jnp
from jax import lax
from jax.experimental import pallas as pl
from jax.experimental.pallas import tpu as pltpu
from jax.sharding import PartitionSpec as P

HSH = 8
CAP = 4
ROWS = 2 * CAP
BLOCK = 128
CHIPS = HSH // 2
BF16 = jnp.bfloat16
F32 = jnp.float32
VMEM_BYTES = 40 * 1024 * 1024
ROUTE_VMEM_BYTES = 62 * 1024 * 1024

NN = (((1,), (0,)), ((), ()))
NT = (((1,), (1,)), ((), ()))
TN = (((0,), (0,)), ((), ()))


def mm(a, b, dims):
    return lax.dot_general(a, b, dims, preferred_element_type=F32)


def call(kernel, outs, scalars, arrays, hbm=(), after=(), scratch=(), flops=0, name=None, far_out=False, limit=VMEM_BYTES):
    moved = sum(math.prod(x.shape) * x.dtype.itemsize for x in (*hbm, *arrays, *outs))
    count = len(scalars) + len(hbm)

    def body(*refs):
        kernel(*refs[:count], *refs[count + len(after) :])

    return pl.pallas_call(
        body,
        out_shape=outs,
        in_specs=[pl.BlockSpec(memory_space=pltpu.SMEM)] * len(scalars)
        + [pl.BlockSpec(memory_space=pltpu.HBM)] * len(hbm)
        + [pl.BlockSpec(memory_space=pltpu.VMEM)] * len(after)
        + [pl.BlockSpec(memory_space=pltpu.VMEM)] * len(arrays),
        out_specs=[pl.BlockSpec(memory_space=pltpu.HBM if far_out else pltpu.VMEM)] * len(outs),
        scratch_shapes=list(scratch),
        compiler_params=pltpu.CompilerParams(vmem_limit_bytes=limit),
        cost_estimate=pl.CostEstimate(flops=flops, bytes_accessed=moved, transcendentals=0),
        name=name,
    )(*scalars, *hbm, *after, *arrays)


def fetch(sources, targets, sems):
    copies = [pltpu.make_async_copy(s, t, sems.at[i]) for i, (s, t) in enumerate(zip(sources, targets))]
    for copy in copies:
        copy.start()
    return copies


def shape(dims, dtype=BF16):
    return jax.ShapeDtypeStruct(dims, dtype)


def swap(x, axis, k):
    return lax.ppermute(x, axis, [(i, i ^ k) for i in range(lax.axis_size(axis))])


def rows_of(value, first, count=ROWS):
    return value[first : first + count]


def route_kernel(groups, experts, me, ids_in, weight_in, tokens_in, cots_in, live, plan, *rest):
    outs, picks, scratch = rest[:groups], rest[groups], rest[groups + 1 :]
    ids, weight, tokens, cots, slices, sems = scratch
    count, width = tokens.shape
    depth = width // groups
    small = fetch((ids_in, weight_in), (ids, weight), sems)
    large = []
    if depth % BLOCK == 0:
        cuts = [(slice(None), pl.ds(i * depth, depth)) for i in range(groups)]
    else:
        cuts = [(slice(None), slice(None))]
    for i, cut in enumerate(cuts):
        for source, target, sem in ((tokens_in, tokens, 2 + i), (cots_in, cots, 2 + groups + i)):
            large.append(pltpu.make_async_copy(source.at[cut], target.at[cut], sems.at[sem]))
            large[-1].start()
    for copy in small:
        copy.wait()
    lists = experts * ROWS
    slot = lax.broadcasted_iota(jnp.int32, (1, count), 1)
    line = lax.broadcasted_iota(jnp.int32, (lists, count), 0)
    alive = slot < live[...]
    odd = slot % 2 == 1
    listed = jnp.zeros((lists, count), F32)
    weights = jnp.zeros((lists, count), F32)
    for e in range(experts):
        match = ids[...] == e
        routed = (jnp.sum(jnp.where(match, 1.0, 0.0), axis=0, keepdims=True) > 0.0) & alive
        total = jnp.sum(jnp.where(match, weight[...], 0.0), axis=0, keepdims=True)
        second = odd & (plan[:, e : e + 1] == 1)
        in_first = jnp.where(routed & ~second, 1.0, 0.0)
        in_second = jnp.where(routed & second, 1.0, 0.0)
        is_first = (line >= e * ROWS) & (line < e * ROWS + CAP)
        is_second = (line >= e * ROWS + CAP) & (line < (e + 1) * ROWS)
        listed = jnp.where(is_first, in_first, jnp.where(is_second, in_second, listed))
        weights = jnp.where(is_first | is_second, total, weights)
    before = lax.broadcasted_iota(jnp.int32, (count, count), 0)
    here = lax.broadcasted_iota(jnp.int32, (count, count), 1)
    upto = jnp.where(before <= here, 1.0, 0.0).astype(BF16)
    place = mm(listed.astype(BF16), upto, NN)
    wanted = (line % CAP + 1).astype(F32)
    picked = jnp.where((listed > 0.0) & (place == wanted), 1.0, 0.0)
    column = jnp.sum(picked * weights, axis=1, keepdims=True)
    for e in range(experts):
        picks[e] = rows_of(picked, e * ROWS)
    picked = picked.astype(BF16)
    for s in range(groups):
        for copy in large[2 * s : 2 * s + 2]:
            copy.wait()
        cut = slice(s * depth, (s + 1) * depth)
        token_rows = mm(picked, tokens[:, cut], NN)
        cot_rows = mm(picked, cots[:, cut], NN) * column
        parts = []
        for e in range(experts):
            parts += [rows_of(token_rows, e * ROWS), rows_of(cot_rows, e * ROWS)]
        slices[s] = jnp.concatenate(parts, axis=0).astype(BF16)
    for k in range(groups):
        outs[k][...] = slices[me[0] ^ k]


def weights_kernel(first, scale_gate, scale_up, scale_down, gate, up, down, gate_up, down_out, packed):
    depth, hid = gate.shape
    step = math.gcd(depth, BLOCK)
    for i in range(depth // step):
        block = (first[0] + i * step) // BLOCK
        for h in range(hid // BLOCK):
            at = (slice(i * step, (i + 1) * step), slice(h * BLOCK, (h + 1) * BLOCK))
            to = (at[0], slice(hid + h * BLOCK, hid + (h + 1) * BLOCK))
            for out in (gate_up, packed):
                out[at] = (gate[at].astype(F32) * scale_gate[h, block]).astype(BF16)
                out[to] = (up[at].astype(F32) * scale_up[h, block]).astype(BF16)
    lane = lax.broadcasted_iota(jnp.int32, (1, depth), 1)
    start = first[0] // BLOCK
    last = scale_down.shape[1] - 1
    for h in range(hid // BLOCK):
        spread = jnp.zeros((1, depth), F32) + scale_down[h, start]
        for j in range(1, depth // BLOCK + 2):
            block = jnp.minimum(start + j, last)
            spread = jnp.where(lane >= (start + j) * BLOCK - first[0], scale_down[h, block], spread)
        at = slice(h * BLOCK, (h + 1) * BLOCK)
        value = (down[at, :].astype(F32) * spread).astype(BF16)
        down_out[at, :] = value
        for i, (begin, end) in enumerate(pieces(depth, 2 * hid)):
            top = depth + i * hid + h * BLOCK
            packed[top : top + BLOCK, : end - begin] = value[:, begin:end]


def pieces(length, size):
    return [(i, min(i + size, length)) for i in range(0, length, size)]


def token_part(chunks):
    return jnp.concatenate([c[: c.shape[0] // 2, :] for c in chunks], axis=0)


def cot_part(chunks):
    return jnp.concatenate([c[c.shape[0] // 2 :, :] for c in chunks], axis=0)


def partial_kernel(groups, chips, *refs):
    chunks, (gate_up, down, packed), outs = refs[:chips], refs[chips : chips + 3], refs[chips + 3 :]
    tokens, cots = token_part(chunks), cot_part(chunks)
    outs[groups][...] = jnp.concatenate([tokens, cots], axis=0)
    hid, depth = down.shape
    dh = 0.0
    for i, (begin, end) in enumerate(pieces(depth, 2 * hid)):
        top = depth + i * hid
        dh = dh + mm(cots[:, begin:end], packed[top : top + hid, : end - begin], NT)
    products = (
        (mm(tokens, gate_up[...], NN), 0),
        (mm(cots, down[...], NT), 2 * hid),
        (mm(tokens, packed[:depth, :], NN), 3 * hid),
        (dh, 5 * hid),
    )
    for product, at in products:
        cut = slice(at, at + product.shape[1])
        for k in range(groups):
            rows = [rows_of(product, (c * groups + k) * ROWS) for c in range(chips)]
            outs[k][:, cut] = jnp.concatenate(rows, axis=0).astype(outs[k].dtype)


def act_kernel(groups, *refs):
    parts, out = refs[:groups], refs[groups]
    hid = out.shape[1] // 6
    for half in range(2):
        values = []
        for i in range(3):
            cut = slice((3 * half + i) * hid, (3 * half + i + 1) * hid)
            total = parts[0][:, cut]
            for part in parts[1:]:
                total = total + part[:, cut].astype(F32)
            values.append(total)
        a, b, dh = values
        sig = jax.nn.sigmoid(a)
        swish = a * sig
        results = (dh * b * sig * (1.0 + a * (1.0 - sig)), dh * swish, swish * b)
        for i, result in enumerate(results):
            cut = slice((3 * half + i) * hid, (3 * half + i + 1) * hid)
            out[:, cut] = result.astype(BF16)


def dx_kernel(groups, chips, *refs):
    acts, (own, other), outs = refs[:groups], refs[groups : groups + 2], refs[groups + 2 :]
    depth, hid = own.shape[0], own.shape[1] // 2
    act = jnp.concatenate([a[...] for a in acts], axis=0)
    dx = mm(act[:, : 2 * hid], own[...], NT)
    dx = dx + mm(act[:, 3 * hid : 5 * hid], other[:depth, :], NT)
    for c in range(chips):
        rows = [rows_of(dx, (k * chips + c) * ROWS) for k in range(groups)]
        outs[c][...] = jnp.concatenate(rows, axis=0).astype(outs[c].dtype)
    outs[chips][...] = regroup(act[:, : 3 * hid], groups, chips)
    outs[chips + 1][...] = regroup(act[:, 3 * hid :], groups, chips)


def collect_kernel(groups, chips, *refs):
    parts, outs = refs[:chips], refs[chips:]
    sums = []
    for first in range(0, chips, CHIPS):
        total = parts[first][...].astype(F32)
        for part in parts[first + 1 : first + CHIPS]:
            total = total + part[...].astype(F32)
        sums.append(total)
    for k in range(groups):
        rows = [rows_of(total, k * ROWS) for total in sums]
        outs[k][...] = jnp.concatenate(rows, axis=0).astype(BF16)


def place_kernel(groups, experts, me, home, *refs):
    parts, (picks, out, slices, result, sems) = refs[:groups], refs[groups:]
    depth = parts[0].shape[1]
    copies = []
    for k in range(groups):
        slices[me[0] ^ k] = parts[k][...].astype(F32)
    for s in range(groups):
        total = jnp.zeros((out.shape[0], depth), F32)
        for x in range(experts):
            rows = slices[s, x * ROWS : (x + 1) * ROWS, :].astype(BF16)
            total = total + mm(picks[home[0] ^ x].astype(BF16), rows, TN)
        cut = slice(s * depth, (s + 1) * depth)
        result[:, cut] = total.astype(BF16)
        if depth % BLOCK == 0:
            copies.append(pltpu.make_async_copy(result.at[:, cut], out.at[:, cut], sems.at[s]))
            copies[-1].start()
    if not copies:
        copies.append(pltpu.make_async_copy(result, out, sems.at[0]))
        copies[-1].start()
    for copy in copies:
        copy.wait()


def regroup(act, groups, chips):
    wide = act.astype(F32)
    rows = [rows_of(wide, (k * chips + c) * ROWS) for c in range(chips) for k in range(groups)]
    return jnp.concatenate(rows, axis=0).astype(BF16)


def grads_kernel(own, other, act_own, act_other, grad_gate, grad_up, grad_down, token):
    hid, half = grad_gate.shape[1], own.shape[0] // 2
    acts = (act_own, act_other)
    tokens = jnp.concatenate([own[:half, :], other[:half, :]], axis=0)
    cots = jnp.concatenate([own[half:, :], other[half:, :]], axis=0)
    act = jnp.concatenate([a[...] for a in acts], axis=0)
    grad_gate[...] = mm(tokens, act[:, :hid], TN).astype(BF16)
    grad_up[...] = mm(tokens, act[:, hid : 2 * hid], TN).astype(BF16)
    grad_down[...] = mm(act[:, 2 * hid :], cots, TN).astype(BF16)
    token[...] = jnp.zeros_like(token)


def chunk_of(parts, experts, slot):
    blocks = [p.reshape(experts, 2, ROWS, p.shape[1]) for p in parts]
    if experts == 1:
        blocks = [b[0] for b in blocks]
    else:
        blocks = [lax.dynamic_index_in_dim(b, slot, 0, keepdims=False) for b in blocks]
    return jnp.concatenate([b[0] for b in blocks] + [b[1] for b in blocks], axis=0)


def on_device(
    tokens,
    cotangent,
    route_weight,
    expert_ids,
    live_tokens,
    replica_plan,
    w_gate,
    w_up,
    w_down,
    scale_gate,
    scale_up,
    scale_down,
):
    members, groups = lax.axis_size("expert"), lax.axis_size("dp")
    experts, chips = members // HSH, members // 2
    count, width = tokens.shape
    depth, hid = w_gate.shape
    group, member = lax.axis_index("dp"), lax.axis_index("expert")
    me = jnp.reshape(group, (1,))
    home = jnp.reshape(member // HSH, (1,))
    rows = groups * chips * ROWS

    *sent, picks = call(
        functools.partial(route_kernel, groups, experts),
        [shape((2 * ROWS * experts, depth))] * groups + [shape((experts, ROWS, count), F32)],
        (me,),
        (live_tokens.reshape(1, 1), replica_plan),
        hbm=(expert_ids.T, route_weight.T, tokens, cotangent),
        scratch=[
            pltpu.VMEM(expert_ids.shape[::-1], jnp.int32),
            pltpu.VMEM(route_weight.shape[::-1], F32),
            pltpu.VMEM(tokens.shape, BF16),
            pltpu.VMEM(cotangent.shape, BF16),
            pltpu.VMEM((groups, 2 * ROWS * experts, depth), BF16),
            pltpu.SemaphoreType.DMA((2 + 2 * groups,)),
        ],
        flops=4 * count * experts * ROWS * width,
        limit=ROUTE_VMEM_BYTES,
        name="route",
    )
    parts = [sent[0]] + [swap(sent[k], "dp", k) for k in range(1, groups)]
    chunks = [chunk_of(parts, experts, member // HSH)]
    for c in range(1, chips):
        out = chunks[0] if experts == 1 else chunk_of(parts, experts, (member ^ (2 * c)) // HSH)
        chunks.append(swap(out, "expert", 2 * c))

    tall = depth + hid * len(pieces(depth, 2 * hid))
    gate_up, down, packed = call(
        weights_kernel,
        [shape((depth, 2 * hid)), shape((hid, depth)), shape((tall, 2 * hid))],
        (me * depth, scale_gate.T, scale_up.T, scale_down),
        (w_gate, w_up, w_down),
        after=(parts[1],),
        flops=6 * depth * hid,
        name="weights",
    )
    other = swap(packed, "expert", 1)

    *partial, own_rows = call(
        functools.partial(partial_kernel, groups, chips),
        [shape((chips * ROWS, 6 * hid), F32 if k == 0 else BF16) for k in range(groups)]
        + [shape((2 * rows, depth))],
        (),
        (*chunks, gate_up, down, other),
        flops=12 * rows * depth * hid,
        name="partial",
    )
    other_rows = swap(own_rows, "expert", 1)
    summands = [partial[0]] + [swap(partial[k], "dp", k) for k in range(1, groups)]
    (act,) = call(
        functools.partial(act_kernel, groups),
        [shape((chips * ROWS, 6 * hid))],
        (),
        summands,
        flops=40 * chips * ROWS * hid,
        name="activations",
    )
    acts = [act] + [swap(act, "dp", k) for k in range(1, groups)]
    *dx, act_own, act_out = call(
        functools.partial(dx_kernel, groups, chips),
        [shape((groups * ROWS, depth), F32 if c == 0 else BF16) for c in range(chips)]
        + [shape((rows, 3 * hid))] * 2,
        (),
        (*acts, gate_up, other),
        flops=8 * rows * depth * hid,
        name="dx",
    )
    returned = [dx[0]] + [swap(dx[c], "expert", 2 * c) for c in range(1, chips)]
    home_rows = call(
        functools.partial(collect_kernel, groups, chips),
        [shape((experts * ROWS, depth))] * groups,
        (),
        returned,
        flops=rows * depth,
        name="collect",
    )
    placed = [home_rows[0]] + [swap(home_rows[k], "dp", k) for k in range(1, groups)]
    act_other = swap(act_out, "expert", 1)
    *grads, done = call(
        grads_kernel,
        [shape((depth, hid)), shape((depth, hid)), shape((hid, depth)), shape((8, BLOCK), F32)],
        (),
        (own_rows, other_rows, act_own, act_other),
        flops=12 * rows * depth * hid,
        name="gradients",
    )
    (d_tokens,) = call(
        functools.partial(place_kernel, groups, experts),
        [shape((count, width))],
        (me, home),
        (*placed, picks),
        after=(done,),
        far_out=True,
        scratch=[
            pltpu.VMEM((groups, experts * ROWS, depth), F32),
            pltpu.VMEM((count, width), BF16),
            pltpu.SemaphoreType.DMA((groups,)),
        ],
        flops=2 * count * experts * ROWS * width,
        name="place",
    )
    return (d_tokens, *grads)


def solution(mesh):
    return jax.shard_map(
        on_device,
        mesh=mesh,
        in_specs=(
            P(("dp", "expert"), None),
            P(("dp", "expert"), None),
            P(("dp", "expert"), None),
            P(("dp", "expert"), None),
            P(("dp", "expert")),
            P(("dp", "expert"), None),
            P("dp", "expert"),
            P("dp", "expert"),
            P("expert", "dp"),
            P(None, "expert"),
            P(None, "expert"),
            P("expert", None),
        ),
        out_specs=(
            P(("dp", "expert"), None),
            P("dp", "expert"),
            P("dp", "expert"),
            P("expert", "dp"),
        ),
        check_vma=False,
    )
```

time: 85.9 us -> 60.8 us (0.71)
  waiting for transfers between devices: 45.6 us -> 25.4 us
  local copies, waits for them, and re-layouts: 4.1 us -> 0.81 us
  starting transfers between devices: 26.8 us -> 24.3 us
    ppermute x25 -> x21, waiting for transfers between devices: 45.6 us -> 25.4 us  [swap(): lax.ppermute(x, axis, [(i, i ^ k) for i in range(lax.axis_size(axis))])]
    unnamed x29 -> x23, local copies, waits for them, and re-layouts: 4.09 us -> 0.8 us
    ppermute x25 -> x21, starting transfers between devices: 26.8 us -> 24.3 us  [swap(): lax.ppermute(x, axis, [(i, i ^ k) for i in range(lax.axis_size(axis))])]
    pallas_call x9 -> x8, Pallas kernels: 7.01 us -> 7.82 us  [call(): pl.pallas_call(body, out_shape=outs, in_specs=[pl.BlockSpec(memory_space=...]
  transfers between devices with their start and end apart: 25 -> 21, of which waited for: 16 -> 14; matrix products, arithmetic and copies ran while one was open for 0% -> 1% of each run, Pallas kernels for 4% -> 5%
where the time goes in v3:
time: 60.8 us; the launch traced here: 60.6 us
  waiting for transfers between devices  25.4 us (42%)
  starting transfers between devices  24.3 us (40%)
  Pallas kernels  7.82 us (13%)
  between operations  2.23 us (4%)
  local copies, waits for them, and re-layouts  0.81 us (1%)
    ppermute x21, waiting for transfers between devices, swap(): lax.ppermute(x, axis, [(i, i ^ k) for i in range(lax.axis_size(axis))])  25.4 us
    ppermute x21, starting transfers between devices, swap(): lax.ppermute(x, axis, [(i, i ^ k) for i in range(lax.axis_size(axis))])  24.3 us
    pallas_call x8, Pallas kernels, call(): pl.pallas_call(body, out_shape=outs, in_specs=[pl.BlockSpec(memory_space=...  7.82 us
  transfers between devices with their start and end apart: 21, of which 14 were waited for; matrix products, arithmetic and copies ran while one was open for 1% of the time, Pallas kernels for 5%

profile of v3, /device:TPU:0, one launch (start us, length us, event | category | flops | bytes accessed | tf_op | source)
XLA Modules:
  0.0 60.6 jit_solution(8632870748250434595)
XLA Ops:
  2.1 2.6 %route.1 = (bf16[16,896]{1,0:T(8,128)(2,1)}, bf16[16,896]{1,0:T(8,128)(2,1)}, bf16[16,896]{1,0:T(8,128)(2,1)}, bf16[16,896]{1,0:T(8,128)(2,1)}, f32[1,8,128]{2,1,0:T(8,128)}) custom-call(s32[1]{0:T(128)} %bitcast.refs_0_, s32[8,128]{1,0:T(8,128)} %bitcast.10, f32[8,128]{1,0:T(8,128)} %bitcast.11, bf16[128,3584]{1,0:T(8,128)(2,1)} %refs_3_.2, ...), custom_call_target="tpu_custom_call" | custom-call | flops 14680064 | bytes 1961992 | tf_op jit(solution)/shard_map/route/pallas_call | solution.py:37
  4.7 0.0 copy-start.7
  4.7 3.0 %collective-permute-start = (bf16[16,896]{1,0:T(8,128)(2,1)}, bf16[16,896]{1,0:T(8,128)(2,1)S(1)}, u32[]{:S(2)}, u32[]{:S(2)}) collective-permute-start(bf16[16,896]{1,0:T(8,128)(2,1)} %get-tuple-element.32), channel_id=1, source_target_pairs={{0,8},{8,0},{16,24},{24,16},{1,9},{9,1},{17,25},{25,17},{2,10},{10... | collective-permute-start | bytes 86024 | tf_op jit(solution)/shard_map/ppermute | solution.py:64
  7.7 1.5 %collective-permute-start.1 = (bf16[16,896]{1,0:T(8,128)(2,1)}, bf16[16,896]{1,0:T(8,128)(2,1)S(1)}, u32[]{:S(2)}, u32[]{:S(2)}) collective-permute-start(bf16[16,896]{1,0:T(8,128)(2,1)} %get-tuple-element.33), channel_id=1, source_target_pairs={{0,16},{8,24},{16,0},{24,8},{1,17},{9,25},{17,1},{25,9},{2,18},{10... | collective-permute-start | bytes 86024 | tf_op jit(solution)/shard_map/ppermute | solution.py:64
  9.2 0.0 collective-permute-start.2
  9.3 0.7 %constant_dynamic-update-slice_fusion.7 = bf16[64,896]{1,0:T(8,128)(2,1)S(1)} fusion(bf16[16,896]{1,0:T(8,128)(2,1)} %get-tuple-element.31), kind=kLoop, calls=%fused_computation.7 | loop fusion | bytes 28672
  10.0 0.0 collective-permute-done.refs_4_
  10.0 1.0 %weights.1 = (bf16[896,512]{1,0:T(8,128)(2,1)S(1)}, bf16[256,896]{1,0:T(8,128)(2,1)S(1)}, bf16[1408,512]{1,0:T(8,128)(2,1)S(1)}) custom-call(s32[1]{0:T(128)S(6)} %mul.3.refs_0_, f32[2,28]{1,0:T(2,128)S(1)} %bitcast.8, f32[2,28]{1,0:T(2,128)S(1)} %bitcast.9, f32[2,28]{1,0:T(2,128)S(1)} %copy-done.6, bf16[16,896]{1,0:T(8,128)(2,1)S(1)} %collective-permute-done.refs_4_, ...), custom_call_target="tpu_custom_call" | custom-call | flops 1376256 | bytes 4194304 | tf_op jit(solution)/shard_map/weights/pallas_call | solution.py:37
  11.1 0.1 collective-permute-start.6
  11.2 0.6 %collective-permute-done.1 = bf16[16,896]{1,0:T(8,128)(2,1)S(1)} collective-permute-done((bf16[16,896]{1,0:T(8,128)(2,1)}, bf16[16,896]{1,0:T(8,128)(2,1)S(1)}, u32[]{:S(2)}, u32[]{:S(2)}) %collective-permute-start.1) | collective-permute-done | bytes 28704 | tf_op jit(solution)/shard_map/ppermute | solution.py:64
  11.8 2.4 %collective-permute-done.2 = bf16[16,896]{1,0:T(8,128)(2,1)S(1)} collective-permute-done((bf16[16,896]{1,0:T(8,128)(2,1)}, bf16[16,896]{1,0:T(8,128)(2,1)S(1)}, u32[]{:S(2)}, u32[]{:S(2)}) %collective-permute-start.2) | collective-permute-done | bytes 28704 | tf_op jit(solution)/shard_map/ppermute | solution.py:64
  14.3 3.7 %collective-permute-start.5 = (bf16[64,896]{1,0:T(8,128)(2,1)S(1)}, bf16[64,896]{1,0:T(8,128)(2,1)S(1)}, u32[]{:S(2)}, u32[]{:S(2)}) collective-permute-start(bf16[64,896]{1,0:T(8,128)(2,1)S(1)} %constant_dynamic-update-slice_fusion.refs_0_), channel_id=1, source_target_pairs={{0,6},{1,7},{2,4},{3,5},{4,2},{5,3},{6,0},{7,1},{8,14},{9,15},{10,... | collective-permute-start | bytes 344072 | tf_op jit(solution)/shard_map/ppermute | solution.py:64
  17.9 0.8 %collective-permute-start.3 = (bf16[64,896]{1,0:T(8,128)(2,1)S(1)}, bf16[64,896]{1,0:T(8,128)(2,1)S(1)}, u32[]{:S(2)}, u32[]{:S(2)}) collective-permute-start(bf16[64,896]{1,0:T(8,128)(2,1)S(1)} %constant_dynamic-update-slice_fusion.refs_0_), channel_id=1, source_target_pairs={{0,2},{1,3},{2,0},{3,1},{4,6},{5,7},{6,4},{7,5},{8,10},{9,11},{10,... | collective-permute-start | bytes 344072 | tf_op jit(solution)/shard_map/ppermute | solution.py:64
  18.7 2.7 %collective-permute-done.5.refs_3_ = bf16[64,896]{1,0:T(8,128)(2,1)S(1)} collective-permute-done((bf16[64,896]{1,0:T(8,128)(2,1)S(1)}, bf16[64,896]{1,0:T(8,128)(2,1)S(1)}, u32[]{:S(2)}, u32[]{:S(2)}) %collective-permute-start.5) | collective-permute-done | bytes 114720 | tf_op jit(solution)/shard_map/ppermute | solution.py:64
  21.4 4.5 %collective-permute-done.4.refs_2_ = bf16[64,896]{1,0:T(8,128)(2,1)S(1)} collective-permute-done((bf16[64,896]{1,0:T(8,128)(2,1)S(1)}, bf16[64,896]{1,0:T(8,128)(2,1)S(1)}, u32[]{:S(2)}, u32[]{:S(2)}) %collective-permute-start.4) | collective-permute-done | bytes 114720 | tf_op jit(solution)/shard_map/ppermute | solution.py:64
  25.9 0.0 collective-permute-done.3.refs_1_
  25.9 0.0 collective-permute-done.6.refs_6_.refs_5_
  25.9 0.7 %partial.1 = (f32[32,1536]{1,0:T(8,128)S(1)}, bf16[32,1536]{1,0:T(8,128)(2,1)S(1)}, bf16[32,1536]{1,0:T(8,128)(2,1)S(1)}, bf16[32,1536]{1,0:T(8,128)(2,1)S(1)}, bf16[256,896]{1,0:T(8,128)(2,1)S(1)}) custom-call(bf16[64,896]{1,0:T(8,128)(2,1)S(1)} %constant_dynamic-update-slice_fusion.refs_0_, bf16[64,896]{1,0:T(8,128)(2,1)S(1)} %collective-permute-done.3.refs_1_, ...), custom_call_target="tpu_custom_call" | custom-call | flops 352321536 | bytes 4227072 | tf_op jit(solution)/shard_map/partial/pallas_call | solution.py:37
  26.6 0.1 collective-permute-start.7
  26.7 1.4 %collective-permute-start.8 = (bf16[32,1536]{1,0:T(8,128)(2,1)S(1)}, bf16[32,1536]{1,0:T(8,128)(2,1)S(1)}, u32[]{:S(2)}, u32[]{:S(2)}) collective-permute-start(bf16[32,1536]{1,0:T(8,128)(2,1)S(1)} %get-tuple-element.40), channel_id=1, source_target_pairs={{0,8},{8,0},{16,24},{24,16},{1,9},{9,1},{17,25},{25,17},{2,10},{10... | collective-permute-start | bytes 294920 | tf_op jit(solution)/shard_map/ppermute | solution.py:64
  28.0 1.5 %collective-permute-start.9 = (bf16[32,1536]{1,0:T(8,128)(2,1)S(1)}, bf16[32,1536]{1,0:T(8,128)(2,1)S(1)}, u32[]{:S(2)}, u32[]{:S(2)}) collective-permute-start(bf16[32,1536]{1,0:T(8,128)(2,1)S(1)} %get-tuple-element.41), channel_id=1, source_target_pairs={{0,16},{8,24},{16,0},{24,8},{1,17},{9,25},{17,1},{25,9},{2,18},{10... | collective-permute-start | bytes 294920 | tf_op jit(solution)/shard_map/ppermute | solution.py:64
  29.6 0.7 %collective-permute-start.10 = (bf16[32,1536]{1,0:T(8,128)(2,1)S(1)}, bf16[32,1536]{1,0:T(8,128)(2,1)S(1)}, u32[]{:S(2)}, u32[]{:S(2)}) collective-permute-start(bf16[32,1536]{1,0:T(8,128)(2,1)S(1)} %get-tuple-element.42), channel_id=1, source_target_pairs={{0,24},{8,16},{16,8},{24,0},{1,25},{9,17},{17,9},{25,1},{2,26},{10... | collective-permute-start | bytes 294920 | tf_op jit(solution)/shard_map/ppermute | solution.py:64
  30.2 1.7 %collective-permute-done.8.refs_1_ = bf16[32,1536]{1,0:T(8,128)(2,1)S(1)} collective-permute-done((bf16[32,1536]{1,0:T(8,128)(2,1)S(1)}, bf16[32,1536]{1,0:T(8,128)(2,1)S(1)}, u32[]{:S(2)}, u32[]{:S(2)}) %collective-permute-start.8) | collective-permute-done | bytes 98336 | tf_op jit(solution)/shard_map/ppermute | solution.py:64
  31.9 2.2 %collective-permute-done.9.refs_2_ = bf16[32,1536]{1,0:T(8,128)(2,1)S(1)} collective-permute-done((bf16[32,1536]{1,0:T(8,128)(2,1)S(1)}, bf16[32,1536]{1,0:T(8,128)(2,1)S(1)}, u32[]{:S(2)}, u32[]{:S(2)}) %collective-permute-start.9) | collective-permute-done | bytes 98336 | tf_op jit(solution)/shard_map/ppermute | solution.py:64
  34.0 1.0 %collective-permute-done.10.refs_3_ = bf16[32,1536]{1,0:T(8,128)(2,1)S(1)} collective-permute-done((bf16[32,1536]{1,0:T(8,128)(2,1)S(1)}, bf16[32,1536]{1,0:T(8,128)(2,1)S(1)}, u32[]{:S(2)}, u32[]{:S(2)}) %collective-permute-start.10) | collective-permute-done | bytes 98336 | tf_op jit(solution)/shard_map/ppermute | solution.py:64
  35.1 0.1 activations.1.refs_0_
  35.1 1.5 %collective-permute-start.13 = (bf16[32,1536]{1,0:T(8,128)(2,1)S(1)}, bf16[32,1536]{1,0:T(8,128)(2,1)S(1)}, u32[]{:S(2)}, u32[]{:S(2)}) collective-permute-start(bf16[32,1536]{1,0:T(8,128)(2,1)S(1)} %activations.1.refs_0_), channel_id=1, source_target_pairs={{0,24},{8,16},{16,8},{24,0},{1,25},{9,17},{17,9},{25,1},{2,26},{10... | collective-permute-start | bytes 294920 | tf_op jit(solution)/shard_map/ppermute | solution.py:64
  36.7 1.2 %collective-permute-start.12 = (bf16[32,1536]{1,0:T(8,128)(2,1)S(1)}, bf16[32,1536]{1,0:T(8,128)(2,1)S(1)}, u32[]{:S(2)}, u32[]{:S(2)}) collective-permute-start(bf16[32,1536]{1,0:T(8,128)(2,1)S(1)} %activations.1.refs_0_), channel_id=1, source_target_pairs={{0,16},{8,24},{16,0},{24,8},{1,17},{9,25},{17,1},{25,9},{2,18},{10... | collective-permute-start | bytes 294920 | tf_op jit(solution)/shard_map/ppermute | solution.py:64
  37.8 0.9 %collective-permute-start.11 = (bf16[32,1536]{1,0:T(8,128)(2,1)S(1)}, bf16[32,1536]{1,0:T(8,128)(2,1)S(1)}, u32[]{:S(2)}, u32[]{:S(2)}) collective-permute-start(bf16[32,1536]{1,0:T(8,128)(2,1)S(1)} %activations.1.refs_0_), channel_id=1, source_target_pairs={{0,8},{8,0},{16,24},{24,16},{1,9},{9,1},{17,25},{25,17},{2,10},{10... | collective-permute-start | bytes 294920 | tf_op jit(solution)/shard_map/ppermute | solution.py:64
  38.7 2.8 %collective-permute-done.13.refs_3_ = bf16[32,1536]{1,0:T(8,128)(2,1)S(1)} collective-permute-done((bf16[32,1536]{1,0:T(8,128)(2,1)S(1)}, bf16[32,1536]{1,0:T(8,128)(2,1)S(1)}, u32[]{:S(2)}, u32[]{:S(2)}) %collective-permute-start.13) | collective-permute-done | bytes 98336 | tf_op jit(solution)/shard_map/ppermute | solution.py:64
  41.5 0.5 collective-permute-done.12.refs_2_
  42.0 0.7 %collective-permute-done.11.refs_1_ = bf16[32,1536]{1,0:T(8,128)(2,1)S(1)} collective-permute-done((bf16[32,1536]{1,0:T(8,128)(2,1)S(1)}, bf16[32,1536]{1,0:T(8,128)(2,1)S(1)}, u32[]{:S(2)}, u32[]{:S(2)}) %collective-permute-start.11) | collective-permute-done | bytes 98336 | tf_op jit(solution)/shard_map/ppermute | solution.py:64
  42.7 0.7 %dx.1 = (f32[32,896]{1,0:T(8,128)S(1)}, bf16[32,896]{1,0:T(8,128)(2,1)S(1)}, bf16[32,896]{1,0:T(8,128)(2,1)S(1)}, bf16[32,896]{1,0:T(8,128)(2,1)S(1)}, bf16[128,...) custom-call(bf16[32,1536]{1,0:T(8,128)(2,1)S(1)} %activations.1.refs_0_, ...), custom_call_target="tpu_custom_call" | custom-call | flops 234881024 | bytes 3432448 | tf_op jit(solution)/shard_map/dx/pallas_call | solution.py:37
  43.4 0.1 collective-permute-start.14
  43.5 0.2 collective-permute-start.15
  43.7 2.9 %collective-permute-start.16 = (bf16[32,896]{1,0:T(8,128)(2,1)S(1)}, bf16[32,896]{1,0:T(8,128)(2,1)S(1)}, u32[]{:S(2)}, u32[]{:S(2)}) collective-permute-start(bf16[32,896]{1,0:T(8,128)(2,1)S(1)} %get-tuple-element.48), channel_id=1, source_target_pairs={{0,4},{1,5},{2,6},{3,7},{4,0},{5,1},{6,2},{7,3},{8,12},{9,13},{10,... | collective-permute-start | bytes 172040 | tf_op jit(solution)/shard_map/ppermute | solution.py:64
  46.6 1.3 %collective-permute-start.17 = (bf16[32,896]{1,0:T(8,128)(2,1)S(1)}, bf16[32,896]{1,0:T(8,128)(2,1)S(1)}, u32[]{:S(2)}, u32[]{:S(2)}) collective-permute-start(bf16[32,896]{1,0:T(8,128)(2,1)S(1)} %get-tuple-element.49), channel_id=1, source_target_pairs={{0,6},{1,7},{2,4},{3,5},{4,2},{5,3},{6,0},{7,1},{8,14},{9,15},{10,... | collective-permute-start | bytes 172040 | tf_op jit(solution)/shard_map/ppermute | solution.py:64
  47.9 1.0 %collective-permute-done.15.refs_1_ = bf16[32,896]{1,0:T(8,128)(2,1)S(1)} collective-permute-done((bf16[32,896]{1,0:T(8,128)(2,1)S(1)}, bf16[32,896]{1,0:T(8,128)(2,1)S(1)}, u32[]{:S(2)}, u32[]{:S(2)}) %collective-permute-start.15) | collective-permute-done | bytes 57376 | tf_op jit(solution)/shard_map/ppermute | solution.py:64
  48.9 1.4 %collective-permute-done.16.refs_2_ = bf16[32,896]{1,0:T(8,128)(2,1)S(1)} collective-permute-done((bf16[32,896]{1,0:T(8,128)(2,1)S(1)}, bf16[32,896]{1,0:T(8,128)(2,1)S(1)}, u32[]{:S(2)}, u32[]{:S(2)}) %collective-permute-start.16) | collective-permute-done | bytes 57376 | tf_op jit(solution)/shard_map/ppermute | solution.py:64
  50.3 2.3 %collective-permute-done.17.refs_3_ = bf16[32,896]{1,0:T(8,128)(2,1)S(1)} collective-permute-done((bf16[32,896]{1,0:T(8,128)(2,1)S(1)}, bf16[32,896]{1,0:T(8,128)(2,1)S(1)}, u32[]{:S(2)}, u32[]{:S(2)}) %collective-permute-start.17) | collective-permute-done | bytes 57376 | tf_op jit(solution)/shard_map/ppermute | solution.py:64
  52.6 1.1 %collective-permute-start.18 = (bf16[8,896]{1,0:T(8,128)(2,1)S(1)}, bf16[8,896]{1,0:T(8,128)(2,1)S(1)}, u32[]{:S(2)}, u32[]{:S(2)}) collective-permute-start(bf16[8,896]{1,0:T(8,128)(2,1)S(1)} %get-tuple-element.51), channel_id=1, source_target_pairs={{0,8},{8,0},{16,24},{24,16},{1,9},{9,1},{17,25},{25,17},{2,10},{10... | collective-permute-start | bytes 43016 | tf_op jit(solution)/shard_map/ppermute | solution.py:64
  53.7 1.0 %collective-permute-start.19 = (bf16[8,896]{1,0:T(8,128)(2,1)S(1)}, bf16[8,896]{1,0:T(8,128)(2,1)S(1)}, u32[]{:S(2)}, u32[]{:S(2)}) collective-permute-start(bf16[8,896]{1,0:T(8,128)(2,1)S(1)} %get-tuple-element.52), channel_id=1, source_target_pairs={{0,16},{8,24},{16,0},{24,8},{1,17},{9,25},{17,1},{25,9},{2,18},{10... | collective-permute-start | bytes 43016 | tf_op jit(solution)/shard_map/ppermute | solution.py:64
  54.7 1.4 %collective-permute-start.20 = (bf16[8,896]{1,0:T(8,128)(2,1)S(1)}, bf16[8,896]{1,0:T(8,128)(2,1)S(1)}, u32[]{:S(2)}, u32[]{:S(2)}) collective-permute-start(bf16[8,896]{1,0:T(8,128)(2,1)S(1)} %get-tuple-element.53), channel_id=1, source_target_pairs={{0,24},{8,16},{16,8},{24,0},{1,25},{9,17},{17,9},{25,1},{2,26},{10... | collective-permute-start | bytes 43016 | tf_op jit(solution)/shard_map/ppermute | solution.py:64
  56.2 0.0 collective-permute-done.14.refs_3_
  56.2 0.0 collective-permute-done.7.refs_1_
  56.2 1.5 %gradients.1 = (bf16[896,256]{1,0:T(8,128)(2,1)}, bf16[896,256]{1,0:T(8,128)(2,1)}, bf16[256,896]{1,0:T(8,128)(2,1)}, f32[8,128]{1,0:T(8,128)S(1)}) custom-call(bf16[256,896]{1,0:T(8,128)(2,1)S(1)} %get-tuple-element.38.refs_0_, bf16[256,896]{1,0:T(8,128)(2,1)S(1)} %collective-permute-done.7.refs_1_, bf16[128,768]{1,0:T(8,128)(2,1)S(1)} %get-tuple-element.43.refs_2_, ...), custom_call_target="tpu_custom_call" | custom-call | flops 352321536 | bytes 2691072 | tf_op jit(solution)/shard_map/gradients/pallas_call | solution.py:37
  57.7 1.7 %collective-permute-done.20.refs_6_ = bf16[8,896]{1,0:T(8,128)(2,1)S(1)} collective-permute-done((bf16[8,896]{1,0:T(8,128)(2,1)S(1)}, bf16[8,896]{1,0:T(8,128)(2,1)S(1)}, u32[]{:S(2)}, u32[]{:S(2)}) %collective-permute-start.20) | collective-permute-done | bytes 14368 | tf_op jit(solution)/shard_map/ppermute | solution.py:64
  59.4 1.2 %place.1 = bf16[128,3584]{1,0:T(8,128)(2,1)} custom-call(s32[1]{0:T(128)} %bitcast.refs_0_, s32[1]{0:T(128)} %bitcast.1.refs_1_, f32[8,128]{1,0:T(8,128)S(1)} %get-tuple-element.45.refs_2_, bf16[8,896]{1,0:T(8,128)(2,1)S(1)} %get-tuple-element.50.refs_3_, bf16[8,896]{1,0:T(8,128)(2,1)S(1)} %collective-permute-done.18.refs_4_, ...), custom_call_target="tpu_custom_call" | custom-call | flops 7340032 | bytes 978944 | tf_op jit(solution)/shard_map/place/pallas_call | solution.py:37
  (26 shorter events, 0.1 us)
Async XLA Ops:
  0.6 9.3 %copy-start.6 = (f32[2,28]{1,0:T(2,128)S(1)}, f32[2,28]{1,0:T(2,128)}, u32[]{:S(2)}) copy-start(f32[2,28]{1,0:T(2,128)} %refs_3_.3) | copy-start | bytes 676
  0.6 9.3 %copy-start.5 = (f32[28,2]{0,1:T(2,128)S(1)}, f32[28,2]{0,1:T(2,128)}, u32[]{:S(2)}) copy-start(f32[28,2]{0,1:T(2,128)} %param.22) | copy-start | bytes 676
  0.7 9.3 %copy-start.4 = (f32[28,2]{0,1:T(2,128)S(1)}, f32[28,2]{0,1:T(2,128)}, u32[]{:S(2)}) copy-start(f32[28,2]{0,1:T(2,128)} %param.21) | copy-start | bytes 676
  0.7 9.3 %copy-start.2 = (bf16[256,896]{1,0:T(8,128)(2,1)S(1)}, bf16[256,896]{1,0:T(8,128)(2,1)}, u32[]{:S(2)}) copy-start(bf16[256,896]{1,0:T(8,128)(2,1)} %refs_7_.1) | copy-start | bytes 1376260
  0.7 9.3 %copy-start.1 = (bf16[896,256]{1,0:T(8,128)(2,1)S(1)}, bf16[896,256]{1,0:T(8,128)(2,1)}, u32[]{:S(2)}) copy-start(bf16[896,256]{1,0:T(8,128)(2,1)} %refs_6_.2) | copy-start | bytes 1376260
  0.7 9.3 %copy-start = (bf16[896,256]{1,0:T(8,128)(2,1)S(1)}, bf16[896,256]{1,0:T(8,128)(2,1)}, u32[]{:S(2)}) copy-start(bf16[896,256]{1,0:T(8,128)(2,1)} %refs_5_.1) | copy-start | bytes 1376260
  4.7 9.5 %copy-start.7 = (bf16[16,896]{1,0:T(8,128)(2,1)S(1)}, bf16[16,896]{1,0:T(8,128)(2,1)}, u32[]{:S(2)}) copy-start(bf16[16,896]{1,0:T(8,128)(2,1)} %get-tuple-element.31) | copy-start | bytes 86020
  4.7 5.3 %collective-permute-start = (bf16[16,896]{1,0:T(8,128)(2,1)}, bf16[16,896]{1,0:T(8,128)(2,1)S(1)}, u32[]{:S(2)}, u32[]{:S(2)}) collective-permute-start(bf16[16,896]{1,0:T(8,128)(2,1)} %get-tuple-element.32), channel_id=1, source_target_pairs={{0,8},{8,0},{16,24},{24,16},{1,9},{9,1},{17,25},{25,17},{2,10},{10... | collective-permute-start | bytes 86024 | tf_op jit(solution)/shard_map/ppermute | solution.py:64
  7.7 4.1 %collective-permute-start.1 = (bf16[16,896]{1,0:T(8,128)(2,1)}, bf16[16,896]{1,0:T(8,128)(2,1)S(1)}, u32[]{:S(2)}, u32[]{:S(2)}) collective-permute-start(bf16[16,896]{1,0:T(8,128)(2,1)} %get-tuple-element.33), channel_id=1, source_target_pairs={{0,16},{8,24},{16,0},{24,8},{1,17},{9,25},{17,1},{25,9},{2,18},{10... | collective-permute-start | bytes 86024 | tf_op jit(solution)/shard_map/ppermute | solution.py:64
  9.2 5.0 %collective-permute-start.2 = (bf16[16,896]{1,0:T(8,128)(2,1)}, bf16[16,896]{1,0:T(8,128)(2,1)S(1)}, u32[]{:S(2)}, u32[]{:S(2)}) collective-permute-start(bf16[16,896]{1,0:T(8,128)(2,1)} %get-tuple-element.34), channel_id=1, source_target_pairs={{0,24},{8,16},{16,8},{24,0},{1,25},{9,17},{17,9},{25,1},{2,26},{10... | collective-permute-start | bytes 86024 | tf_op jit(solution)/shard_map/ppermute | solution.py:64
  11.1 14.8 %collective-permute-start.6 = (bf16[1408,512]{1,0:T(8,128)(2,1)S(1)}, bf16[1408,512]{1,0:T(8,128)(2,1)S(1)}, u32[]{:S(2)}, u32[]{:S(2)}) collective-permute-start(bf16[1408,512]{1,0:T(8,128)(2,1)S(1)} %get-tuple-element.37), channel_id=1, source_target_pairs={{0,1},{1,0},{2,3},{3,2},{4,5},{5,4},{6,7},{7,6},{8,9},{9,8},{10,11... | collective-permute-start | bytes 4325384 | tf_op jit(solution)/shard_map/ppermute | solution.py:64
  14.3 7.2 %collective-permute-start.5 = (bf16[64,896]{1,0:T(8,128)(2,1)S(1)}, bf16[64,896]{1,0:T(8,128)(2,1)S(1)}, u32[]{:S(2)}, u32[]{:S(2)}) collective-permute-start(bf16[64,896]{1,0:T(8,128)(2,1)S(1)} %constant_dynamic-update-slice_fusion.refs_0_), channel_id=1, source_target_pairs={{0,6},{1,7},{2,4},{3,5},{4,2},{5,3},{6,0},{7,1},{8,14},{9,15},{10,... | collective-permute-start | bytes 344072 | tf_op jit(solution)/shard_map/ppermute | solution.py:64
  17.9 8.0 %collective-permute-start.4 = (bf16[64,896]{1,0:T(8,128)(2,1)S(1)}, bf16[64,896]{1,0:T(8,128)(2,1)S(1)}, u32[]{:S(2)}, u32[]{:S(2)}) collective-permute-start(bf16[64,896]{1,0:T(8,128)(2,1)S(1)} %constant_dynamic-update-slice_fusion.refs_0_), channel_id=1, source_target_pairs={{0,4},{1,5},{2,6},{3,7},{4,0},{5,1},{6,2},{7,3},{8,12},{9,13},{10,... | collective-permute-start | bytes 344072 | tf_op jit(solution)/shard_map/ppermute | solution.py:64
  17.9 8.0 %collective-permute-start.3 = (bf16[64,896]{1,0:T(8,128)(2,1)S(1)}, bf16[64,896]{1,0:T(8,128)(2,1)S(1)}, u32[]{:S(2)}, u32[]{:S(2)}) collective-permute-start(bf16[64,896]{1,0:T(8,128)(2,1)S(1)} %constant_dynamic-update-slice_fusion.refs_0_), channel_id=1, source_target_pairs={{0,2},{1,3},{2,0},{3,1},{4,6},{5,7},{6,4},{7,5},{8,10},{9,11},{10,... | collective-permute-start | bytes 344072 | tf_op jit(solution)/shard_map/ppermute | solution.py:64
  26.6 29.6 %collective-permute-start.7 = (bf16[256,896]{1,0:T(8,128)(2,1)S(1)}, bf16[256,896]{1,0:T(8,128)(2,1)S(1)}, u32[]{:S(2)}, u32[]{:S(2)}) collective-permute-start(bf16[256,896]{1,0:T(8,128)(2,1)S(1)} %get-tuple-element.38.refs_0_), channel_id=1, source_target_pairs={{0,1},{1,0},{2,3},{3,2},{4,5},{5,4},{6,7},{7,6},{8,9},{9,8},{10,11... | collective-permute-start | bytes 1376264 | tf_op jit(solution)/shard_map/ppermute | solution.py:64
  26.7 5.2 %collective-permute-start.8 = (bf16[32,1536]{1,0:T(8,128)(2,1)S(1)}, bf16[32,1536]{1,0:T(8,128)(2,1)S(1)}, u32[]{:S(2)}, u32[]{:S(2)}) collective-permute-start(bf16[32,1536]{1,0:T(8,128)(2,1)S(1)} %get-tuple-element.40), channel_id=1, source_target_pairs={{0,8},{8,0},{16,24},{24,16},{1,9},{9,1},{17,25},{25,17},{2,10},{10... | collective-permute-start | bytes 294920 | tf_op jit(solution)/shard_map/ppermute | solution.py:64
  28.0 6.0 %collective-permute-start.9 = (bf16[32,1536]{1,0:T(8,128)(2,1)S(1)}, bf16[32,1536]{1,0:T(8,128)(2,1)S(1)}, u32[]{:S(2)}, u32[]{:S(2)}) collective-permute-start(bf16[32,1536]{1,0:T(8,128)(2,1)S(1)} %get-tuple-element.41), channel_id=1, source_target_pairs={{0,16},{8,24},{16,0},{24,8},{1,17},{9,25},{17,1},{25,9},{2,18},{10... | collective-permute-start | bytes 294920 | tf_op jit(solution)/shard_map/ppermute | solution.py:64
  29.6 5.5 %collective-permute-start.10 = (bf16[32,1536]{1,0:T(8,128)(2,1)S(1)}, bf16[32,1536]{1,0:T(8,128)(2,1)S(1)}, u32[]{:S(2)}, u32[]{:S(2)}) collective-permute-start(bf16[32,1536]{1,0:T(8,128)(2,1)S(1)} %get-tuple-element.42), channel_id=1, source_target_pairs={{0,24},{8,16},{16,8},{24,0},{1,25},{9,17},{17,9},{25,1},{2,26},{10... | collective-permute-start | bytes 294920 | tf_op jit(solution)/shard_map/ppermute | solution.py:64
  35.1 6.3 %collective-permute-start.13 = (bf16[32,1536]{1,0:T(8,128)(2,1)S(1)}, bf16[32,1536]{1,0:T(8,128)(2,1)S(1)}, u32[]{:S(2)}, u32[]{:S(2)}) collective-permute-start(bf16[32,1536]{1,0:T(8,128)(2,1)S(1)} %activations.1.refs_0_), channel_id=1, source_target_pairs={{0,24},{8,16},{16,8},{24,0},{1,25},{9,17},{17,9},{25,1},{2,26},{10... | collective-permute-start | bytes 294920 | tf_op jit(solution)/shard_map/ppermute | solution.py:64
  36.7 5.4 %collective-permute-start.12 = (bf16[32,1536]{1,0:T(8,128)(2,1)S(1)}, bf16[32,1536]{1,0:T(8,128)(2,1)S(1)}, u32[]{:S(2)}, u32[]{:S(2)}) collective-permute-start(bf16[32,1536]{1,0:T(8,128)(2,1)S(1)} %activations.1.refs_0_), channel_id=1, source_target_pairs={{0,16},{8,24},{16,0},{24,8},{1,17},{9,25},{17,1},{25,9},{2,18},{10... | collective-permute-start | bytes 294920 | tf_op jit(solution)/shard_map/ppermute | solution.py:64
  37.8 4.9 %collective-permute-start.11 = (bf16[32,1536]{1,0:T(8,128)(2,1)S(1)}, bf16[32,1536]{1,0:T(8,128)(2,1)S(1)}, u32[]{:S(2)}, u32[]{:S(2)}) collective-permute-start(bf16[32,1536]{1,0:T(8,128)(2,1)S(1)} %activations.1.refs_0_), channel_id=1, source_target_pairs={{0,8},{8,0},{16,24},{24,16},{1,9},{9,1},{17,25},{25,17},{2,10},{10... | collective-permute-start | bytes 294920 | tf_op jit(solution)/shard_map/ppermute | solution.py:64
  43.4 16.0 %copy-start.3 = (f32[1,8,128]{2,1,0:T(8,128)S(1)}, f32[1,8,128]{2,1,0:T(8,128)}, u32[]{:S(2)}) copy-start(f32[1,8,128]{2,1,0:T(8,128)} %get-tuple-element.54.refs_7_) | copy-start | bytes 12292
  43.4 12.8 %collective-permute-start.14 = (bf16[128,768]{1,0:T(8,128)(2,1)S(1)}, bf16[128,768]{1,0:T(8,128)(2,1)S(1)}, u32[]{:S(2)}, u32[]{:S(2)}) collective-permute-start(bf16[128,768]{1,0:T(8,128)(2,1)S(1)} %get-tuple-element.44), channel_id=1, source_target_pairs={{0,1},{1,0},{2,3},{3,2},{4,5},{5,4},{6,7},{7,6},{8,9},{9,8},{10,11... | collective-permute-start | bytes 589832 | tf_op jit(solution)/shard_map/ppermute | solution.py:64
  43.5 5.4 %collective-permute-start.15 = (bf16[32,896]{1,0:T(8,128)(2,1)S(1)}, bf16[32,896]{1,0:T(8,128)(2,1)S(1)}, u32[]{:S(2)}, u32[]{:S(2)}) collective-permute-start(bf16[32,896]{1,0:T(8,128)(2,1)S(1)} %get-tuple-element.47), channel_id=1, source_target_pairs={{0,2},{1,3},{2,0},{3,1},{4,6},{5,7},{6,4},{7,5},{8,10},{9,11},{10,... | collective-permute-start | bytes 172040 | tf_op jit(solution)/shard_map/ppermute | solution.py:64
  43.7 6.6 %collective-permute-start.16 = (bf16[32,896]{1,0:T(8,128)(2,1)S(1)}, bf16[32,896]{1,0:T(8,128)(2,1)S(1)}, u32[]{:S(2)}, u32[]{:S(2)}) collective-permute-start(bf16[32,896]{1,0:T(8,128)(2,1)S(1)} %get-tuple-element.48), channel_id=1, source_target_pairs={{0,4},{1,5},{2,6},{3,7},{4,0},{5,1},{6,2},{7,3},{8,12},{9,13},{10,... | collective-permute-start | bytes 172040 | tf_op jit(solution)/shard_map/ppermute | solution.py:64
  46.6 6.0 %collective-permute-start.17 = (bf16[32,896]{1,0:T(8,128)(2,1)S(1)}, bf16[32,896]{1,0:T(8,128)(2,1)S(1)}, u32[]{:S(2)}, u32[]{:S(2)}) collective-permute-start(bf16[32,896]{1,0:T(8,128)(2,1)S(1)} %get-tuple-element.49), channel_id=1, source_target_pairs={{0,6},{1,7},{2,4},{3,5},{4,2},{5,3},{6,0},{7,1},{8,14},{9,15},{10,... | collective-permute-start | bytes 172040 | tf_op jit(solution)/shard_map/ppermute | solution.py:64
  52.6 5.1 %collective-permute-start.18 = (bf16[8,896]{1,0:T(8,128)(2,1)S(1)}, bf16[8,896]{1,0:T(8,128)(2,1)S(1)}, u32[]{:S(2)}, u32[]{:S(2)}) collective-permute-start(bf16[8,896]{1,0:T(8,128)(2,1)S(1)} %get-tuple-element.51), channel_id=1, source_target_pairs={{0,8},{8,0},{16,24},{24,16},{1,9},{9,1},{17,25},{25,17},{2,10},{10... | collective-permute-start | bytes 43016 | tf_op jit(solution)/shard_map/ppermute | solution.py:64
  53.7 4.0 %collective-permute-start.19 = (bf16[8,896]{1,0:T(8,128)(2,1)S(1)}, bf16[8,896]{1,0:T(8,128)(2,1)S(1)}, u32[]{:S(2)}, u32[]{:S(2)}) collective-permute-start(bf16[8,896]{1,0:T(8,128)(2,1)S(1)} %get-tuple-element.52), channel_id=1, source_target_pairs={{0,16},{8,24},{16,0},{24,8},{1,17},{9,25},{17,1},{25,9},{2,18},{10... | collective-permute-start | bytes 43016 | tf_op jit(solution)/shard_map/ppermute | solution.py:64
  54.7 4.6 %collective-permute-start.20 = (bf16[8,896]{1,0:T(8,128)(2,1)S(1)}, bf16[8,896]{1,0:T(8,128)(2,1)S(1)}, u32[]{:S(2)}, u32[]{:S(2)}) collective-permute-start(bf16[8,896]{1,0:T(8,128)(2,1)S(1)} %get-tuple-element.53), channel_id=1, source_target_pairs={{0,24},{8,16},{16,8},{24,0},{1,25},{9,17},{17,9},{25,1},{2,26},{10... | collective-permute-start | bytes 43016 | tf_op jit(solution)/shard_map/ppermute | solution.py:64

commit v4 on v3

--- a/solution.py
+++ b/solution.py
@@ -16,7 +16,7 @@
 BF16 = jnp.bfloat16
 F32 = jnp.float32
 VMEM_BYTES = 40 * 1024 * 1024
-ROUTE_VMEM_BYTES = 62 * 1024 * 1024
+ROUTE_VMEM_BYTES = 61 * 1024 * 1024
 
 NN = (((1,), (0,)), ((), ()))
 NT = (((1,), (1,)), ((), ()))
@@ -188,8 +188,8 @@
             outs[k][:, cut] = jnp.concatenate(rows, axis=0).astype(outs[k].dtype)
 
 
-def act_kernel(groups, *refs):
-    parts, out = refs[:groups], refs[groups]
+def act_kernel(groups, chips, chip, *refs):
+    parts, out, ordered = refs[:groups], refs[groups], refs[groups + 1]
     hid = out.shape[1] // 6
     for half in range(2):
         values = []
@@ -205,46 +205,44 @@
         results = (dh * b * sig * (1.0 + a * (1.0 - sig)), dh * swish, swish * b)
         for i, result in enumerate(results):
             cut = slice((3 * half + i) * hid, (3 * half + i + 1) * hid)
-            out[:, cut] = result.astype(BF16)
-
-
-def dx_kernel(groups, chips, *refs):
-    acts, (own, other), outs = refs[:groups], refs[groups : groups + 2], refs[groups + 2 :]
+            for c in range(chips):
+                ordered[chip[0] ^ c, :, cut] = rows_of(result, c * ROWS)
+    out[...] = jnp.concatenate([ordered[c] for c in range(chips)], axis=0).astype(BF16)
+
+
+def dx_kernel(groups, chips, me, *refs):
+    acts, (own, other, out) = refs[:groups], refs[groups:]
     depth, hid = own.shape[0], own.shape[1] // 2
     act = jnp.concatenate([a[...] for a in acts], axis=0)
     dx = mm(act[:, : 2 * hid], own[...], NT)
     dx = dx + mm(act[:, 3 * hid : 5 * hid], other[:depth, :], NT)
-    for c in range(chips):
-        rows = [rows_of(dx, (k * chips + c) * ROWS) for k in range(groups)]
-        outs[c][...] = jnp.concatenate(rows, axis=0).astype(outs[c].dtype)
-    outs[chips][...] = regroup(act[:, : 3 * hid], groups, chips)
-    outs[chips + 1][...] = regroup(act[:, 3 * hid :], groups, chips)
-
-
-def collect_kernel(groups, chips, *refs):
-    parts, outs = refs[:chips], refs[chips:]
-    sums = []
-    for first in range(0, chips, CHIPS):
-        total = parts[first][...].astype(F32)
-        for part in parts[first + 1 : first + CHIPS]:
-            total = total + part[...].astype(F32)
-        sums.append(total)
+    count = chips * ROWS
     for k in range(groups):
-        rows = [rows_of(total, k * ROWS) for total in sums]
-        outs[k][...] = jnp.concatenate(rows, axis=0).astype(BF16)
-
-
-def place_kernel(groups, experts, me, home, *refs):
-    parts, (picks, out, slices, result, sems) = refs[:groups], refs[groups:]
-    depth = parts[0].shape[1]
+        out[me[0] ^ k] = dx[k * count : (k + 1) * count].astype(BF16)
+
+
+def share_kernel(groups, chips, chip, *refs):
+    acts, own, out, blocks = refs[:groups], refs[groups], refs[groups + 1], refs[groups + 2]
+    hid = own.shape[1] // 3
+    for half, target in enumerate((own, out)):
+        for k in range(groups):
+            wide = acts[k][:, 3 * hid * half : 3 * hid * (half + 1)].astype(F32)
+            for c in range(chips):
+                blocks[k * chips + c] = rows_of(wide, c * ROWS)
+        order = [blocks[k * chips + (chip[0] ^ c)] for c in range(chips) for k in range(groups)]
+        target[...] = jnp.concatenate(order, axis=0).astype(BF16)
+
+
+def place_kernel(groups, experts, chips, returned, picks, after, out, result, sems):
+    depth = returned.shape[2]
     copies = []
-    for k in range(groups):
-        slices[me[0] ^ k] = parts[k][...].astype(F32)
     for s in range(groups):
         total = jnp.zeros((out.shape[0], depth), F32)
-        for x in range(experts):
-            rows = slices[s, x * ROWS : (x + 1) * ROWS, :].astype(BF16)
-            total = total + mm(picks[home[0] ^ x].astype(BF16), rows, TN)
+        for e in range(experts):
+            rows = jnp.zeros((ROWS, depth), F32)
+            for c in range(CHIPS):
+                rows = rows + returned[s * chips + e * CHIPS + c].astype(F32)
+            total = total + mm(picks[e].astype(BF16), rows.astype(BF16), TN)
         cut = slice(s * depth, (s + 1) * depth)
         result[:, cut] = total.astype(BF16)
         if depth % BLOCK == 0:
@@ -255,12 +253,6 @@
         copies[-1].start()
     for copy in copies:
         copy.wait()
-
-
-def regroup(act, groups, chips):
-    wide = act.astype(F32)
-    rows = [rows_of(wide, (k * chips + c) * ROWS) for c in range(chips) for k in range(groups)]
-    return jnp.concatenate(rows, axis=0).astype(BF16)
 
 
 def grads_kernel(own, other, act_own, act_other, grad_gate, grad_up, grad_down, token):
@@ -304,8 +296,8 @@
     depth, hid = w_gate.shape
     group, member = lax.axis_index("dp"), lax.axis_index("expert")
     me = jnp.reshape(group, (1,))
-    home = jnp.reshape(member // HSH, (1,))
     rows = groups * chips * ROWS
+    chip = jnp.reshape(member // 2, (1,))
 
     *sent, picks = call(
         functools.partial(route_kernel, groups, experts),
@@ -355,33 +347,39 @@
     other_rows = swap(own_rows, "expert", 1)
     summands = [partial[0]] + [swap(partial[k], "dp", k) for k in range(1, groups)]
     (act,) = call(
-        functools.partial(act_kernel, groups),
+        functools.partial(act_kernel, groups, chips),
         [shape((chips * ROWS, 6 * hid))],
-        (),
+        (chip,),
         summands,
+        scratch=[pltpu.VMEM((chips, ROWS, 6 * hid), F32)],
         flops=40 * chips * ROWS * hid,
         name="activations",
     )
     acts = [act] + [swap(act, "dp", k) for k in range(1, groups)]
-    *dx, act_own, act_out = call(
+    (dx,) = call(
         functools.partial(dx_kernel, groups, chips),
-        [shape((groups * ROWS, depth), F32 if c == 0 else BF16) for c in range(chips)]
-        + [shape((rows, 3 * hid))] * 2,
-        (),
+        [shape((groups, chips * ROWS, depth))],
+        (me,),
         (*acts, gate_up, other),
         flops=8 * rows * depth * hid,
         name="dx",
     )
-    returned = [dx[0]] + [swap(dx[c], "expert", 2 * c) for c in range(1, chips)]
-    home_rows = call(
-        functools.partial(collect_kernel, groups, chips),
-        [shape((experts * ROWS, depth))] * groups,
-        (),
-        returned,
-        flops=rows * depth,
-        name="collect",
-    )
-    placed = [home_rows[0]] + [swap(home_rows[k], "dp", k) for k in range(1, groups)]
+    act_own, act_out = call(
+        functools.partial(share_kernel, groups, chips),
+        [shape((rows, 3 * hid))] * 2,
+        (chip,),
+        acts,
+        after=(dx,),
+        scratch=[pltpu.VMEM((groups * chips, ROWS, 3 * hid), F32)],
+        name="share",
+    )
+    dx = dx.reshape(groups * chips, ROWS, depth)
+    same_core = [
+        [g * members + 2 * c + core for g in range(groups) for c in range(chips)] for core in range(2)
+    ]
+    returned = lax.all_to_all(
+        dx, ("dp", "expert"), split_axis=0, concat_axis=0, axis_index_groups=same_core, tiled=True
+    )
     act_other = swap(act_out, "expert", 1)
     *grads, done = call(
         grads_kernel,
@@ -392,17 +390,12 @@
         name="gradients",
     )
     (d_tokens,) = call(
-        functools.partial(place_kernel, groups, experts),
+        functools.partial(place_kernel, groups, experts, chips),
         [shape((count, width))],
-        (me, home),
-        (*placed, picks),
-        after=(done,),
+        (),
+        (returned, picks, done),
         far_out=True,
-        scratch=[
-            pltpu.VMEM((groups, experts * ROWS, depth), F32),
-            pltpu.VMEM((count, width), BF16),
-            pltpu.SemaphoreType.DMA((groups,)),
-        ],
+        scratch=[pltpu.VMEM((count, width), BF16), pltpu.SemaphoreType.DMA((groups,))],
         flops=2 * count * experts * ROWS * width,
         name="place",
     )

time: 60.8 us -> 58.8 us (0.967)
  starting transfers between devices: 24.3 us -> 21.1 us
  waiting for transfers between devices: 25.4 us -> 22.3 us
  Pallas kernels: 7.82 us -> 10.2 us
  local copies, waits for them, and re-layouts: 0.81 us -> 2.59 us
    ppermute x21 -> x15, starting transfers between devices: 24.3 us -> 16.2 us  [swap(): lax.ppermute(x, axis, [(i, i ^ k) for i in range(lax.axis_size(axis))])]
    ppermute x21 -> x15, waiting for transfers between devices: 25.4 us -> 19.6 us  [swap(): lax.ppermute(x, axis, [(i, i ^ k) for i in range(lax.axis_size(axis))])]
    all_to_all x0 -> x1, starting transfers between devices: none -> 4.9 us  [on_device(): lax.all_to_all(dx, ('dp', 'expert'), split_axis=0, concat_axis=0, axis_in...]
    all_to_all x0 -> x1, waiting for transfers between devices: none -> 2.67 us  [on_device(): lax.all_to_all(dx, ('dp', 'expert'), split_axis=0, concat_axis=0, axis_in...]
    pallas_call x8, Pallas kernels: 7.82 us -> 10.2 us  [call(): pl.pallas_call(body, out_shape=outs, in_specs=[pl.BlockSpec(memory_space=...]
    unnamed x23 -> x31, local copies, waits for them, and re-layouts: 0.8 us -> 2.58 us
  transfers between devices with their start and end apart: 21 -> 16, of which waited for: 14 -> 12; matrix products, arithmetic and copies ran while one was open for 1% -> 1% of each run, Pallas kernels for 5% -> 8%
where the time goes in v4:
time: 58.8 us; the launch traced here: 58.4 us
  waiting for transfers between devices  22.3 us (38%)
  starting transfers between devices  21.1 us (36%)
  Pallas kernels  10.2 us (17%)
  local copies, waits for them, and re-layouts  2.59 us (4%)
  between operations  2.22 us (4%)
    ppermute x15, waiting for transfers between devices, swap(): lax.ppermute(x, axis, [(i, i ^ k) for i in range(lax.axis_size(axis))])  19.6 us
    ppermute x15, starting transfers between devices, swap(): lax.ppermute(x, axis, [(i, i ^ k) for i in range(lax.axis_size(axis))])  16.2 us
    pallas_call x8, Pallas kernels, call(): pl.pallas_call(body, out_shape=outs, in_specs=[pl.BlockSpec(memory_space=...  10.2 us
    all_to_all x1, starting transfers between devices, on_device(): lax.all_to_all(dx, ('dp', 'expert'), split_axis=0, concat_axis=0, axis_in...  4.9 us
    all_to_all x1, waiting for transfers between devices, on_device(): lax.all_to_all(dx, ('dp', 'expert'), split_axis=0, concat_axis=0, axis_in...  2.67 us
    unnamed x31, local copies, waits for them, and re-layouts  2.58 us
  transfers between devices with their start and end apart: 16, of which 12 were waited for; matrix products, arithmetic and copies ran while one was open for 1% of the time, Pallas kernels for 8%

profile of v4, /device:TPU:0, one launch (start us, length us, event | category | flops | bytes accessed | tf_op | source)
XLA Modules:
  0.0 58.4 jit_solution(12401660032734738495)
XLA Ops:
  0.6 0.0 copy-start.10
  0.6 0.0 copy-start.9
  2.1 2.6 %route.1 = (bf16[16,896]{1,0:T(8,128)(2,1)}, bf16[16,896]{1,0:T(8,128)(2,1)}, bf16[16,896]{1,0:T(8,128)(2,1)}, bf16[16,896]{1,0:T(8,128)(2,1)}, f32[1,8,128]{2,1,0:T(8,128)}) custom-call(s32[1]{0:T(128)} %bitcast.refs_0_, s32[8,128]{1,0:T(8,128)} %bitcast.11, f32[8,128]{1,0:T(8,128)} %bitcast.12, bf16[128,3584]{1,0:T(8,128)(2,1)} %refs_3_.2, ...), custom_call_target="tpu_custom_call" | custom-call | flops 14680064 | bytes 1961992 | tf_op jit(solution)/shard_map/route/pallas_call | solution.py:37
  4.7 0.0 copy-start.11
  4.7 3.0 %collective-permute-start = (bf16[16,896]{1,0:T(8,128)(2,1)}, bf16[16,896]{1,0:T(8,128)(2,1)S(1)}, u32[]{:S(2)}, u32[]{:S(2)}) collective-permute-start(bf16[16,896]{1,0:T(8,128)(2,1)} %get-tuple-element.24), channel_id=1, source_target_pairs={{0,8},{8,0},{16,24},{24,16},{1,9},{9,1},{17,25},{25,17},{2,10},{10... | collective-permute-start | bytes 86024 | tf_op jit(solution)/shard_map/ppermute | solution.py:64
  7.7 1.5 %collective-permute-start.1 = (bf16[16,896]{1,0:T(8,128)(2,1)}, bf16[16,896]{1,0:T(8,128)(2,1)S(1)}, u32[]{:S(2)}, u32[]{:S(2)}) collective-permute-start(bf16[16,896]{1,0:T(8,128)(2,1)} %get-tuple-element.25), channel_id=1, source_target_pairs={{0,16},{8,24},{16,0},{24,8},{1,17},{9,25},{17,1},{25,9},{2,18},{10... | collective-permute-start | bytes 86024 | tf_op jit(solution)/shard_map/ppermute | solution.py:64
  9.2 0.0 collective-permute-start.2
  9.3 0.7 %constant_dynamic-update-slice_fusion.7 = bf16[64,896]{1,0:T(8,128)(2,1)S(1)} fusion(bf16[16,896]{1,0:T(8,128)(2,1)} %get-tuple-element.23), kind=kLoop, calls=%fused_computation.7 | loop fusion | bytes 28672
  10.0 0.0 collective-permute-done.refs_4_
  10.0 1.0 %weights.1 = (bf16[896,512]{1,0:T(8,128)(2,1)S(1)}, bf16[256,896]{1,0:T(8,128)(2,1)S(1)}, bf16[1408,512]{1,0:T(8,128)(2,1)S(1)}) custom-call(s32[1]{0:T(128)S(6)} %mul.3.refs_0_, f32[2,28]{1,0:T(2,128)S(1)} %bitcast.9, f32[2,28]{1,0:T(2,128)S(1)} %bitcast.10, f32[2,28]{1,0:T(2,128)S(1)} %copy-done.10, bf16[16,896]{1,0:T(8,128)(2,1)S(1)} %collective-permute-done.refs_4_, ...), custom_call_target="tpu_custom_call" | custom-call | flops 1376256 | bytes 4194304 | tf_op jit(solution)/shard_map/weights/pallas_call | solution.py:37
  11.1 0.1 collective-permute-start.6
  11.2 0.6 %collective-permute-done.1 = bf16[16,896]{1,0:T(8,128)(2,1)S(1)} collective-permute-done((bf16[16,896]{1,0:T(8,128)(2,1)}, bf16[16,896]{1,0:T(8,128)(2,1)S(1)}, u32[]{:S(2)}, u32[]{:S(2)}) %collective-permute-start.1) | collective-permute-done | bytes 28704 | tf_op jit(solution)/shard_map/ppermute | solution.py:64
  11.8 2.4 %collective-permute-done.2 = bf16[16,896]{1,0:T(8,128)(2,1)S(1)} collective-permute-done((bf16[16,896]{1,0:T(8,128)(2,1)}, bf16[16,896]{1,0:T(8,128)(2,1)S(1)}, u32[]{:S(2)}, u32[]{:S(2)}) %collective-permute-start.2) | collective-permute-done | bytes 28704 | tf_op jit(solution)/shard_map/ppermute | solution.py:64
  14.3 3.7 %collective-permute-start.5 = (bf16[64,896]{1,0:T(8,128)(2,1)S(1)}, bf16[64,896]{1,0:T(8,128)(2,1)S(1)}, u32[]{:S(2)}, u32[]{:S(2)}) collective-permute-start(bf16[64,896]{1,0:T(8,128)(2,1)S(1)} %constant_dynamic-update-slice_fusion.refs_0_), channel_id=1, source_target_pairs={{0,6},{1,7},{2,4},{3,5},{4,2},{5,3},{6,0},{7,1},{8,14},{9,15},{10,... | collective-permute-start | bytes 344072 | tf_op jit(solution)/shard_map/ppermute | solution.py:64
  17.9 0.0 collective-permute-start.4
  17.9 0.8 %collective-permute-start.3 = (bf16[64,896]{1,0:T(8,128)(2,1)S(1)}, bf16[64,896]{1,0:T(8,128)(2,1)S(1)}, u32[]{:S(2)}, u32[]{:S(2)}) collective-permute-start(bf16[64,896]{1,0:T(8,128)(2,1)S(1)} %constant_dynamic-update-slice_fusion.refs_0_), channel_id=1, source_target_pairs={{0,2},{1,3},{2,0},{3,1},{4,6},{5,7},{6,4},{7,5},{8,10},{9,11},{10,... | collective-permute-start | bytes 344072 | tf_op jit(solution)/shard_map/ppermute | solution.py:64
  18.7 2.7 %collective-permute-done.5.refs_3_ = bf16[64,896]{1,0:T(8,128)(2,1)S(1)} collective-permute-done((bf16[64,896]{1,0:T(8,128)(2,1)S(1)}, bf16[64,896]{1,0:T(8,128)(2,1)S(1)}, u32[]{:S(2)}, u32[]{:S(2)}) %collective-permute-start.5) | collective-permute-done | bytes 114720 | tf_op jit(solution)/shard_map/ppermute | solution.py:64
  21.4 4.5 %collective-permute-done.4.refs_2_ = bf16[64,896]{1,0:T(8,128)(2,1)S(1)} collective-permute-done((bf16[64,896]{1,0:T(8,128)(2,1)S(1)}, bf16[64,896]{1,0:T(8,128)(2,1)S(1)}, u32[]{:S(2)}, u32[]{:S(2)}) %collective-permute-start.4) | collective-permute-done | bytes 114720 | tf_op jit(solution)/shard_map/ppermute | solution.py:64
  25.9 0.0 collective-permute-done.3.refs_1_
  25.9 0.0 collective-permute-done.6.refs_6_
  25.9 1.3 %partial.1 = (f32[32,1536]{1,0:T(8,128)S(1)}, bf16[32,1536]{1,0:T(8,128)(2,1)}, bf16[32,1536]{1,0:T(8,128)(2,1)S(1)}, bf16[32,1536]{1,0:T(8,128)(2,1)S(1)}, bf16[256,896]{1,0:T(8,128)(2,1)S(1)}) custom-call(bf16[64,896]{1,0:T(8,128)(2,1)S(1)} %constant_dynamic-update-slice_fusion.refs_0_, bf16[64,896]{1,0:T(8,128)(2,1)S(1)} %collective-permute-done.3.refs_1_, ...), custom_call_target="tpu_custom_call" | custom-call | flops 352321536 | bytes 4227072 | tf_op jit(solution)/shard_map/partial/pallas_call | solution.py:37
  27.2 1.3 %collective-permute-start.7 = (bf16[32,1536]{1,0:T(8,128)(2,1)}, bf16[32,1536]{1,0:T(8,128)(2,1)S(1)}, u32[]{:S(2)}, u32[]{:S(2)}) collective-permute-start(bf16[32,1536]{1,0:T(8,128)(2,1)} %get-tuple-element.31), channel_id=1, source_target_pairs={{0,8},{8,0},{16,24},{24,16},{1,9},{9,1},{17,25},{25,17},{2,10},{10... | collective-permute-start | bytes 294920 | tf_op jit(solution)/shard_map/ppermute | solution.py:64
  28.5 1.5 %collective-permute-start.8 = (bf16[32,1536]{1,0:T(8,128)(2,1)S(1)}, bf16[32,1536]{1,0:T(8,128)(2,1)S(1)}, u32[]{:S(2)}, u32[]{:S(2)}) collective-permute-start(bf16[32,1536]{1,0:T(8,128)(2,1)S(1)} %get-tuple-element.32), channel_id=1, source_target_pairs={{0,16},{8,24},{16,0},{24,8},{1,17},{9,25},{17,1},{25,9},{2,18},{10... | collective-permute-start | bytes 294920 | tf_op jit(solution)/shard_map/ppermute | solution.py:64
  30.0 0.7 %collective-permute-start.9 = (bf16[32,1536]{1,0:T(8,128)(2,1)S(1)}, bf16[32,1536]{1,0:T(8,128)(2,1)S(1)}, u32[]{:S(2)}, u32[]{:S(2)}) collective-permute-start(bf16[32,1536]{1,0:T(8,128)(2,1)S(1)} %get-tuple-element.33), channel_id=1, source_target_pairs={{0,24},{8,16},{16,8},{24,0},{1,25},{9,17},{17,9},{25,1},{2,26},{10... | collective-permute-start | bytes 294920 | tf_op jit(solution)/shard_map/ppermute | solution.py:64
  30.7 2.3 %collective-permute-done.7.refs_2_ = bf16[32,1536]{1,0:T(8,128)(2,1)S(1)} collective-permute-done((bf16[32,1536]{1,0:T(8,128)(2,1)}, bf16[32,1536]{1,0:T(8,128)(2,1)S(1)}, u32[]{:S(2)}, u32[]{:S(2)}) %collective-permute-start.7) | collective-permute-done | bytes 98336 | tf_op jit(solution)/shard_map/ppermute | solution.py:64
  33.0 1.2 %collective-permute-done.8.refs_3_ = bf16[32,1536]{1,0:T(8,128)(2,1)S(1)} collective-permute-done((bf16[32,1536]{1,0:T(8,128)(2,1)S(1)}, bf16[32,1536]{1,0:T(8,128)(2,1)S(1)}, u32[]{:S(2)}, u32[]{:S(2)}) %collective-permute-start.8) | collective-permute-done | bytes 98336 | tf_op jit(solution)/shard_map/ppermute | solution.py:64
  34.2 1.4 %collective-permute-done.9.refs_4_ = bf16[32,1536]{1,0:T(8,128)(2,1)S(1)} collective-permute-done((bf16[32,1536]{1,0:T(8,128)(2,1)S(1)}, bf16[32,1536]{1,0:T(8,128)(2,1)S(1)}, u32[]{:S(2)}, u32[]{:S(2)}) %collective-permute-start.9) | collective-permute-done | bytes 98336 | tf_op jit(solution)/shard_map/ppermute | solution.py:64
  35.6 0.1 activations.1.refs_1_.refs_2_
  35.6 0.7 %collective-permute-start.12 = (bf16[32,1536]{1,0:T(8,128)(2,1)S(1)}, bf16[32,1536]{1,0:T(8,128)(2,1)S(1)}, u32[]{:S(2)}, u32[]{:S(2)}) collective-permute-start(bf16[32,1536]{1,0:T(8,128)(2,1)S(1)} %activations.1.refs_1_.refs_2_), channel_id=1, source_target_pairs={{0,24},{8,16},{16,8},{24,0},{1,25},{9,17},{17,9},{25,1},{2,26},{10... | collective-permute-start | bytes 294920 | tf_op jit(solution)/shard_map/ppermute | solution.py:64
  36.4 1.3 %collective-permute-start.11 = (bf16[32,1536]{1,0:T(8,128)(2,1)S(1)}, bf16[32,1536]{1,0:T(8,128)(2,1)S(1)}, u32[]{:S(2)}, u32[]{:S(2)}) collective-permute-start(bf16[32,1536]{1,0:T(8,128)(2,1)S(1)} %activations.1.refs_1_.refs_2_), channel_id=1, source_target_pairs={{0,16},{8,24},{16,0},{24,8},{1,17},{9,25},{17,1},{25,9},{2,18},{10... | collective-permute-start | bytes 294920 | tf_op jit(solution)/shard_map/ppermute | solution.py:64
  37.7 1.5 %collective-permute-start.10 = (bf16[32,1536]{1,0:T(8,128)(2,1)S(1)}, bf16[32,1536]{1,0:T(8,128)(2,1)S(1)}, u32[]{:S(2)}, u32[]{:S(2)}) collective-permute-start(bf16[32,1536]{1,0:T(8,128)(2,1)S(1)} %activations.1.refs_1_.refs_2_), channel_id=1, source_target_pairs={{0,8},{8,0},{16,24},{24,16},{1,9},{9,1},{17,25},{25,17},{2,10},{10... | collective-permute-start | bytes 294920 | tf_op jit(solution)/shard_map/ppermute | solution.py:64
  39.2 0.0 collective-permute-start.13
  39.2 2.1 %collective-permute-done.12.refs_4_.refs_5_ = bf16[32,1536]{1,0:T(8,128)(2,1)S(1)} collective-permute-done((bf16[32,1536]{1,0:T(8,128)(2,1)S(1)}, bf16[32,1536]{1,0:T(8,128)(2,1)S(1)}, u32[]{:S(2)}, u32[]{:S(2)}) %collective-permute-start.12) | collective-permute-done | bytes 98336 | tf_op jit(solution)/shard_map/ppermute | solution.py:64
  41.3 0.7 %collective-permute-done.11.refs_3_.refs_4_ = bf16[32,1536]{1,0:T(8,128)(2,1)S(1)} collective-permute-done((bf16[32,1536]{1,0:T(8,128)(2,1)S(1)}, bf16[32,1536]{1,0:T(8,128)(2,1)S(1)}, u32[]{:S(2)}, u32[]{:S(2)}) %collective-permute-start.11) | collective-permute-done | bytes 98336 | tf_op jit(solution)/shard_map/ppermute | solution.py:64
  42.1 0.3 collective-permute-done.10.refs_2_.refs_3_
  42.3 1.4 %dx.1.refs_1_ = bf16[4,32,896]{2,1,0:T(8,128)(2,1)} custom-call(s32[1]{0:T(128)} %bitcast.refs_0_, bf16[32,1536]{1,0:T(8,128)(2,1)S(1)} %activations.1.refs_1_.refs_2_, bf16[32,1536]{1,0:T(8,128)(2,1)S(1)} %collective-permute-done.10.refs_2_.refs_3_, bf16[32,1536]{1,0:T(8,128)(2,1)S(1)} %collective-permute-done.11.refs_3_.refs_4_, ...), custom_call_target="tpu_custom_call" | custom-call | flops 234881024 | bytes 2981888 | tf_op jit(solution)/shard_map/dx/pallas_call | solution.py:37
  43.7 0.0 copy-done.3
  43.7 4.9 %all-to-all-start = ((bf16[16,8,896]{2,1,0:T(8,128)(2,1)}), bf16[16,8,896]{2,1,0:T(8,128)(2,1)S(1)}, u32[]{:S(2)}, u32[]{:S(2)}) async-start(bf16[16,8,896]{2,1,0:T(8,128)(2,1)} %bitcast.7), calls=%async_computation | async-start | bytes 458752 | tf_op jit(solution)/shard_map/all_to_all | solution.py:380
  48.6 0.0 copy-start.4
  48.7 0.9 %copy-done.4 = bf16[32,1536]{1,0:T(8,128)(2,1)S(1)} copy-done((bf16[32,1536]{1,0:T(8,128)(2,1)S(1)}, bf16[32,1536]{1,0:T(8,128)(2,1)}, u32[]{:S(2)}) %copy-start.4) | copy-done | bytes 98328
  49.5 0.9 %copy-done.6 = bf16[32,1536]{1,0:T(8,128)(2,1)S(1)} copy-done((bf16[32,1536]{1,0:T(8,128)(2,1)S(1)}, bf16[32,1536]{1,0:T(8,128)(2,1)}, u32[]{:S(2)}) %copy-start.6) | copy-done | bytes 98328
  50.4 1.0 %share.1 = (bf16[128,768]{1,0:T(8,128)(2,1)S(1)}, bf16[128,768]{1,0:T(8,128)(2,1)S(1)}) custom-call(s32[1]{0:T(128)} %bitcast.1.refs_0_, bf16[4,32,896]{2,1,0:T(8,128)(2,1)} %dx.1.refs_1_, bf16[32,1536]{1,0:T(8,128)(2,1)S(1)} %activations.1.refs_1_.refs_2_, bf16[32,1536]{1,0:T(8,128)(2,1)S(1)} %copy-done.6, bf16[32,1536]{1,0:T(8,128)(2,1)S(1)} %copy-done.4, ...), custom_call_target="tpu_custom_call" | custom-call | bytes 786432 | tf_op jit(solution)/shard_map/share/pallas_call | solution.py:37
  51.5 0.1 collective-permute-start.14
  51.6 1.4 %collective-permute-done.14.refs_3_ = bf16[128,768]{1,0:T(8,128)(2,1)S(1)} collective-permute-done((bf16[128,768]{1,0:T(8,128)(2,1)S(1)}, bf16[128,768]{1,0:T(8,128)(2,1)S(1)}, u32[]{:S(2)}, u32[]{:S(2)}) %collective-permute-start.14) | collective-permute-done | bytes 196640 | tf_op jit(solution)/shard_map/ppermute | solution.py:64
  53.0 0.0 collective-permute-done.13.refs_1_
  53.0 1.5 %gradients.1 = (bf16[896,256]{1,0:T(8,128)(2,1)}, bf16[896,256]{1,0:T(8,128)(2,1)}, bf16[256,896]{1,0:T(8,128)(2,1)}, f32[8,128]{1,0:T(8,128)S(1)}) custom-call(bf16[256,896]{1,0:T(8,128)(2,1)S(1)} %get-tuple-element.35.refs_0_, bf16[256,896]{1,0:T(8,128)(2,1)S(1)} %collective-permute-done.13.refs_1_, bf16[128,768]{1,0:T(8,128)(2,1)S(1)} %get-tuple-element.36.refs_2_, ...), custom_call_target="tpu_custom_call" | custom-call | flops 352321536 | bytes 2691072 | tf_op jit(solution)/shard_map/gradients/pallas_call | solution.py:37
  54.5 2.7 %all-to-all-done.refs_0_ = bf16[16,8,896]{2,1,0:T(8,128)(2,1)S(1)} async-done(((bf16[16,8,896]{2,1,0:T(8,128)(2,1)}), bf16[16,8,896]{2,1,0:T(8,128)(2,1)S(1)}, u32[]{:S(2)}, u32[]{:S(2)}) %all-to-all-start) | async-done | bytes 229408 | tf_op jit(solution)/shard_map/all_to_all | solution.py:380
  57.2 1.2 %place.1 = bf16[128,3584]{1,0:T(8,128)(2,1)} custom-call(bf16[16,8,896]{2,1,0:T(8,128)(2,1)S(1)} %all-to-all-done.refs_0_, f32[1,8,128]{2,1,0:T(8,128)S(1)} %copy-done.7, f32[8,128]{1,0:T(8,128)S(1)} %get-tuple-element.38.refs_2_), custom_call_target="tpu_custom_call" | custom-call | flops 7340032 | bytes 1155072 | tf_op jit(solution)/shard_map/place/pallas_call | solution.py:37
  (24 shorter events, 0.1 us)
Async XLA Ops:
  0.6 9.3 %copy-start.10 = (f32[2,28]{1,0:T(2,128)S(1)}, f32[2,28]{1,0:T(2,128)}, u32[]{:S(2)}) copy-start(f32[2,28]{1,0:T(2,128)} %refs_3_.3) | copy-start | bytes 676
  0.6 9.3 %copy-start.9 = (f32[28,2]{0,1:T(2,128)S(1)}, f32[28,2]{0,1:T(2,128)}, u32[]{:S(2)}) copy-start(f32[28,2]{0,1:T(2,128)} %param.22) | copy-start | bytes 676
  0.7 9.3 %copy-start.8 = (f32[28,2]{0,1:T(2,128)S(1)}, f32[28,2]{0,1:T(2,128)}, u32[]{:S(2)}) copy-start(f32[28,2]{0,1:T(2,128)} %param.21) | copy-start | bytes 676
  0.7 9.3 %copy-start.2 = (bf16[256,896]{1,0:T(8,128)(2,1)S(1)}, bf16[256,896]{1,0:T(8,128)(2,1)}, u32[]{:S(2)}) copy-start(bf16[256,896]{1,0:T(8,128)(2,1)} %refs_7_.1) | copy-start | bytes 1376260
  0.7 9.3 %copy-start.1 = (bf16[896,256]{1,0:T(8,128)(2,1)S(1)}, bf16[896,256]{1,0:T(8,128)(2,1)}, u32[]{:S(2)}) copy-start(bf16[896,256]{1,0:T(8,128)(2,1)} %refs_6_.2) | copy-start | bytes 1376260
  0.7 9.3 %copy-start = (bf16[896,256]{1,0:T(8,128)(2,1)S(1)}, bf16[896,256]{1,0:T(8,128)(2,1)}, u32[]{:S(2)}) copy-start(bf16[896,256]{1,0:T(8,128)(2,1)} %refs_5_.1) | copy-start | bytes 1376260
  4.7 9.5 %copy-start.11 = (bf16[16,896]{1,0:T(8,128)(2,1)S(1)}, bf16[16,896]{1,0:T(8,128)(2,1)}, u32[]{:S(2)}) copy-start(bf16[16,896]{1,0:T(8,128)(2,1)} %get-tuple-element.23) | copy-start | bytes 86020
  4.7 5.3 %collective-permute-start = (bf16[16,896]{1,0:T(8,128)(2,1)}, bf16[16,896]{1,0:T(8,128)(2,1)S(1)}, u32[]{:S(2)}, u32[]{:S(2)}) collective-permute-start(bf16[16,896]{1,0:T(8,128)(2,1)} %get-tuple-element.24), channel_id=1, source_target_pairs={{0,8},{8,0},{16,24},{24,16},{1,9},{9,1},{17,25},{25,17},{2,10},{10... | collective-permute-start | bytes 86024 | tf_op jit(solution)/shard_map/ppermute | solution.py:64
  7.7 4.1 %collective-permute-start.1 = (bf16[16,896]{1,0:T(8,128)(2,1)}, bf16[16,896]{1,0:T(8,128)(2,1)S(1)}, u32[]{:S(2)}, u32[]{:S(2)}) collective-permute-start(bf16[16,896]{1,0:T(8,128)(2,1)} %get-tuple-element.25), channel_id=1, source_target_pairs={{0,16},{8,24},{16,0},{24,8},{1,17},{9,25},{17,1},{25,9},{2,18},{10... | collective-permute-start | bytes 86024 | tf_op jit(solution)/shard_map/ppermute | solution.py:64
  9.2 5.0 %collective-permute-start.2 = (bf16[16,896]{1,0:T(8,128)(2,1)}, bf16[16,896]{1,0:T(8,128)(2,1)S(1)}, u32[]{:S(2)}, u32[]{:S(2)}) collective-permute-start(bf16[16,896]{1,0:T(8,128)(2,1)} %get-tuple-element.26), channel_id=1, source_target_pairs={{0,24},{8,16},{16,8},{24,0},{1,25},{9,17},{17,9},{25,1},{2,26},{10... | collective-permute-start | bytes 86024 | tf_op jit(solution)/shard_map/ppermute | solution.py:64
  11.1 14.8 %collective-permute-start.6 = (bf16[1408,512]{1,0:T(8,128)(2,1)S(1)}, bf16[1408,512]{1,0:T(8,128)(2,1)S(1)}, u32[]{:S(2)}, u32[]{:S(2)}) collective-permute-start(bf16[1408,512]{1,0:T(8,128)(2,1)S(1)} %get-tuple-element.29), channel_id=1, source_target_pairs={{0,1},{1,0},{2,3},{3,2},{4,5},{5,4},{6,7},{7,6},{8,9},{9,8},{10,11... | collective-permute-start | bytes 4325384 | tf_op jit(solution)/shard_map/ppermute | solution.py:64
  14.3 7.2 %collective-permute-start.5 = (bf16[64,896]{1,0:T(8,128)(2,1)S(1)}, bf16[64,896]{1,0:T(8,128)(2,1)S(1)}, u32[]{:S(2)}, u32[]{:S(2)}) collective-permute-start(bf16[64,896]{1,0:T(8,128)(2,1)S(1)} %constant_dynamic-update-slice_fusion.refs_0_), channel_id=1, source_target_pairs={{0,6},{1,7},{2,4},{3,5},{4,2},{5,3},{6,0},{7,1},{8,14},{9,15},{10,... | collective-permute-start | bytes 344072 | tf_op jit(solution)/shard_map/ppermute | solution.py:64
  17.9 8.0 %collective-permute-start.4 = (bf16[64,896]{1,0:T(8,128)(2,1)S(1)}, bf16[64,896]{1,0:T(8,128)(2,1)S(1)}, u32[]{:S(2)}, u32[]{:S(2)}) collective-permute-start(bf16[64,896]{1,0:T(8,128)(2,1)S(1)} %constant_dynamic-update-slice_fusion.refs_0_), channel_id=1, source_target_pairs={{0,4},{1,5},{2,6},{3,7},{4,0},{5,1},{6,2},{7,3},{8,12},{9,13},{10,... | collective-permute-start | bytes 344072 | tf_op jit(solution)/shard_map/ppermute | solution.py:64
  17.9 8.0 %collective-permute-start.3 = (bf16[64,896]{1,0:T(8,128)(2,1)S(1)}, bf16[64,896]{1,0:T(8,128)(2,1)S(1)}, u32[]{:S(2)}, u32[]{:S(2)}) collective-permute-start(bf16[64,896]{1,0:T(8,128)(2,1)S(1)} %constant_dynamic-update-slice_fusion.refs_0_), channel_id=1, source_target_pairs={{0,2},{1,3},{2,0},{3,1},{4,6},{5,7},{6,4},{7,5},{8,10},{9,11},{10,... | collective-permute-start | bytes 344072 | tf_op jit(solution)/shard_map/ppermute | solution.py:64
  27.2 5.8 %collective-permute-start.7 = (bf16[32,1536]{1,0:T(8,128)(2,1)}, bf16[32,1536]{1,0:T(8,128)(2,1)S(1)}, u32[]{:S(2)}, u32[]{:S(2)}) collective-permute-start(bf16[32,1536]{1,0:T(8,128)(2,1)} %get-tuple-element.31), channel_id=1, source_target_pairs={{0,8},{8,0},{16,24},{24,16},{1,9},{9,1},{17,25},{25,17},{2,10},{10... | collective-permute-start | bytes 294920 | tf_op jit(solution)/shard_map/ppermute | solution.py:64
  28.5 5.7 %collective-permute-start.8 = (bf16[32,1536]{1,0:T(8,128)(2,1)S(1)}, bf16[32,1536]{1,0:T(8,128)(2,1)S(1)}, u32[]{:S(2)}, u32[]{:S(2)}) collective-permute-start(bf16[32,1536]{1,0:T(8,128)(2,1)S(1)} %get-tuple-element.32), channel_id=1, source_target_pairs={{0,16},{8,24},{16,0},{24,8},{1,17},{9,25},{17,1},{25,9},{2,18},{10... | collective-permute-start | bytes 294920 | tf_op jit(solution)/shard_map/ppermute | solution.py:64
  30.0 5.5 %collective-permute-start.9 = (bf16[32,1536]{1,0:T(8,128)(2,1)S(1)}, bf16[32,1536]{1,0:T(8,128)(2,1)S(1)}, u32[]{:S(2)}, u32[]{:S(2)}) collective-permute-start(bf16[32,1536]{1,0:T(8,128)(2,1)S(1)} %get-tuple-element.33), channel_id=1, source_target_pairs={{0,24},{8,16},{16,8},{24,0},{1,25},{9,17},{17,9},{25,1},{2,26},{10... | collective-permute-start | bytes 294920 | tf_op jit(solution)/shard_map/ppermute | solution.py:64
  35.6 5.7 %collective-permute-start.12 = (bf16[32,1536]{1,0:T(8,128)(2,1)S(1)}, bf16[32,1536]{1,0:T(8,128)(2,1)S(1)}, u32[]{:S(2)}, u32[]{:S(2)}) collective-permute-start(bf16[32,1536]{1,0:T(8,128)(2,1)S(1)} %activations.1.refs_1_.refs_2_), channel_id=1, source_target_pairs={{0,24},{8,16},{16,8},{24,0},{1,25},{9,17},{17,9},{25,1},{2,26},{10... | collective-permute-start | bytes 294920 | tf_op jit(solution)/shard_map/ppermute | solution.py:64
  36.4 5.7 %collective-permute-start.11 = (bf16[32,1536]{1,0:T(8,128)(2,1)S(1)}, bf16[32,1536]{1,0:T(8,128)(2,1)S(1)}, u32[]{:S(2)}, u32[]{:S(2)}) collective-permute-start(bf16[32,1536]{1,0:T(8,128)(2,1)S(1)} %activations.1.refs_1_.refs_2_), channel_id=1, source_target_pairs={{0,16},{8,24},{16,0},{24,8},{1,17},{9,25},{17,1},{25,9},{2,18},{10... | collective-permute-start | bytes 294920 | tf_op jit(solution)/shard_map/ppermute | solution.py:64
  37.7 4.6 %collective-permute-start.10 = (bf16[32,1536]{1,0:T(8,128)(2,1)S(1)}, bf16[32,1536]{1,0:T(8,128)(2,1)S(1)}, u32[]{:S(2)}, u32[]{:S(2)}) collective-permute-start(bf16[32,1536]{1,0:T(8,128)(2,1)S(1)} %activations.1.refs_1_.refs_2_), channel_id=1, source_target_pairs={{0,8},{8,0},{16,24},{24,16},{1,9},{9,1},{17,25},{25,17},{2,10},{10... | collective-permute-start | bytes 294920 | tf_op jit(solution)/shard_map/ppermute | solution.py:64
  39.2 13.8 %collective-permute-start.13 = (bf16[256,896]{1,0:T(8,128)(2,1)S(1)}, bf16[256,896]{1,0:T(8,128)(2,1)S(1)}, u32[]{:S(2)}, u32[]{:S(2)}) collective-permute-start(bf16[256,896]{1,0:T(8,128)(2,1)S(1)} %get-tuple-element.35.refs_0_), channel_id=1, source_target_pairs={{0,1},{1,0},{2,3},{3,2},{4,5},{5,4},{6,7},{7,6},{8,9},{9,8},{10,11... | collective-permute-start | bytes 1376264 | tf_op jit(solution)/shard_map/ppermute | solution.py:64
  42.1 1.7 %copy-start.3 = (bf16[32,1536]{1,0:T(8,128)(2,1)}, bf16[32,1536]{1,0:T(8,128)(2,1)S(1)}, u32[]{:S(2)}) copy-start(bf16[32,1536]{1,0:T(8,128)(2,1)S(1)} %collective-permute-done.11.refs_3_.refs_4_) | copy-start | bytes 294916
  42.3 1.4 %copy-start.5 = (bf16[32,1536]{1,0:T(8,128)(2,1)}, bf16[32,1536]{1,0:T(8,128)(2,1)S(1)}, u32[]{:S(2)}) copy-start(bf16[32,1536]{1,0:T(8,128)(2,1)S(1)} %collective-permute-done.10.refs_2_.refs_3_) | copy-start | bytes 294916
  43.7 13.4 %copy-start.7 = (f32[1,8,128]{2,1,0:T(8,128)S(1)}, f32[1,8,128]{2,1,0:T(8,128)}, u32[]{:S(2)}) copy-start(f32[1,8,128]{2,1,0:T(8,128)} %get-tuple-element.34.refs_1_) | copy-start | bytes 12292
  43.7 13.4 %all-to-all-start = ((bf16[16,8,896]{2,1,0:T(8,128)(2,1)}), bf16[16,8,896]{2,1,0:T(8,128)(2,1)S(1)}, u32[]{:S(2)}, u32[]{:S(2)}) async-start(bf16[16,8,896]{2,1,0:T(8,128)(2,1)} %bitcast.7), calls=%async_computation | async-start | bytes 458752 | tf_op jit(solution)/shard_map/all_to_all | solution.py:380
  48.6 0.9 %copy-start.4 = (bf16[32,1536]{1,0:T(8,128)(2,1)S(1)}, bf16[32,1536]{1,0:T(8,128)(2,1)}, u32[]{:S(2)}) copy-start(bf16[32,1536]{1,0:T(8,128)(2,1)} %copy-done.3) | copy-start | bytes 294916
  49.5 0.9 %copy-start.6 = (bf16[32,1536]{1,0:T(8,128)(2,1)S(1)}, bf16[32,1536]{1,0:T(8,128)(2,1)}, u32[]{:S(2)}) copy-start(bf16[32,1536]{1,0:T(8,128)(2,1)} %copy-done.5) | copy-start | bytes 294916
  51.5 1.5 %collective-permute-start.14 = (bf16[128,768]{1,0:T(8,128)(2,1)S(1)}, bf16[128,768]{1,0:T(8,128)(2,1)S(1)}, u32[]{:S(2)}, u32[]{:S(2)}) collective-permute-start(bf16[128,768]{1,0:T(8,128)(2,1)S(1)} %get-tuple-element.37), channel_id=1, source_target_pairs={{0,1},{1,0},{2,3},{3,2},{4,5},{5,4},{6,7},{7,6},{8,9},{9,8},{10,11... | collective-permute-start | bytes 589832 | tf_op jit(solution)/shard_map/ppermute | solution.py:64

commit v5 on v4

--- a/solution.py
+++ b/solution.py
@@ -68,7 +68,7 @@
     return value[first : first + count]
 
 
-def route_kernel(groups, experts, me, ids_in, weight_in, tokens_in, cots_in, live, plan, *rest):
+def route_kernel(groups, experts, ids_in, weight_in, tokens_in, cots_in, live, plan, *rest):
     outs, picks, scratch = rest[:groups], rest[groups], rest[groups + 1 :]
     ids, weight, tokens, cots, slices, sems = scratch
     count, width = tokens.shape
@@ -124,14 +124,15 @@
             parts += [rows_of(token_rows, e * ROWS), rows_of(cot_rows, e * ROWS)]
         slices[s] = jnp.concatenate(parts, axis=0).astype(BF16)
     for k in range(groups):
-        outs[k][...] = slices[me[0] ^ k]
-
-
-def weights_kernel(first, scale_gate, scale_up, scale_down, gate, up, down, gate_up, down_out, packed):
+        outs[k][...] = slices[lax.axis_index("dp") ^ k]
+
+
+def weights_kernel(scale_gate, scale_up, scale_down, gate, up, down, gate_up, down_out, packed):
     depth, hid = gate.shape
+    first = lax.axis_index("dp") * depth
     step = math.gcd(depth, BLOCK)
     for i in range(depth // step):
-        block = (first[0] + i * step) // BLOCK
+        block = (first + i * step) // BLOCK
         for h in range(hid // BLOCK):
             at = (slice(i * step, (i + 1) * step), slice(h * BLOCK, (h + 1) * BLOCK))
             to = (at[0], slice(hid + h * BLOCK, hid + (h + 1) * BLOCK))
@@ -139,13 +140,13 @@
                 out[at] = (gate[at].astype(F32) * scale_gate[h, block]).astype(BF16)
                 out[to] = (up[at].astype(F32) * scale_up[h, block]).astype(BF16)
     lane = lax.broadcasted_iota(jnp.int32, (1, depth), 1)
-    start = first[0] // BLOCK
+    start = first // BLOCK
     last = scale_down.shape[1] - 1
     for h in range(hid // BLOCK):
         spread = jnp.zeros((1, depth), F32) + scale_down[h, start]
         for j in range(1, depth // BLOCK + 2):
             block = jnp.minimum(start + j, last)
-            spread = jnp.where(lane >= (start + j) * BLOCK - first[0], scale_down[h, block], spread)
+            spread = jnp.where(lane >= (start + j) * BLOCK - first, scale_down[h, block], spread)
         at = slice(h * BLOCK, (h + 1) * BLOCK)
         value = (down[at, :].astype(F32) * spread).astype(BF16)
         down_out[at, :] = value
@@ -188,7 +189,7 @@
             outs[k][:, cut] = jnp.concatenate(rows, axis=0).astype(outs[k].dtype)
 
 
-def act_kernel(groups, chips, chip, *refs):
+def act_kernel(groups, chips, *refs):
     parts, out, ordered = refs[:groups], refs[groups], refs[groups + 1]
     hid = out.shape[1] // 6
     for half in range(2):
@@ -206,11 +207,11 @@
         for i, result in enumerate(results):
             cut = slice((3 * half + i) * hid, (3 * half + i + 1) * hid)
             for c in range(chips):
-                ordered[chip[0] ^ c, :, cut] = rows_of(result, c * ROWS)
+                ordered[(lax.axis_index("expert") // 2) ^ c, :, cut] = rows_of(result, c * ROWS)
     out[...] = jnp.concatenate([ordered[c] for c in range(chips)], axis=0).astype(BF16)
 
 
-def dx_kernel(groups, chips, me, *refs):
+def dx_kernel(groups, chips, *refs):
     acts, (own, other, out) = refs[:groups], refs[groups:]
     depth, hid = own.shape[0], own.shape[1] // 2
     act = jnp.concatenate([a[...] for a in acts], axis=0)
@@ -218,19 +219,12 @@
     dx = dx + mm(act[:, 3 * hid : 5 * hid], other[:depth, :], NT)
     count = chips * ROWS
     for k in range(groups):
-        out[me[0] ^ k] = dx[k * count : (k + 1) * count].astype(BF16)
-
-
-def share_kernel(groups, chips, chip, *refs):
-    acts, own, out, blocks = refs[:groups], refs[groups], refs[groups + 1], refs[groups + 2]
-    hid = own.shape[1] // 3
-    for half, target in enumerate((own, out)):
-        for k in range(groups):
-            wide = acts[k][:, 3 * hid * half : 3 * hid * (half + 1)].astype(F32)
-            for c in range(chips):
-                blocks[k * chips + c] = rows_of(wide, c * ROWS)
-        order = [blocks[k * chips + (chip[0] ^ c)] for c in range(chips) for k in range(groups)]
-        target[...] = jnp.concatenate(order, axis=0).astype(BF16)
+        out[lax.axis_index("dp") ^ k] = dx[k * count : (k + 1) * count].astype(BF16)
+
+
+def share_kernel(groups, *refs):
+    half = refs[groups].shape[1]
+    refs[groups][...] = jnp.concatenate([act[:, half:] for act in refs[:groups]], axis=0)
 
 
 def place_kernel(groups, experts, chips, returned, picks, after, out, result, sems):
@@ -255,12 +249,25 @@
         copy.wait()
 
 
-def grads_kernel(own, other, act_own, act_other, grad_gate, grad_up, grad_down, token):
-    hid, half = grad_gate.shape[1], own.shape[0] // 2
-    acts = (act_own, act_other)
+def grads_kernel(groups, chips, own, other, *refs):
+    acts, act_other = refs[:groups], refs[groups]
+    grad_gate, grad_up, grad_down, token, blocks = refs[groups + 1 :]
+    hid, half, count = grad_gate.shape[1], own.shape[0] // 2, chips * ROWS
     tokens = jnp.concatenate([own[:half, :], other[:half, :]], axis=0)
     cots = jnp.concatenate([own[half:, :], other[half:, :]], axis=0)
-    act = jnp.concatenate([a[...] for a in acts], axis=0)
+    for k in range(groups):
+        pair = acts[k][:, : 3 * hid], act_other[k * count : (k + 1) * count, :]
+        for i, part in enumerate(pair):
+            wide = part.astype(F32)
+            for c in range(chips):
+                blocks[i, k * chips + c] = rows_of(wide, c * ROWS)
+    order = [
+        blocks[i, k * chips + ((lax.axis_index("expert") // 2) ^ c)]
+        for i in range(2)
+        for c in range(chips)
+        for k in range(groups)
+    ]
+    act = jnp.concatenate(order, axis=0).astype(BF16)
     grad_gate[...] = mm(tokens, act[:, :hid], TN).astype(BF16)
     grad_up[...] = mm(tokens, act[:, hid : 2 * hid], TN).astype(BF16)
     grad_down[...] = mm(act[:, 2 * hid :], cots, TN).astype(BF16)
@@ -295,14 +302,12 @@
     count, width = tokens.shape
     depth, hid = w_gate.shape
     group, member = lax.axis_index("dp"), lax.axis_index("expert")
-    me = jnp.reshape(group, (1,))
     rows = groups * chips * ROWS
-    chip = jnp.reshape(member // 2, (1,))
 
     *sent, picks = call(
         functools.partial(route_kernel, groups, experts),
         [shape((2 * ROWS * experts, depth))] * groups + [shape((experts, ROWS, count), F32)],
-        (me,),
+        (),
         (live_tokens.reshape(1, 1), replica_plan),
         hbm=(expert_ids.T, route_weight.T, tokens, cotangent),
         scratch=[
@@ -327,7 +332,7 @@
     gate_up, down, packed = call(
         weights_kernel,
         [shape((depth, 2 * hid)), shape((hid, depth)), shape((tall, 2 * hid))],
-        (me * depth, scale_gate.T, scale_up.T, scale_down),
+        (scale_gate.T, scale_up.T, scale_down),
         (w_gate, w_up, w_down),
         after=(parts[1],),
         flops=6 * depth * hid,
@@ -349,29 +354,29 @@
     (act,) = call(
         functools.partial(act_kernel, groups, chips),
         [shape((chips * ROWS, 6 * hid))],
-        (chip,),
+        (),
         summands,
         scratch=[pltpu.VMEM((chips, ROWS, 6 * hid), F32)],
         flops=40 * chips * ROWS * hid,
         name="activations",
     )
     acts = [act] + [swap(act, "dp", k) for k in range(1, groups)]
+    (act_out,) = call(
+        functools.partial(share_kernel, groups),
+        [shape((rows, 3 * hid))],
+        (),
+        acts,
+        name="share",
+    )
+    act_other = swap(act_out, "expert", 1)
     (dx,) = call(
         functools.partial(dx_kernel, groups, chips),
         [shape((groups, chips * ROWS, depth))],
-        (me,),
+        (),
         (*acts, gate_up, other),
+        after=(act_out,),
         flops=8 * rows * depth * hid,
         name="dx",
-    )
-    act_own, act_out = call(
-        functools.partial(share_kernel, groups, chips),
-        [shape((rows, 3 * hid))] * 2,
-        (chip,),
-        acts,
-        after=(dx,),
-        scratch=[pltpu.VMEM((groups * chips, ROWS, 3 * hid), F32)],
-        name="share",
     )
     dx = dx.reshape(groups * chips, ROWS, depth)
     same_core = [
@@ -380,12 +385,12 @@
     returned = lax.all_to_all(
         dx, ("dp", "expert"), split_axis=0, concat_axis=0, axis_index_groups=same_core, tiled=True
     )
-    act_other = swap(act_out, "expert", 1)
     *grads, done = call(
-        grads_kernel,
+        functools.partial(grads_kernel, groups, chips),
         [shape((depth, hid)), shape((depth, hid)), shape((hid, depth)), shape((8, BLOCK), F32)],
         (),
-        (own_rows, other_rows, act_own, act_other),
+        (own_rows, other_rows, *acts, act_other),
+        scratch=[pltpu.VMEM((2, groups * chips, ROWS, 3 * hid), F32)],
         flops=12 * rows * depth * hid,
         name="gradients",
     )

time: 58.8 us -> 58.2 us (0.990)
  waiting for transfers between devices: 22.3 us -> 25.1 us
  local copies, waits for them, and re-layouts: 2.59 us -> 0.81 us
  Pallas kernels: 10.2 us -> 8.56 us
    all_to_all x1, waiting for transfers between devices: 2.67 us -> 5.47 us  [on_device(): lax.all_to_all(dx, ('dp', 'expert'), split_axis=0, concat_axis=0, axis_in...]
    unnamed x31 -> x23, local copies, waits for them, and re-layouts: 2.58 us -> 0.8 us
    pallas_call x8, Pallas kernels: 10.2 us -> 8.56 us  [call(): pl.pallas_call(body, out_shape=outs, in_specs=[pl.BlockSpec(memory_space=...]
  transfers between devices with their start and end apart: 16 -> 16, of which waited for: 12 -> 12; matrix products, arithmetic and copies ran while one was open for 1% -> 1% of each run, Pallas kernels for 8% -> 7%
where the time goes in v5:
time: 58.2 us; the launch traced here: 57.8 us
  waiting for transfers between devices  25.1 us (43%)
  starting transfers between devices  21.2 us (36%)
  Pallas kernels  8.56 us (15%)
  between operations  2.21 us (4%)
  local copies, waits for them, and re-layouts  0.81 us (1%)
    ppermute x15, waiting for transfers between devices, swap(): lax.ppermute(x, axis, [(i, i ^ k) for i in range(lax.axis_size(axis))])  19.6 us
    ppermute x15, starting transfers between devices, swap(): lax.ppermute(x, axis, [(i, i ^ k) for i in range(lax.axis_size(axis))])  16.2 us
    pallas_call x8, Pallas kernels, call(): pl.pallas_call(body, out_shape=outs, in_specs=[pl.BlockSpec(memory_space=...  8.56 us
    all_to_all x1, waiting for transfers between devices, on_device(): lax.all_to_all(dx, ('dp', 'expert'), split_axis=0, concat_axis=0, axis_in...  5.47 us
    all_to_all x1, starting transfers between devices, on_device(): lax.all_to_all(dx, ('dp', 'expert'), split_axis=0, concat_axis=0, axis_in...  4.92 us
  transfers between devices with their start and end apart: 16, of which 12 were waited for; matrix products, arithmetic and copies ran while one was open for 1% of the time, Pallas kernels for 7%

profile of v5, /device:TPU:0, one launch (start us, length us, event | category | flops | bytes accessed | tf_op | source)
XLA Modules:
  0.0 57.8 jit_solution(3181076251591305915)
XLA Ops:
  0.6 0.0 copy-start.6
  0.6 0.0 copy-start.5
  0.7 0.0 copy-start.4
  0.7 0.0 copy-start.2
  0.7 0.0 copy-start.1
  0.7 0.0 copy-start
  2.1 2.6 %route.1 = (bf16[16,896]{1,0:T(8,128)(2,1)}, bf16[16,896]{1,0:T(8,128)(2,1)}, bf16[16,896]{1,0:T(8,128)(2,1)}, bf16[16,896]{1,0:T(8,128)(2,1)}, f32[1,8,128]{2,1,0:T(8,128)}) custom-call(s32[8,128]{1,0:T(8,128)} %bitcast.9, f32[8,128]{1,0:T(8,128)} %bitcast.10, bf16[128,3584]{1,0:T(8,128)(2,1)} %refs_2_.2, bf16[128,3584]{1,0:T(8,128)(2,1)} %refs_3_.1, ...), custom_call_target="tpu_custom_call" | custom-call | flops 14680064 | bytes 1961992 | tf_op jit(solution)/shard_map/route/pallas_call | solution.py:37
  4.7 0.0 copy-start.7
  4.7 3.0 %collective-permute-start = (bf16[16,896]{1,0:T(8,128)(2,1)}, bf16[16,896]{1,0:T(8,128)(2,1)S(1)}, u32[]{:S(2)}, u32[]{:S(2)}) collective-permute-start(bf16[16,896]{1,0:T(8,128)(2,1)} %get-tuple-element.22), channel_id=1, source_target_pairs={{0,8},{8,0},{16,24},{24,16},{1,9},{9,1},{17,25},{25,17},{2,10},{10... | collective-permute-start | bytes 86024 | tf_op jit(solution)/shard_map/ppermute | solution.py:64
  7.7 1.5 %collective-permute-start.1 = (bf16[16,896]{1,0:T(8,128)(2,1)}, bf16[16,896]{1,0:T(8,128)(2,1)S(1)}, u32[]{:S(2)}, u32[]{:S(2)}) collective-permute-start(bf16[16,896]{1,0:T(8,128)(2,1)} %get-tuple-element.23), channel_id=1, source_target_pairs={{0,16},{8,24},{16,0},{24,8},{1,17},{9,25},{17,1},{25,9},{2,18},{10... | collective-permute-start | bytes 86024 | tf_op jit(solution)/shard_map/ppermute | solution.py:64
  9.2 0.0 collective-permute-start.2
  9.3 0.7 %constant_dynamic-update-slice_fusion.7 = bf16[64,896]{1,0:T(8,128)(2,1)S(1)} fusion(bf16[16,896]{1,0:T(8,128)(2,1)} %get-tuple-element.21), kind=kLoop, calls=%fused_computation.7 | loop fusion | bytes 28672
  10.0 0.0 collective-permute-done.refs_3_
  10.0 0.0 copy-done.5
  10.0 1.0 %weights.1 = (bf16[896,512]{1,0:T(8,128)(2,1)S(1)}, bf16[256,896]{1,0:T(8,128)(2,1)S(1)}, bf16[1408,512]{1,0:T(8,128)(2,1)S(1)}) custom-call(f32[2,28]{1,0:T(2,128)S(1)} %bitcast.7, f32[2,28]{1,0:T(2,128)S(1)} %bitcast.8, f32[2,28]{1,0:T(2,128)S(1)} %copy-done.6, bf16[16,896]{1,0:T(8,128)(2,1)S(1)} %collective-permute-done.refs_3_, ...), custom_call_target="tpu_custom_call" | custom-call | flops 1376256 | bytes 4194304 | tf_op jit(solution)/shard_map/weights/pallas_call | solution.py:37
  11.1 0.1 collective-permute-start.6
  11.2 0.6 %collective-permute-done.1 = bf16[16,896]{1,0:T(8,128)(2,1)S(1)} collective-permute-done((bf16[16,896]{1,0:T(8,128)(2,1)}, bf16[16,896]{1,0:T(8,128)(2,1)S(1)}, u32[]{:S(2)}, u32[]{:S(2)}) %collective-permute-start.1) | collective-permute-done | bytes 28704 | tf_op jit(solution)/shard_map/ppermute | solution.py:64
  11.8 2.4 %collective-permute-done.2 = bf16[16,896]{1,0:T(8,128)(2,1)S(1)} collective-permute-done((bf16[16,896]{1,0:T(8,128)(2,1)}, bf16[16,896]{1,0:T(8,128)(2,1)S(1)}, u32[]{:S(2)}, u32[]{:S(2)}) %collective-permute-start.2) | collective-permute-done | bytes 28704 | tf_op jit(solution)/shard_map/ppermute | solution.py:64
  14.3 3.7 %collective-permute-start.5 = (bf16[64,896]{1,0:T(8,128)(2,1)S(1)}, bf16[64,896]{1,0:T(8,128)(2,1)S(1)}, u32[]{:S(2)}, u32[]{:S(2)}) collective-permute-start(bf16[64,896]{1,0:T(8,128)(2,1)S(1)} %constant_dynamic-update-slice_fusion.refs_0_), channel_id=1, source_target_pairs={{0,6},{1,7},{2,4},{3,5},{4,2},{5,3},{6,0},{7,1},{8,14},{9,15},{10,... | collective-permute-start | bytes 344072 | tf_op jit(solution)/shard_map/ppermute | solution.py:64
  17.9 0.0 collective-permute-start.4
  17.9 0.8 %collective-permute-start.3 = (bf16[64,896]{1,0:T(8,128)(2,1)S(1)}, bf16[64,896]{1,0:T(8,128)(2,1)S(1)}, u32[]{:S(2)}, u32[]{:S(2)}) collective-permute-start(bf16[64,896]{1,0:T(8,128)(2,1)S(1)} %constant_dynamic-update-slice_fusion.refs_0_), channel_id=1, source_target_pairs={{0,2},{1,3},{2,0},{3,1},{4,6},{5,7},{6,4},{7,5},{8,10},{9,11},{10,... | collective-permute-start | bytes 344072 | tf_op jit(solution)/shard_map/ppermute | solution.py:64
  18.7 2.7 %collective-permute-done.5.refs_3_ = bf16[64,896]{1,0:T(8,128)(2,1)S(1)} collective-permute-done((bf16[64,896]{1,0:T(8,128)(2,1)S(1)}, bf16[64,896]{1,0:T(8,128)(2,1)S(1)}, u32[]{:S(2)}, u32[]{:S(2)}) %collective-permute-start.5) | collective-permute-done | bytes 114720 | tf_op jit(solution)/shard_map/ppermute | solution.py:64
  21.4 4.5 %collective-permute-done.4.refs_2_ = bf16[64,896]{1,0:T(8,128)(2,1)S(1)} collective-permute-done((bf16[64,896]{1,0:T(8,128)(2,1)S(1)}, bf16[64,896]{1,0:T(8,128)(2,1)S(1)}, u32[]{:S(2)}, u32[]{:S(2)}) %collective-permute-start.4) | collective-permute-done | bytes 114720 | tf_op jit(solution)/shard_map/ppermute | solution.py:64
  25.9 0.0 collective-permute-done.3.refs_1_
  25.9 0.0 collective-permute-done.6.refs_6_
  25.9 0.7 %partial.1 = (f32[32,1536]{1,0:T(8,128)S(1)}, bf16[32,1536]{1,0:T(8,128)(2,1)S(1)}, bf16[32,1536]{1,0:T(8,128)(2,1)S(1)}, bf16[32,1536]{1,0:T(8,128)(2,1)S(1)}, bf16[256,896]{1,0:T(8,128)(2,1)S(1)}) custom-call(bf16[64,896]{1,0:T(8,128)(2,1)S(1)} %constant_dynamic-update-slice_fusion.refs_0_, bf16[64,896]{1,0:T(8,128)(2,1)S(1)} %collective-permute-done.3.refs_1_, ...), custom_call_target="tpu_custom_call" | custom-call | flops 352321536 | bytes 4227072 | tf_op jit(solution)/shard_map/partial/pallas_call | solution.py:37
  26.6 1.4 %collective-permute-start.7 = (bf16[32,1536]{1,0:T(8,128)(2,1)S(1)}, bf16[32,1536]{1,0:T(8,128)(2,1)S(1)}, u32[]{:S(2)}, u32[]{:S(2)}) collective-permute-start(bf16[32,1536]{1,0:T(8,128)(2,1)S(1)} %get-tuple-element.29), channel_id=1, source_target_pairs={{0,8},{8,0},{16,24},{24,16},{1,9},{9,1},{17,25},{25,17},{2,10},{10... | collective-permute-start | bytes 294920 | tf_op jit(solution)/shard_map/ppermute | solution.py:64
  28.0 1.5 %collective-permute-start.8 = (bf16[32,1536]{1,0:T(8,128)(2,1)S(1)}, bf16[32,1536]{1,0:T(8,128)(2,1)S(1)}, u32[]{:S(2)}, u32[]{:S(2)}) collective-permute-start(bf16[32,1536]{1,0:T(8,128)(2,1)S(1)} %get-tuple-element.30), channel_id=1, source_target_pairs={{0,16},{8,24},{16,0},{24,8},{1,17},{9,25},{17,1},{25,9},{2,18},{10... | collective-permute-start | bytes 294920 | tf_op jit(solution)/shard_map/ppermute | solution.py:64
  29.5 0.7 %collective-permute-start.9 = (bf16[32,1536]{1,0:T(8,128)(2,1)S(1)}, bf16[32,1536]{1,0:T(8,128)(2,1)S(1)}, u32[]{:S(2)}, u32[]{:S(2)}) collective-permute-start(bf16[32,1536]{1,0:T(8,128)(2,1)S(1)} %get-tuple-element.31), channel_id=1, source_target_pairs={{0,24},{8,16},{16,8},{24,0},{1,25},{9,17},{17,9},{25,1},{2,26},{10... | collective-permute-start | bytes 294920 | tf_op jit(solution)/shard_map/ppermute | solution.py:64
  30.2 1.8 %collective-permute-done.7.refs_1_ = bf16[32,1536]{1,0:T(8,128)(2,1)S(1)} collective-permute-done((bf16[32,1536]{1,0:T(8,128)(2,1)S(1)}, bf16[32,1536]{1,0:T(8,128)(2,1)S(1)}, u32[]{:S(2)}, u32[]{:S(2)}) %collective-permute-start.7) | collective-permute-done | bytes 98336 | tf_op jit(solution)/shard_map/ppermute | solution.py:64
  32.0 1.6 %collective-permute-done.8.refs_2_ = bf16[32,1536]{1,0:T(8,128)(2,1)S(1)} collective-permute-done((bf16[32,1536]{1,0:T(8,128)(2,1)S(1)}, bf16[32,1536]{1,0:T(8,128)(2,1)S(1)}, u32[]{:S(2)}, u32[]{:S(2)}) %collective-permute-start.8) | collective-permute-done | bytes 98336 | tf_op jit(solution)/shard_map/ppermute | solution.py:64
  33.6 1.4 %collective-permute-done.9.refs_3_ = bf16[32,1536]{1,0:T(8,128)(2,1)S(1)} collective-permute-done((bf16[32,1536]{1,0:T(8,128)(2,1)S(1)}, bf16[32,1536]{1,0:T(8,128)(2,1)S(1)}, u32[]{:S(2)}, u32[]{:S(2)}) %collective-permute-start.9) | collective-permute-done | bytes 98336 | tf_op jit(solution)/shard_map/ppermute | solution.py:64
  35.0 0.1 activations.1.refs_0_.refs_1_.refs_2_
  35.1 0.7 %collective-permute-start.12 = (bf16[32,1536]{1,0:T(8,128)(2,1)S(1)}, bf16[32,1536]{1,0:T(8,128)(2,1)S(1)}, u32[]{:S(2)}, u32[]{:S(2)}) collective-permute-start(bf16[32,1536]{1,0:T(8,128)(2,1)S(1)} %activations.1.refs_0_.refs_1_.refs_2_), channel_id=1, source_target_pairs={{0,24},{8,16},{16,8},{24,0},{1,25},{9,17},{17,9},{25,1},{2,26},{10... | collective-permute-start | bytes 294920 | tf_op jit(solution)/shard_map/ppermute | solution.py:64
  35.8 1.3 %collective-permute-start.11 = (bf16[32,1536]{1,0:T(8,128)(2,1)S(1)}, bf16[32,1536]{1,0:T(8,128)(2,1)S(1)}, u32[]{:S(2)}, u32[]{:S(2)}) collective-permute-start(bf16[32,1536]{1,0:T(8,128)(2,1)S(1)} %activations.1.refs_0_.refs_1_.refs_2_), channel_id=1, source_target_pairs={{0,16},{8,24},{16,0},{24,8},{1,17},{9,25},{17,1},{25,9},{2,18},{10... | collective-permute-start | bytes 294920 | tf_op jit(solution)/shard_map/ppermute | solution.py:64
  37.2 1.5 %collective-permute-start.10 = (bf16[32,1536]{1,0:T(8,128)(2,1)S(1)}, bf16[32,1536]{1,0:T(8,128)(2,1)S(1)}, u32[]{:S(2)}, u32[]{:S(2)}) collective-permute-start(bf16[32,1536]{1,0:T(8,128)(2,1)S(1)} %activations.1.refs_0_.refs_1_.refs_2_), channel_id=1, source_target_pairs={{0,8},{8,0},{16,24},{24,16},{1,9},{9,1},{17,25},{25,17},{2,10},{10... | collective-permute-start | bytes 294920 | tf_op jit(solution)/shard_map/ppermute | solution.py:64
  38.7 0.0 collective-permute-start.13
  38.7 2.1 %collective-permute-done.12.refs_3_.refs_4_.refs_5_ = bf16[32,1536]{1,0:T(8,128)(2,1)S(1)} collective-permute-done((bf16[32,1536]{1,0:T(8,128)(2,1)S(1)}, bf16[32,1536]{1,0:T(8,128)(2,1)S(1)}, u32[]{:S(2)}, u32[]{:S(2)}) %collective-permute-start.12) | collective-permute-done | bytes 98336 | tf_op jit(solution)/shard_map/ppermute | solution.py:64
  40.8 0.7 %collective-permute-done.11.refs_2_.refs_3_.refs_4_ = bf16[32,1536]{1,0:T(8,128)(2,1)S(1)} collective-permute-done((bf16[32,1536]{1,0:T(8,128)(2,1)S(1)}, bf16[32,1536]{1,0:T(8,128)(2,1)S(1)}, u32[]{:S(2)}, u32[]{:S(2)}) %collective-permute-start.11) | collective-permute-done | bytes 98336 | tf_op jit(solution)/shard_map/ppermute | solution.py:64
  41.5 0.3 collective-permute-done.10.refs_1_.refs_2_.refs_3_
  41.8 1.4 %dx.1 = bf16[4,32,896]{2,1,0:T(8,128)(2,1)} custom-call(bf16[128,768]{1,0:T(8,128)(2,1)S(1)} %share.1.refs_0_, bf16[32,1536]{1,0:T(8,128)(2,1)S(1)} %activations.1.refs_0_.refs_1_.refs_2_, bf16[32,1536]{1,0:T(8,128)(2,1)S(1)} %collective-permute-done.10.refs_1_.refs_2_.refs_3_, bf16[32,1536]{1,0:T(8,128)(2,1)S(1)} %collective-permute-done.11.refs_2_.refs_3_.refs_4_, ...), custom_call_target="tpu_custom_call" | custom-call | flops 234881024 | bytes 2981888 | tf_op jit(solution)/shard_map/dx/pallas_call | solution.py:37
  43.2 4.9 %all-to-all-start = ((bf16[16,8,896]{2,1,0:T(8,128)(2,1)}), bf16[16,8,896]{2,1,0:T(8,128)(2,1)S(1)}, u32[]{:S(2)}, u32[]{:S(2)}) async-start(bf16[16,8,896]{2,1,0:T(8,128)(2,1)} %bitcast.5), calls=%async_computation | async-start | bytes 458752 | tf_op jit(solution)/shard_map/all_to_all | solution.py:385
  48.1 0.1 collective-permute-start.14
  48.2 1.4 %collective-permute-done.14.refs_6_ = bf16[128,768]{1,0:T(8,128)(2,1)S(1)} collective-permute-done((bf16[128,768]{1,0:T(8,128)(2,1)S(1)}, bf16[128,768]{1,0:T(8,128)(2,1)S(1)}, u32[]{:S(2)}, u32[]{:S(2)}) %collective-permute-start.14) | collective-permute-done | bytes 196640 | tf_op jit(solution)/shard_map/ppermute | solution.py:64
  49.6 0.0 collective-permute-done.13.refs_1_
  49.6 1.5 %gradients.1 = (bf16[896,256]{1,0:T(8,128)(2,1)}, bf16[896,256]{1,0:T(8,128)(2,1)}, bf16[256,896]{1,0:T(8,128)(2,1)}, f32[8,128]{1,0:T(8,128)S(1)}) custom-call(bf16[256,896]{1,0:T(8,128)(2,1)S(1)} %get-tuple-element.33.refs_0_, bf16[256,896]{1,0:T(8,128)(2,1)S(1)} %collective-permute-done.13.refs_1_, ...), custom_call_target="tpu_custom_call" | custom-call | flops 352321536 | bytes 2887680 | tf_op jit(solution)/shard_map/gradients/pallas_call | solution.py:37
  51.2 5.5 %all-to-all-done.refs_0_ = bf16[16,8,896]{2,1,0:T(8,128)(2,1)S(1)} async-done(((bf16[16,8,896]{2,1,0:T(8,128)(2,1)}), bf16[16,8,896]{2,1,0:T(8,128)(2,1)S(1)}, u32[]{:S(2)}, u32[]{:S(2)}) %all-to-all-start) | async-done | bytes 229408 | tf_op jit(solution)/shard_map/all_to_all | solution.py:385
  56.6 1.2 %place.1 = bf16[128,3584]{1,0:T(8,128)(2,1)} custom-call(bf16[16,8,896]{2,1,0:T(8,128)(2,1)S(1)} %all-to-all-done.refs_0_, f32[1,8,128]{2,1,0:T(8,128)S(1)} %copy-done.3, f32[8,128]{1,0:T(8,128)S(1)} %get-tuple-element.34.refs_2_), custom_call_target="tpu_custom_call" | custom-call | flops 7340032 | bytes 1155072 | tf_op jit(solution)/shard_map/place/pallas_call | solution.py:37
  (16 shorter events, 0.1 us)
Async XLA Ops:
  0.6 9.3 %copy-start.6 = (f32[2,28]{1,0:T(2,128)S(1)}, f32[2,28]{1,0:T(2,128)}, u32[]{:S(2)}) copy-start(f32[2,28]{1,0:T(2,128)} %refs_2_.3) | copy-start | bytes 676
  0.6 9.3 %copy-start.5 = (f32[28,2]{0,1:T(2,128)S(1)}, f32[28,2]{0,1:T(2,128)}, u32[]{:S(2)}) copy-start(f32[28,2]{0,1:T(2,128)} %param.22) | copy-start | bytes 676
  0.7 9.3 %copy-start.4 = (f32[28,2]{0,1:T(2,128)S(1)}, f32[28,2]{0,1:T(2,128)}, u32[]{:S(2)}) copy-start(f32[28,2]{0,1:T(2,128)} %param.21) | copy-start | bytes 676
  0.7 9.3 %copy-start.2 = (bf16[256,896]{1,0:T(8,128)(2,1)S(1)}, bf16[256,896]{1,0:T(8,128)(2,1)}, u32[]{:S(2)}) copy-start(bf16[256,896]{1,0:T(8,128)(2,1)} %refs_6_.1) | copy-start | bytes 1376260
  0.7 9.3 %copy-start.1 = (bf16[896,256]{1,0:T(8,128)(2,1)S(1)}, bf16[896,256]{1,0:T(8,128)(2,1)}, u32[]{:S(2)}) copy-start(bf16[896,256]{1,0:T(8,128)(2,1)} %refs_5_.2) | copy-start | bytes 1376260
  0.7 9.3 %copy-start = (bf16[896,256]{1,0:T(8,128)(2,1)S(1)}, bf16[896,256]{1,0:T(8,128)(2,1)}, u32[]{:S(2)}) copy-start(bf16[896,256]{1,0:T(8,128)(2,1)} %refs_4_.1) | copy-start | bytes 1376260
  4.7 9.5 %copy-start.7 = (bf16[16,896]{1,0:T(8,128)(2,1)S(1)}, bf16[16,896]{1,0:T(8,128)(2,1)}, u32[]{:S(2)}) copy-start(bf16[16,896]{1,0:T(8,128)(2,1)} %get-tuple-element.21) | copy-start | bytes 86020
  4.7 5.3 %collective-permute-start = (bf16[16,896]{1,0:T(8,128)(2,1)}, bf16[16,896]{1,0:T(8,128)(2,1)S(1)}, u32[]{:S(2)}, u32[]{:S(2)}) collective-permute-start(bf16[16,896]{1,0:T(8,128)(2,1)} %get-tuple-element.22), channel_id=1, source_target_pairs={{0,8},{8,0},{16,24},{24,16},{1,9},{9,1},{17,25},{25,17},{2,10},{10... | collective-permute-start | bytes 86024 | tf_op jit(solution)/shard_map/ppermute | solution.py:64
  7.7 4.1 %collective-permute-start.1 = (bf16[16,896]{1,0:T(8,128)(2,1)}, bf16[16,896]{1,0:T(8,128)(2,1)S(1)}, u32[]{:S(2)}, u32[]{:S(2)}) collective-permute-start(bf16[16,896]{1,0:T(8,128)(2,1)} %get-tuple-element.23), channel_id=1, source_target_pairs={{0,16},{8,24},{16,0},{24,8},{1,17},{9,25},{17,1},{25,9},{2,18},{10... | collective-permute-start | bytes 86024 | tf_op jit(solution)/shard_map/ppermute | solution.py:64
  9.2 5.0 %collective-permute-start.2 = (bf16[16,896]{1,0:T(8,128)(2,1)}, bf16[16,896]{1,0:T(8,128)(2,1)S(1)}, u32[]{:S(2)}, u32[]{:S(2)}) collective-permute-start(bf16[16,896]{1,0:T(8,128)(2,1)} %get-tuple-element.24), channel_id=1, source_target_pairs={{0,24},{8,16},{16,8},{24,0},{1,25},{9,17},{17,9},{25,1},{2,26},{10... | collective-permute-start | bytes 86024 | tf_op jit(solution)/shard_map/ppermute | solution.py:64
  11.1 14.8 %collective-permute-start.6 = (bf16[1408,512]{1,0:T(8,128)(2,1)S(1)}, bf16[1408,512]{1,0:T(8,128)(2,1)S(1)}, u32[]{:S(2)}, u32[]{:S(2)}) collective-permute-start(bf16[1408,512]{1,0:T(8,128)(2,1)S(1)} %get-tuple-element.27), channel_id=1, source_target_pairs={{0,1},{1,0},{2,3},{3,2},{4,5},{5,4},{6,7},{7,6},{8,9},{9,8},{10,11... | collective-permute-start | bytes 4325384 | tf_op jit(solution)/shard_map/ppermute | solution.py:64
  14.3 7.2 %collective-permute-start.5 = (bf16[64,896]{1,0:T(8,128)(2,1)S(1)}, bf16[64,896]{1,0:T(8,128)(2,1)S(1)}, u32[]{:S(2)}, u32[]{:S(2)}) collective-permute-start(bf16[64,896]{1,0:T(8,128)(2,1)S(1)} %constant_dynamic-update-slice_fusion.refs_0_), channel_id=1, source_target_pairs={{0,6},{1,7},{2,4},{3,5},{4,2},{5,3},{6,0},{7,1},{8,14},{9,15},{10,... | collective-permute-start | bytes 344072 | tf_op jit(solution)/shard_map/ppermute | solution.py:64
  17.9 8.0 %collective-permute-start.4 = (bf16[64,896]{1,0:T(8,128)(2,1)S(1)}, bf16[64,896]{1,0:T(8,128)(2,1)S(1)}, u32[]{:S(2)}, u32[]{:S(2)}) collective-permute-start(bf16[64,896]{1,0:T(8,128)(2,1)S(1)} %constant_dynamic-update-slice_fusion.refs_0_), channel_id=1, source_target_pairs={{0,4},{1,5},{2,6},{3,7},{4,0},{5,1},{6,2},{7,3},{8,12},{9,13},{10,... | collective-permute-start | bytes 344072 | tf_op jit(solution)/shard_map/ppermute | solution.py:64
  17.9 8.0 %collective-permute-start.3 = (bf16[64,896]{1,0:T(8,128)(2,1)S(1)}, bf16[64,896]{1,0:T(8,128)(2,1)S(1)}, u32[]{:S(2)}, u32[]{:S(2)}) collective-permute-start(bf16[64,896]{1,0:T(8,128)(2,1)S(1)} %constant_dynamic-update-slice_fusion.refs_0_), channel_id=1, source_target_pairs={{0,2},{1,3},{2,0},{3,1},{4,6},{5,7},{6,4},{7,5},{8,10},{9,11},{10,... | collective-permute-start | bytes 344072 | tf_op jit(solution)/shard_map/ppermute | solution.py:64
  26.6 5.4 %collective-permute-start.7 = (bf16[32,1536]{1,0:T(8,128)(2,1)S(1)}, bf16[32,1536]{1,0:T(8,128)(2,1)S(1)}, u32[]{:S(2)}, u32[]{:S(2)}) collective-permute-start(bf16[32,1536]{1,0:T(8,128)(2,1)S(1)} %get-tuple-element.29), channel_id=1, source_target_pairs={{0,8},{8,0},{16,24},{24,16},{1,9},{9,1},{17,25},{25,17},{2,10},{10... | collective-permute-start | bytes 294920 | tf_op jit(solution)/shard_map/ppermute | solution.py:64
  28.0 5.7 %collective-permute-start.8 = (bf16[32,1536]{1,0:T(8,128)(2,1)S(1)}, bf16[32,1536]{1,0:T(8,128)(2,1)S(1)}, u32[]{:S(2)}, u32[]{:S(2)}) collective-permute-start(bf16[32,1536]{1,0:T(8,128)(2,1)S(1)} %get-tuple-element.30), channel_id=1, source_target_pairs={{0,16},{8,24},{16,0},{24,8},{1,17},{9,25},{17,1},{25,9},{2,18},{10... | collective-permute-start | bytes 294920 | tf_op jit(solution)/shard_map/ppermute | solution.py:64
  29.5 5.5 %collective-permute-start.9 = (bf16[32,1536]{1,0:T(8,128)(2,1)S(1)}, bf16[32,1536]{1,0:T(8,128)(2,1)S(1)}, u32[]{:S(2)}, u32[]{:S(2)}) collective-permute-start(bf16[32,1536]{1,0:T(8,128)(2,1)S(1)} %get-tuple-element.31), channel_id=1, source_target_pairs={{0,24},{8,16},{16,8},{24,0},{1,25},{9,17},{17,9},{25,1},{2,26},{10... | collective-permute-start | bytes 294920 | tf_op jit(solution)/shard_map/ppermute | solution.py:64
  35.1 5.7 %collective-permute-start.12 = (bf16[32,1536]{1,0:T(8,128)(2,1)S(1)}, bf16[32,1536]{1,0:T(8,128)(2,1)S(1)}, u32[]{:S(2)}, u32[]{:S(2)}) collective-permute-start(bf16[32,1536]{1,0:T(8,128)(2,1)S(1)} %activations.1.refs_0_.refs_1_.refs_2_), channel_id=1, source_target_pairs={{0,24},{8,16},{16,8},{24,0},{1,25},{9,17},{17,9},{25,1},{2,26},{10... | collective-permute-start | bytes 294920 | tf_op jit(solution)/shard_map/ppermute | solution.py:64
  35.8 5.7 %collective-permute-start.11 = (bf16[32,1536]{1,0:T(8,128)(2,1)S(1)}, bf16[32,1536]{1,0:T(8,128)(2,1)S(1)}, u32[]{:S(2)}, u32[]{:S(2)}) collective-permute-start(bf16[32,1536]{1,0:T(8,128)(2,1)S(1)} %activations.1.refs_0_.refs_1_.refs_2_), channel_id=1, source_target_pairs={{0,16},{8,24},{16,0},{24,8},{1,17},{9,25},{17,1},{25,9},{2,18},{10... | collective-permute-start | bytes 294920 | tf_op jit(solution)/shard_map/ppermute | solution.py:64
  37.2 4.6 %collective-permute-start.10 = (bf16[32,1536]{1,0:T(8,128)(2,1)S(1)}, bf16[32,1536]{1,0:T(8,128)(2,1)S(1)}, u32[]{:S(2)}, u32[]{:S(2)}) collective-permute-start(bf16[32,1536]{1,0:T(8,128)(2,1)S(1)} %activations.1.refs_0_.refs_1_.refs_2_), channel_id=1, source_target_pairs={{0,8},{8,0},{16,24},{24,16},{1,9},{9,1},{17,25},{25,17},{2,10},{10... | collective-permute-start | bytes 294920 | tf_op jit(solution)/shard_map/ppermute | solution.py:64
  38.7 11.0 %collective-permute-start.13 = (bf16[256,896]{1,0:T(8,128)(2,1)S(1)}, bf16[256,896]{1,0:T(8,128)(2,1)S(1)}, u32[]{:S(2)}, u32[]{:S(2)}) collective-permute-start(bf16[256,896]{1,0:T(8,128)(2,1)S(1)} %get-tuple-element.33.refs_0_), channel_id=1, source_target_pairs={{0,1},{1,0},{2,3},{3,2},{4,5},{5,4},{6,7},{7,6},{8,9},{9,8},{10,11... | collective-permute-start | bytes 1376264 | tf_op jit(solution)/shard_map/ppermute | solution.py:64
  43.2 13.5 %copy-start.3 = (f32[1,8,128]{2,1,0:T(8,128)S(1)}, f32[1,8,128]{2,1,0:T(8,128)}, u32[]{:S(2)}) copy-start(f32[1,8,128]{2,1,0:T(8,128)} %get-tuple-element.32.refs_1_) | copy-start | bytes 12292
  43.2 13.4 %all-to-all-start = ((bf16[16,8,896]{2,1,0:T(8,128)(2,1)}), bf16[16,8,896]{2,1,0:T(8,128)(2,1)S(1)}, u32[]{:S(2)}, u32[]{:S(2)}) async-start(bf16[16,8,896]{2,1,0:T(8,128)(2,1)} %bitcast.5), calls=%async_computation | async-start | bytes 458752 | tf_op jit(solution)/shard_map/all_to_all | solution.py:385
  48.1 1.5 %collective-permute-start.14 = (bf16[128,768]{1,0:T(8,128)(2,1)S(1)}, bf16[128,768]{1,0:T(8,128)(2,1)S(1)}, u32[]{:S(2)}, u32[]{:S(2)}) collective-permute-start(bf16[128,768]{1,0:T(8,128)(2,1)S(1)} %share.1.refs_0_), channel_id=1, source_target_pairs={{0,1},{1,0},{2,3},{3,2},{4,5},{5,4},{6,7},{7,6},{8,9},{9,8},{10,11... | collective-permute-start | bytes 589832 | tf_op jit(solution)/shard_map/ppermute | solution.py:64

commit v6 on v5

--- a/solution.py
+++ b/solution.py
@@ -16,7 +16,7 @@
 BF16 = jnp.bfloat16
 F32 = jnp.float32
 VMEM_BYTES = 40 * 1024 * 1024
-ROUTE_VMEM_BYTES = 61 * 1024 * 1024
+MASKS_FLOPS = 1 << 29
 
 NN = (((1,), (0,)), ((), ()))
 NT = (((1,), (1,)), ((), ()))
@@ -68,40 +68,31 @@
     return value[first : first + count]
 
 
-def route_kernel(groups, experts, ids_in, weight_in, tokens_in, cots_in, live, plan, *rest):
-    outs, picks, scratch = rest[:groups], rest[groups], rest[groups + 1 :]
-    ids, weight, tokens, cots, slices, sems = scratch
-    count, width = tokens.shape
-    depth = width // groups
-    small = fetch((ids_in, weight_in), (ids, weight), sems)
-    large = []
-    if depth % BLOCK == 0:
-        cuts = [(slice(None), pl.ds(i * depth, depth)) for i in range(groups)]
-    else:
-        cuts = [(slice(None), slice(None))]
-    for i, cut in enumerate(cuts):
-        for source, target, sem in ((tokens_in, tokens, 2 + i), (cots_in, cots, 2 + groups + i)):
-            large.append(pltpu.make_async_copy(source.at[cut], target.at[cut], sems.at[sem]))
-            large[-1].start()
-    for copy in small:
-        copy.wait()
+def masks_kernel(live, plan, masks):
+    slot = lax.broadcasted_iota(jnp.int32, (1, masks.shape[1]), 1)
+    masks[0:1, :] = jnp.where(slot < live[0], 1.0, 0.0)
+    for e in range(plan.shape[1]):
+        masks[e + 1 : e + 2, :] = jnp.where((slot % 2 == 1) & (plan[0, e] == 1), 1.0, 0.0)
+
+
+def lists_kernel(experts, masks, ids, weight, picks, columns):
+    count = ids.shape[1]
     lists = experts * ROWS
-    slot = lax.broadcasted_iota(jnp.int32, (1, count), 1)
     line = lax.broadcasted_iota(jnp.int32, (lists, count), 0)
-    alive = slot < live[...]
-    odd = slot % 2 == 1
+    alive = masks[0:1, :]
     listed = jnp.zeros((lists, count), F32)
     weights = jnp.zeros((lists, count), F32)
     for e in range(experts):
         match = ids[...] == e
-        routed = (jnp.sum(jnp.where(match, 1.0, 0.0), axis=0, keepdims=True) > 0.0) & alive
+        routed = jnp.sum(jnp.where(match, 1.0, 0.0), axis=0, keepdims=True)
+        routed = jnp.where(routed > 0.0, alive, 0.0)
         total = jnp.sum(jnp.where(match, weight[...], 0.0), axis=0, keepdims=True)
-        second = odd & (plan[:, e : e + 1] == 1)
-        in_first = jnp.where(routed & ~second, 1.0, 0.0)
-        in_second = jnp.where(routed & second, 1.0, 0.0)
+        second = masks[e + 1 : e + 2, :]
         is_first = (line >= e * ROWS) & (line < e * ROWS + CAP)
         is_second = (line >= e * ROWS + CAP) & (line < (e + 1) * ROWS)
-        listed = jnp.where(is_first, in_first, jnp.where(is_second, in_second, listed))
+        listed = jnp.where(
+            is_first, routed * (1.0 - second), jnp.where(is_second, routed * second, listed)
+        )
         weights = jnp.where(is_first | is_second, total, weights)
     before = lax.broadcasted_iota(jnp.int32, (count, count), 0)
     here = lax.broadcasted_iota(jnp.int32, (count, count), 1)
@@ -112,16 +103,21 @@
     column = jnp.sum(picked * weights, axis=1, keepdims=True)
     for e in range(experts):
         picks[e] = rows_of(picked, e * ROWS)
-    picked = picked.astype(BF16)
+        columns[e] = jnp.broadcast_to(rows_of(column, e * ROWS), columns.shape[1:])
+
+
+def route_kernel(groups, experts, picks, columns, tokens, cots, *rest):
+    outs, slices = rest[:groups], rest[groups]
+    depth = tokens.shape[1] // groups
+    picked = jnp.concatenate([picks[e] for e in range(experts)], axis=0).astype(BF16)
     for s in range(groups):
-        for copy in large[2 * s : 2 * s + 2]:
-            copy.wait()
         cut = slice(s * depth, (s + 1) * depth)
         token_rows = mm(picked, tokens[:, cut], NN)
-        cot_rows = mm(picked, cots[:, cut], NN) * column
+        cot_rows = mm(picked, cots[:, cut], NN)
         parts = []
         for e in range(experts):
-            parts += [rows_of(token_rows, e * ROWS), rows_of(cot_rows, e * ROWS)]
+            weighted = rows_of(cot_rows, e * ROWS) * columns[e][:, :1]
+            parts += [rows_of(token_rows, e * ROWS), weighted]
         slices[s] = jnp.concatenate(parts, axis=0).astype(BF16)
     for k in range(groups):
         outs[k][...] = slices[lax.axis_index("dp") ^ k]
@@ -304,22 +300,29 @@
     group, member = lax.axis_index("dp"), lax.axis_index("expert")
     rows = groups * chips * ROWS
 
-    *sent, picks = call(
+    (masks,) = call(
+        masks_kernel,
+        [shape((experts + 1, count), F32)],
+        (live_tokens, replica_plan),
+        (),
+        flops=MASKS_FLOPS,
+        name="masks",
+    )
+    picks, columns = call(
+        functools.partial(lists_kernel, experts),
+        [shape((experts, ROWS, count), F32), shape((experts, ROWS, BLOCK), F32)],
+        (),
+        (masks, expert_ids.T, route_weight.T),
+        flops=2 * experts * ROWS * count * count,
+        name="lists",
+    )
+    sent = call(
         functools.partial(route_kernel, groups, experts),
-        [shape((2 * ROWS * experts, depth))] * groups + [shape((experts, ROWS, count), F32)],
-        (),
-        (live_tokens.reshape(1, 1), replica_plan),
-        hbm=(expert_ids.T, route_weight.T, tokens, cotangent),
-        scratch=[
-            pltpu.VMEM(expert_ids.shape[::-1], jnp.int32),
-            pltpu.VMEM(route_weight.shape[::-1], F32),
-            pltpu.VMEM(tokens.shape, BF16),
-            pltpu.VMEM(cotangent.shape, BF16),
-            pltpu.VMEM((groups, 2 * ROWS * experts, depth), BF16),
-            pltpu.SemaphoreType.DMA((2 + 2 * groups,)),
-        ],
+        [shape((2 * ROWS * experts, depth))] * groups,
+        (),
+        (picks, columns, tokens, cotangent),
+        scratch=[pltpu.VMEM((groups, 2 * ROWS * experts, depth), BF16)],
         flops=4 * count * experts * ROWS * width,
-        limit=ROUTE_VMEM_BYTES,
         name="route",
     )
     parts = [sent[0]] + [swap(sent[k], "dp", k) for k in range(1, groups)]

time: 58.2 us -> 55.7 us (0.957)
  Pallas kernels: 8.56 us -> 6.59 us
  local copies, waits for them, and re-layouts: 0.81 us -> 0.11 us
    pallas_call x8 -> x10, Pallas kernels: 8.56 us -> 6.59 us  [call(): pl.pallas_call(body, out_shape=outs, in_specs=[pl.BlockSpec(memory_space=...]
    unnamed x23 -> x27, local copies, waits for them, and re-layouts: 0.8 us -> 0.11 us
  transfers between devices with their start and end apart: 16 -> 16, of which waited for: 12 -> 13; matrix products, arithmetic and copies ran while one was open for 1% -> 0% of each run, Pallas kernels for 7% -> 7%
where the time goes in v6:
time: 55.7 us; the launch traced here: 55.5 us
  waiting for transfers between devices  25.5 us (46%)
  starting transfers between devices  21 us (38%)
  Pallas kernels  6.59 us (12%)
  between operations  2.27 us (4%)
    ppermute x15, waiting for transfers between devices, swap(): lax.ppermute(x, axis, [(i, i ^ k) for i in range(lax.axis_size(axis))])  20 us
    ppermute x15, starting transfers between devices, swap(): lax.ppermute(x, axis, [(i, i ^ k) for i in range(lax.axis_size(axis))])  16.2 us
    pallas_call x10, Pallas kernels, call(): pl.pallas_call(body, out_shape=outs, in_specs=[pl.BlockSpec(memory_space=...  6.59 us
    all_to_all x1, waiting for transfers between devices, on_device(): lax.all_to_all(dx, ('dp', 'expert'), split_axis=0, concat_axis=0, axis_in...  5.46 us
    all_to_all x1, starting transfers between devices, on_device(): lax.all_to_all(dx, ('dp', 'expert'), split_axis=0, concat_axis=0, axis_in...  4.78 us
  transfers between devices with their start and end apart: 16, of which 13 were waited for; matrix products, arithmetic and copies ran while one was open for 0% of the time, Pallas kernels for 7%

profile of v6, /device:TPU:0, one launch (start us, length us, event | category | flops | bytes accessed | tf_op | source)
XLA Modules:
  0.0 55.5 jit_solution(15401992786099185613)
XLA Ops:
  2.1 0.0 copy-start.2
  2.1 0.0 copy-start.3
  2.1 0.0 copy-start.4
  2.1 0.0 copy-start.7
  2.2 0.0 copy-start.8
  2.2 0.0 copy-start.9
  2.2 0.2 lists.1
  2.4 0.4 route.1
  2.8 3.0 %collective-permute-start = (bf16[16,896]{1,0:T(8,128)(2,1)S(1)}, bf16[16,896]{1,0:T(8,128)(2,1)S(1)}, u32[]{:S(2)}, u32[]{:S(2)}) collective-permute-start(bf16[16,896]{1,0:T(8,128)(2,1)S(1)} %get-tuple-element.25), channel_id=1, source_target_pairs={{0,8},{8,0},{16,24},{24,16},{1,9},{9,1},{17,25},{25,17},{2,10},{10... | collective-permute-start | bytes 86024 | tf_op jit(solution)/shard_map/ppermute | solution.py:64
  5.8 1.5 %collective-permute-start.1 = (bf16[16,896]{1,0:T(8,128)(2,1)S(1)}, bf16[16,896]{1,0:T(8,128)(2,1)S(1)}, u32[]{:S(2)}, u32[]{:S(2)}) collective-permute-start(bf16[16,896]{1,0:T(8,128)(2,1)S(1)} %get-tuple-element.26), channel_id=1, source_target_pairs={{0,16},{8,24},{16,0},{24,8},{1,17},{9,25},{17,1},{25,9},{2,18},{10... | collective-permute-start | bytes 86024 | tf_op jit(solution)/shard_map/ppermute | solution.py:64
  7.4 0.0 collective-permute-start.2
  7.4 0.3 collective-permute-done.refs_3_
  7.7 0.0 copy-done.7
  7.7 0.0 copy-done.8
  7.7 1.0 %weights.1 = (bf16[896,512]{1,0:T(8,128)(2,1)S(1)}, bf16[256,896]{1,0:T(8,128)(2,1)S(1)}, bf16[1408,512]{1,0:T(8,128)(2,1)S(1)}) custom-call(f32[2,28]{1,0:T(2,128)S(1)} %bitcast.7, f32[2,28]{1,0:T(2,128)S(1)} %bitcast.8, f32[2,28]{1,0:T(2,128)S(1)} %copy-done.9, bf16[16,896]{1,0:T(8,128)(2,1)S(1)} %collective-permute-done.refs_3_, ...), custom_call_target="tpu_custom_call" | custom-call | flops 1376256 | bytes 4194304 | tf_op jit(solution)/shard_map/weights/pallas_call | solution.py:37
  8.8 0.1 collective-permute-start.6
  8.9 0.8 %collective-permute-done.1 = bf16[16,896]{1,0:T(8,128)(2,1)S(1)} collective-permute-done((bf16[16,896]{1,0:T(8,128)(2,1)S(1)}, bf16[16,896]{1,0:T(8,128)(2,1)S(1)}, u32[]{:S(2)}, u32[]{:S(2)}) %collective-permute-start.1) | collective-permute-done | bytes 28704 | tf_op jit(solution)/shard_map/ppermute | solution.py:64
  9.7 2.4 %collective-permute-done.2 = bf16[16,896]{1,0:T(8,128)(2,1)S(1)} collective-permute-done((bf16[16,896]{1,0:T(8,128)(2,1)S(1)}, bf16[16,896]{1,0:T(8,128)(2,1)S(1)}, u32[]{:S(2)}, u32[]{:S(2)}) %collective-permute-start.2) | collective-permute-done | bytes 28704 | tf_op jit(solution)/shard_map/ppermute | solution.py:64
  12.2 3.7 %collective-permute-start.5 = (bf16[64,896]{1,0:T(8,128)(2,1)S(1)}, bf16[64,896]{1,0:T(8,128)(2,1)S(1)}, u32[]{:S(2)}, u32[]{:S(2)}) collective-permute-start(bf16[64,896]{1,0:T(8,128)(2,1)S(1)} %constant_dynamic-update-slice_fusion.refs_0_), channel_id=1, source_target_pairs={{0,6},{1,7},{2,4},{3,5},{4,2},{5,3},{6,0},{7,1},{8,14},{9,15},{10,... | collective-permute-start | bytes 344072 | tf_op jit(solution)/shard_map/ppermute | solution.py:64
  15.8 0.0 collective-permute-start.4
  15.8 0.8 %collective-permute-start.3 = (bf16[64,896]{1,0:T(8,128)(2,1)S(1)}, bf16[64,896]{1,0:T(8,128)(2,1)S(1)}, u32[]{:S(2)}, u32[]{:S(2)}) collective-permute-start(bf16[64,896]{1,0:T(8,128)(2,1)S(1)} %constant_dynamic-update-slice_fusion.refs_0_), channel_id=1, source_target_pairs={{0,2},{1,3},{2,0},{3,1},{4,6},{5,7},{6,4},{7,5},{8,10},{9,11},{10,... | collective-permute-start | bytes 344072 | tf_op jit(solution)/shard_map/ppermute | solution.py:64
  16.6 2.7 %collective-permute-done.5.refs_3_ = bf16[64,896]{1,0:T(8,128)(2,1)S(1)} collective-permute-done((bf16[64,896]{1,0:T(8,128)(2,1)S(1)}, bf16[64,896]{1,0:T(8,128)(2,1)S(1)}, u32[]{:S(2)}, u32[]{:S(2)}) %collective-permute-start.5) | collective-permute-done | bytes 114720 | tf_op jit(solution)/shard_map/ppermute | solution.py:64
  19.3 4.5 %collective-permute-done.4.refs_2_ = bf16[64,896]{1,0:T(8,128)(2,1)S(1)} collective-permute-done((bf16[64,896]{1,0:T(8,128)(2,1)S(1)}, bf16[64,896]{1,0:T(8,128)(2,1)S(1)}, u32[]{:S(2)}, u32[]{:S(2)}) %collective-permute-start.4) | collective-permute-done | bytes 114720 | tf_op jit(solution)/shard_map/ppermute | solution.py:64
  23.8 0.0 collective-permute-done.3.refs_1_
  23.8 0.0 collective-permute-done.6.refs_6_
  23.8 0.7 %partial.1 = (f32[32,1536]{1,0:T(8,128)S(1)}, bf16[32,1536]{1,0:T(8,128)(2,1)S(1)}, bf16[32,1536]{1,0:T(8,128)(2,1)S(1)}, bf16[32,1536]{1,0:T(8,128)(2,1)S(1)}, bf16[256,896]{1,0:T(8,128)(2,1)S(1)}) custom-call(bf16[64,896]{1,0:T(8,128)(2,1)S(1)} %constant_dynamic-update-slice_fusion.refs_0_, bf16[64,896]{1,0:T(8,128)(2,1)S(1)} %collective-permute-done.3.refs_1_, ...), custom_call_target="tpu_custom_call" | custom-call | flops 352321536 | bytes 4227072 | tf_op jit(solution)/shard_map/partial/pallas_call | solution.py:37
  24.5 1.2 %collective-permute-start.7 = (bf16[32,1536]{1,0:T(8,128)(2,1)S(1)}, bf16[32,1536]{1,0:T(8,128)(2,1)S(1)}, u32[]{:S(2)}, u32[]{:S(2)}) collective-permute-start(bf16[32,1536]{1,0:T(8,128)(2,1)S(1)} %get-tuple-element.32), channel_id=1, source_target_pairs={{0,8},{8,0},{16,24},{24,16},{1,9},{9,1},{17,25},{25,17},{2,10},{10... | collective-permute-start | bytes 294920 | tf_op jit(solution)/shard_map/ppermute | solution.py:64
  25.7 1.5 %collective-permute-start.8 = (bf16[32,1536]{1,0:T(8,128)(2,1)S(1)}, bf16[32,1536]{1,0:T(8,128)(2,1)S(1)}, u32[]{:S(2)}, u32[]{:S(2)}) collective-permute-start(bf16[32,1536]{1,0:T(8,128)(2,1)S(1)} %get-tuple-element.33), channel_id=1, source_target_pairs={{0,16},{8,24},{16,0},{24,8},{1,17},{9,25},{17,1},{25,9},{2,18},{10... | collective-permute-start | bytes 294920 | tf_op jit(solution)/shard_map/ppermute | solution.py:64
  27.3 0.8 %collective-permute-start.9 = (bf16[32,1536]{1,0:T(8,128)(2,1)S(1)}, bf16[32,1536]{1,0:T(8,128)(2,1)S(1)}, u32[]{:S(2)}, u32[]{:S(2)}) collective-permute-start(bf16[32,1536]{1,0:T(8,128)(2,1)S(1)} %get-tuple-element.34), channel_id=1, source_target_pairs={{0,24},{8,16},{16,8},{24,0},{1,25},{9,17},{17,9},{25,1},{2,26},{10... | collective-permute-start | bytes 294920 | tf_op jit(solution)/shard_map/ppermute | solution.py:64
  28.1 2.1 %collective-permute-done.7.refs_1_ = bf16[32,1536]{1,0:T(8,128)(2,1)S(1)} collective-permute-done((bf16[32,1536]{1,0:T(8,128)(2,1)S(1)}, bf16[32,1536]{1,0:T(8,128)(2,1)S(1)}, u32[]{:S(2)}, u32[]{:S(2)}) %collective-permute-start.7) | collective-permute-done | bytes 98336 | tf_op jit(solution)/shard_map/ppermute | solution.py:64
  30.1 1.3 %collective-permute-done.8.refs_2_ = bf16[32,1536]{1,0:T(8,128)(2,1)S(1)} collective-permute-done((bf16[32,1536]{1,0:T(8,128)(2,1)S(1)}, bf16[32,1536]{1,0:T(8,128)(2,1)S(1)}, u32[]{:S(2)}, u32[]{:S(2)}) %collective-permute-start.8) | collective-permute-done | bytes 98336 | tf_op jit(solution)/shard_map/ppermute | solution.py:64
  31.4 1.4 %collective-permute-done.9.refs_3_ = bf16[32,1536]{1,0:T(8,128)(2,1)S(1)} collective-permute-done((bf16[32,1536]{1,0:T(8,128)(2,1)S(1)}, bf16[32,1536]{1,0:T(8,128)(2,1)S(1)}, u32[]{:S(2)}, u32[]{:S(2)}) %collective-permute-start.9) | collective-permute-done | bytes 98336 | tf_op jit(solution)/shard_map/ppermute | solution.py:64
  32.8 0.1 activations.1.refs_0_.refs_1_.refs_2_
  32.9 0.9 %collective-permute-start.12 = (bf16[32,1536]{1,0:T(8,128)(2,1)S(1)}, bf16[32,1536]{1,0:T(8,128)(2,1)S(1)}, u32[]{:S(2)}, u32[]{:S(2)}) collective-permute-start(bf16[32,1536]{1,0:T(8,128)(2,1)S(1)} %activations.1.refs_0_.refs_1_.refs_2_), channel_id=1, source_target_pairs={{0,24},{8,16},{16,8},{24,0},{1,25},{9,17},{17,9},{25,1},{2,26},{10... | collective-permute-start | bytes 294920 | tf_op jit(solution)/shard_map/ppermute | solution.py:64
  33.7 1.2 %collective-permute-start.11 = (bf16[32,1536]{1,0:T(8,128)(2,1)S(1)}, bf16[32,1536]{1,0:T(8,128)(2,1)S(1)}, u32[]{:S(2)}, u32[]{:S(2)}) collective-permute-start(bf16[32,1536]{1,0:T(8,128)(2,1)S(1)} %activations.1.refs_0_.refs_1_.refs_2_), channel_id=1, source_target_pairs={{0,16},{8,24},{16,0},{24,8},{1,17},{9,25},{17,1},{25,9},{2,18},{10... | collective-permute-start | bytes 294920 | tf_op jit(solution)/shard_map/ppermute | solution.py:64
  34.9 1.5 %collective-permute-start.10 = (bf16[32,1536]{1,0:T(8,128)(2,1)S(1)}, bf16[32,1536]{1,0:T(8,128)(2,1)S(1)}, u32[]{:S(2)}, u32[]{:S(2)}) collective-permute-start(bf16[32,1536]{1,0:T(8,128)(2,1)S(1)} %activations.1.refs_0_.refs_1_.refs_2_), channel_id=1, source_target_pairs={{0,8},{8,0},{16,24},{24,16},{1,9},{9,1},{17,25},{25,17},{2,10},{10... | collective-permute-start | bytes 294920 | tf_op jit(solution)/shard_map/ppermute | solution.py:64
  36.4 0.0 collective-permute-start.13
  36.4 2.1 %collective-permute-done.12.refs_3_.refs_4_.refs_5_ = bf16[32,1536]{1,0:T(8,128)(2,1)S(1)} collective-permute-done((bf16[32,1536]{1,0:T(8,128)(2,1)S(1)}, bf16[32,1536]{1,0:T(8,128)(2,1)S(1)}, u32[]{:S(2)}, u32[]{:S(2)}) %collective-permute-start.12) | collective-permute-done | bytes 98336 | tf_op jit(solution)/shard_map/ppermute | solution.py:64
  38.5 0.8 %collective-permute-done.11.refs_2_.refs_3_.refs_4_ = bf16[32,1536]{1,0:T(8,128)(2,1)S(1)} collective-permute-done((bf16[32,1536]{1,0:T(8,128)(2,1)S(1)}, bf16[32,1536]{1,0:T(8,128)(2,1)S(1)}, u32[]{:S(2)}, u32[]{:S(2)}) %collective-permute-start.11) | collective-permute-done | bytes 98336 | tf_op jit(solution)/shard_map/ppermute | solution.py:64
  39.4 0.1 collective-permute-done.10.refs_1_.refs_2_.refs_3_
  39.6 1.4 %dx.1 = bf16[4,32,896]{2,1,0:T(8,128)(2,1)} custom-call(bf16[128,768]{1,0:T(8,128)(2,1)S(1)} %share.1.refs_0_, bf16[32,1536]{1,0:T(8,128)(2,1)S(1)} %activations.1.refs_0_.refs_1_.refs_2_, bf16[32,1536]{1,0:T(8,128)(2,1)S(1)} %collective-permute-done.10.refs_1_.refs_2_.refs_3_, bf16[32,1536]{1,0:T(8,128)(2,1)S(1)} %collective-permute-done.11.refs_2_.refs_3_.refs_4_, ...), custom_call_target="tpu_custom_call" | custom-call | flops 234881024 | bytes 2981888 | tf_op jit(solution)/shard_map/dx/pallas_call | solution.py:37
  40.9 4.8 %all-to-all-start = ((bf16[16,8,896]{2,1,0:T(8,128)(2,1)}), bf16[16,8,896]{2,1,0:T(8,128)(2,1)S(1)}, u32[]{:S(2)}, u32[]{:S(2)}) async-start(bf16[16,8,896]{2,1,0:T(8,128)(2,1)} %bitcast.4), calls=%async_computation | async-start | bytes 458752 | tf_op jit(solution)/shard_map/all_to_all | solution.py:388
  45.7 0.1 collective-permute-start.14
  45.8 1.4 %collective-permute-done.14.refs_6_ = bf16[128,768]{1,0:T(8,128)(2,1)S(1)} collective-permute-done((bf16[128,768]{1,0:T(8,128)(2,1)S(1)}, bf16[128,768]{1,0:T(8,128)(2,1)S(1)}, u32[]{:S(2)}, u32[]{:S(2)}) %collective-permute-start.14) | collective-permute-done | bytes 196640 | tf_op jit(solution)/shard_map/ppermute | solution.py:64
  47.2 0.0 collective-permute-done.13.refs_1_
  47.2 1.5 %gradients.1 = (bf16[896,256]{1,0:T(8,128)(2,1)}, bf16[896,256]{1,0:T(8,128)(2,1)}, bf16[256,896]{1,0:T(8,128)(2,1)}, f32[8,128]{1,0:T(8,128)S(1)}) custom-call(bf16[256,896]{1,0:T(8,128)(2,1)S(1)} %get-tuple-element.35.refs_0_, bf16[256,896]{1,0:T(8,128)(2,1)S(1)} %collective-permute-done.13.refs_1_, ...), custom_call_target="tpu_custom_call" | custom-call | flops 352321536 | bytes 2887680 | tf_op jit(solution)/shard_map/gradients/pallas_call | solution.py:37
  48.8 5.5 %all-to-all-done.refs_0_ = bf16[16,8,896]{2,1,0:T(8,128)(2,1)S(1)} async-done(((bf16[16,8,896]{2,1,0:T(8,128)(2,1)}), bf16[16,8,896]{2,1,0:T(8,128)(2,1)S(1)}, u32[]{:S(2)}, u32[]{:S(2)}) %all-to-all-start) | async-done | bytes 229408 | tf_op jit(solution)/shard_map/all_to_all | solution.py:388
  54.3 1.2 %place.1 = bf16[128,3584]{1,0:T(8,128)(2,1)} custom-call(bf16[16,8,896]{2,1,0:T(8,128)(2,1)S(1)} %all-to-all-done.refs_0_, f32[1,8,128]{2,1,0:T(8,128)S(1)} %get-tuple-element.22.refs_0_.refs_1_, f32[8,128]{1,0:T(8,128)S(1)} %get-tuple-element.36.refs_2_), custom_call_target="tpu_custom_call" | custom-call | flops 7340032 | bytes 1155072 | tf_op jit(solution)/shard_map/place/pallas_call | solution.py:37
  (22 shorter events, 0.1 us)
Async XLA Ops:
  0.6 1.6 %copy-start.5 = (s32[128,8]{0,1:T(8,128)S(1)}, s32[128,8]{0,1:T(8,128)}, u32[]{:S(2)}) copy-start(s32[128,8]{0,1:T(8,128)} %param.15) | copy-start | bytes 12292
  0.6 1.6 %copy-start.6 = (f32[128,8]{0,1:T(8,128)S(1)}, f32[128,8]{0,1:T(8,128)}, u32[]{:S(2)}) copy-start(f32[128,8]{0,1:T(8,128)} %param.14) | copy-start | bytes 12292
  0.7 1.8 %copy-start.1 = (bf16[128,3584]{1,0:T(8,128)(2,1)S(1)}, bf16[128,3584]{1,0:T(8,128)(2,1)}, u32[]{:S(2)}) copy-start(bf16[128,3584]{1,0:T(8,128)(2,1)} %refs_3_.1) | copy-start | bytes 2752516
  0.7 1.8 %copy-start = (bf16[128,3584]{1,0:T(8,128)(2,1)S(1)}, bf16[128,3584]{1,0:T(8,128)(2,1)}, u32[]{:S(2)}) copy-start(bf16[128,3584]{1,0:T(8,128)(2,1)} %refs_2_.2) | copy-start | bytes 2752516
  2.1 5.6 %copy-start.2 = (bf16[896,256]{1,0:T(8,128)(2,1)S(1)}, bf16[896,256]{1,0:T(8,128)(2,1)}, u32[]{:S(2)}) copy-start(bf16[896,256]{1,0:T(8,128)(2,1)} %refs_4_.1) | copy-start | bytes 1376260
  2.1 5.6 %copy-start.3 = (bf16[896,256]{1,0:T(8,128)(2,1)S(1)}, bf16[896,256]{1,0:T(8,128)(2,1)}, u32[]{:S(2)}) copy-start(bf16[896,256]{1,0:T(8,128)(2,1)} %refs_5_.1) | copy-start | bytes 1376260
  2.1 5.6 %copy-start.4 = (bf16[256,896]{1,0:T(8,128)(2,1)S(1)}, bf16[256,896]{1,0:T(8,128)(2,1)}, u32[]{:S(2)}) copy-start(bf16[256,896]{1,0:T(8,128)(2,1)} %refs_6_.1) | copy-start | bytes 1376260
  2.1 5.5 %copy-start.7 = (f32[28,2]{0,1:T(2,128)S(1)}, f32[28,2]{0,1:T(2,128)}, u32[]{:S(2)}) copy-start(f32[28,2]{0,1:T(2,128)} %param.21) | copy-start | bytes 676
  2.2 5.5 %copy-start.8 = (f32[28,2]{0,1:T(2,128)S(1)}, f32[28,2]{0,1:T(2,128)}, u32[]{:S(2)}) copy-start(f32[28,2]{0,1:T(2,128)} %param.22) | copy-start | bytes 676
  2.2 5.5 %copy-start.9 = (f32[2,28]{1,0:T(2,128)S(1)}, f32[2,28]{1,0:T(2,128)}, u32[]{:S(2)}) copy-start(f32[2,28]{1,0:T(2,128)} %refs_2_.3) | copy-start | bytes 676
  2.8 4.9 %collective-permute-start = (bf16[16,896]{1,0:T(8,128)(2,1)S(1)}, bf16[16,896]{1,0:T(8,128)(2,1)S(1)}, u32[]{:S(2)}, u32[]{:S(2)}) collective-permute-start(bf16[16,896]{1,0:T(8,128)(2,1)S(1)} %get-tuple-element.25), channel_id=1, source_target_pairs={{0,8},{8,0},{16,24},{24,16},{1,9},{9,1},{17,25},{25,17},{2,10},{10... | collective-permute-start | bytes 86024 | tf_op jit(solution)/shard_map/ppermute | solution.py:64
  5.8 3.9 %collective-permute-start.1 = (bf16[16,896]{1,0:T(8,128)(2,1)S(1)}, bf16[16,896]{1,0:T(8,128)(2,1)S(1)}, u32[]{:S(2)}, u32[]{:S(2)}) collective-permute-start(bf16[16,896]{1,0:T(8,128)(2,1)S(1)} %get-tuple-element.26), channel_id=1, source_target_pairs={{0,16},{8,24},{16,0},{24,8},{1,17},{9,25},{17,1},{25,9},{2,18},{10... | collective-permute-start | bytes 86024 | tf_op jit(solution)/shard_map/ppermute | solution.py:64
  7.4 4.8 %collective-permute-start.2 = (bf16[16,896]{1,0:T(8,128)(2,1)S(1)}, bf16[16,896]{1,0:T(8,128)(2,1)S(1)}, u32[]{:S(2)}, u32[]{:S(2)}) collective-permute-start(bf16[16,896]{1,0:T(8,128)(2,1)S(1)} %get-tuple-element.27), channel_id=1, source_target_pairs={{0,24},{8,16},{16,8},{24,0},{1,25},{9,17},{17,9},{25,1},{2,26},{10... | collective-permute-start | bytes 86024 | tf_op jit(solution)/shard_map/ppermute | solution.py:64
  8.8 15.0 %collective-permute-start.6 = (bf16[1408,512]{1,0:T(8,128)(2,1)S(1)}, bf16[1408,512]{1,0:T(8,128)(2,1)S(1)}, u32[]{:S(2)}, u32[]{:S(2)}) collective-permute-start(bf16[1408,512]{1,0:T(8,128)(2,1)S(1)} %get-tuple-element.30), channel_id=1, source_target_pairs={{0,1},{1,0},{2,3},{3,2},{4,5},{5,4},{6,7},{7,6},{8,9},{9,8},{10,11... | collective-permute-start | bytes 4325384 | tf_op jit(solution)/shard_map/ppermute | solution.py:64
  12.2 7.2 %collective-permute-start.5 = (bf16[64,896]{1,0:T(8,128)(2,1)S(1)}, bf16[64,896]{1,0:T(8,128)(2,1)S(1)}, u32[]{:S(2)}, u32[]{:S(2)}) collective-permute-start(bf16[64,896]{1,0:T(8,128)(2,1)S(1)} %constant_dynamic-update-slice_fusion.refs_0_), channel_id=1, source_target_pairs={{0,6},{1,7},{2,4},{3,5},{4,2},{5,3},{6,0},{7,1},{8,14},{9,15},{10,... | collective-permute-start | bytes 344072 | tf_op jit(solution)/shard_map/ppermute | solution.py:64
  15.8 8.0 %collective-permute-start.4 = (bf16[64,896]{1,0:T(8,128)(2,1)S(1)}, bf16[64,896]{1,0:T(8,128)(2,1)S(1)}, u32[]{:S(2)}, u32[]{:S(2)}) collective-permute-start(bf16[64,896]{1,0:T(8,128)(2,1)S(1)} %constant_dynamic-update-slice_fusion.refs_0_), channel_id=1, source_target_pairs={{0,4},{1,5},{2,6},{3,7},{4,0},{5,1},{6,2},{7,3},{8,12},{9,13},{10,... | collective-permute-start | bytes 344072 | tf_op jit(solution)/shard_map/ppermute | solution.py:64
  15.8 8.0 %collective-permute-start.3 = (bf16[64,896]{1,0:T(8,128)(2,1)S(1)}, bf16[64,896]{1,0:T(8,128)(2,1)S(1)}, u32[]{:S(2)}, u32[]{:S(2)}) collective-permute-start(bf16[64,896]{1,0:T(8,128)(2,1)S(1)} %constant_dynamic-update-slice_fusion.refs_0_), channel_id=1, source_target_pairs={{0,2},{1,3},{2,0},{3,1},{4,6},{5,7},{6,4},{7,5},{8,10},{9,11},{10,... | collective-permute-start | bytes 344072 | tf_op jit(solution)/shard_map/ppermute | solution.py:64
  24.5 5.6 %collective-permute-start.7 = (bf16[32,1536]{1,0:T(8,128)(2,1)S(1)}, bf16[32,1536]{1,0:T(8,128)(2,1)S(1)}, u32[]{:S(2)}, u32[]{:S(2)}) collective-permute-start(bf16[32,1536]{1,0:T(8,128)(2,1)S(1)} %get-tuple-element.32), channel_id=1, source_target_pairs={{0,8},{8,0},{16,24},{24,16},{1,9},{9,1},{17,25},{25,17},{2,10},{10... | collective-permute-start | bytes 294920 | tf_op jit(solution)/shard_map/ppermute | solution.py:64
  25.7 5.7 %collective-permute-start.8 = (bf16[32,1536]{1,0:T(8,128)(2,1)S(1)}, bf16[32,1536]{1,0:T(8,128)(2,1)S(1)}, u32[]{:S(2)}, u32[]{:S(2)}) collective-permute-start(bf16[32,1536]{1,0:T(8,128)(2,1)S(1)} %get-tuple-element.33), channel_id=1, source_target_pairs={{0,16},{8,24},{16,0},{24,8},{1,17},{9,25},{17,1},{25,9},{2,18},{10... | collective-permute-start | bytes 294920 | tf_op jit(solution)/shard_map/ppermute | solution.py:64
  27.3 5.5 %collective-permute-start.9 = (bf16[32,1536]{1,0:T(8,128)(2,1)S(1)}, bf16[32,1536]{1,0:T(8,128)(2,1)S(1)}, u32[]{:S(2)}, u32[]{:S(2)}) collective-permute-start(bf16[32,1536]{1,0:T(8,128)(2,1)S(1)} %get-tuple-element.34), channel_id=1, source_target_pairs={{0,24},{8,16},{16,8},{24,0},{1,25},{9,17},{17,9},{25,1},{2,26},{10... | collective-permute-start | bytes 294920 | tf_op jit(solution)/shard_map/ppermute | solution.py:64
  32.9 5.7 %collective-permute-start.12 = (bf16[32,1536]{1,0:T(8,128)(2,1)S(1)}, bf16[32,1536]{1,0:T(8,128)(2,1)S(1)}, u32[]{:S(2)}, u32[]{:S(2)}) collective-permute-start(bf16[32,1536]{1,0:T(8,128)(2,1)S(1)} %activations.1.refs_0_.refs_1_.refs_2_), channel_id=1, source_target_pairs={{0,24},{8,16},{16,8},{24,0},{1,25},{9,17},{17,9},{25,1},{2,26},{10... | collective-permute-start | bytes 294920 | tf_op jit(solution)/shard_map/ppermute | solution.py:64
  33.7 5.7 %collective-permute-start.11 = (bf16[32,1536]{1,0:T(8,128)(2,1)S(1)}, bf16[32,1536]{1,0:T(8,128)(2,1)S(1)}, u32[]{:S(2)}, u32[]{:S(2)}) collective-permute-start(bf16[32,1536]{1,0:T(8,128)(2,1)S(1)} %activations.1.refs_0_.refs_1_.refs_2_), channel_id=1, source_target_pairs={{0,16},{8,24},{16,0},{24,8},{1,17},{9,25},{17,1},{25,9},{2,18},{10... | collective-permute-start | bytes 294920 | tf_op jit(solution)/shard_map/ppermute | solution.py:64
  34.9 4.6 %collective-permute-start.10 = (bf16[32,1536]{1,0:T(8,128)(2,1)S(1)}, bf16[32,1536]{1,0:T(8,128)(2,1)S(1)}, u32[]{:S(2)}, u32[]{:S(2)}) collective-permute-start(bf16[32,1536]{1,0:T(8,128)(2,1)S(1)} %activations.1.refs_0_.refs_1_.refs_2_), channel_id=1, source_target_pairs={{0,8},{8,0},{16,24},{24,16},{1,9},{9,1},{17,25},{25,17},{2,10},{10... | collective-permute-start | bytes 294920 | tf_op jit(solution)/shard_map/ppermute | solution.py:64
  36.4 10.8 %collective-permute-start.13 = (bf16[256,896]{1,0:T(8,128)(2,1)S(1)}, bf16[256,896]{1,0:T(8,128)(2,1)S(1)}, u32[]{:S(2)}, u32[]{:S(2)}) collective-permute-start(bf16[256,896]{1,0:T(8,128)(2,1)S(1)} %get-tuple-element.35.refs_0_), channel_id=1, source_target_pairs={{0,1},{1,0},{2,3},{3,2},{4,5},{5,4},{6,7},{7,6},{8,9},{9,8},{10,11... | collective-permute-start | bytes 1376264 | tf_op jit(solution)/shard_map/ppermute | solution.py:64
  40.9 13.3 %all-to-all-start = ((bf16[16,8,896]{2,1,0:T(8,128)(2,1)}), bf16[16,8,896]{2,1,0:T(8,128)(2,1)S(1)}, u32[]{:S(2)}, u32[]{:S(2)}) async-start(bf16[16,8,896]{2,1,0:T(8,128)(2,1)} %bitcast.4), calls=%async_computation | async-start | bytes 458752 | tf_op jit(solution)/shard_map/all_to_all | solution.py:388
  45.7 1.5 %collective-permute-start.14 = (bf16[128,768]{1,0:T(8,128)(2,1)S(1)}, bf16[128,768]{1,0:T(8,128)(2,1)S(1)}, u32[]{:S(2)}, u32[]{:S(2)}) collective-permute-start(bf16[128,768]{1,0:T(8,128)(2,1)S(1)} %share.1.refs_0_), channel_id=1, source_target_pairs={{0,1},{1,0},{2,3},{3,2},{4,5},{5,4},{6,7},{7,6},{8,9},{9,8},{10,11... | collective-permute-start | bytes 589832 | tf_op jit(solution)/shard_map/ppermute | solution.py:64

commit v7 on v6

--- a/solution.py
+++ b/solution.py
@@ -62,6 +62,25 @@
 
 def swap(x, axis, k):
     return lax.ppermute(x, axis, [(i, i ^ k) for i in range(lax.axis_size(axis))])
+
+
+def crossed(k):
+    return k & ~3 | (k & 1) << 1 | (k >> 1) & 1
+
+
+def partner(k):
+    other = jnp.where(lax.axis_index("expert") % 2 == 1, crossed(k), k)
+    return lax.axis_index("dp") ^ (k if crossed(k) == k else other)
+
+
+def swap_slot(x, k):
+    groups, members = lax.axis_size("dp"), lax.axis_size("expert")
+    pairs = [
+        (g * members + m, (g ^ (crossed(k) if m % 2 else k)) * members + m)
+        for g in range(groups)
+        for m in range(members)
+    ]
+    return lax.ppermute(x, ("dp", "expert"), pairs)
 
 
 def rows_of(value, first, count=ROWS):
@@ -120,7 +139,7 @@
             parts += [rows_of(token_rows, e * ROWS), weighted]
         slices[s] = jnp.concatenate(parts, axis=0).astype(BF16)
     for k in range(groups):
-        outs[k][...] = slices[lax.axis_index("dp") ^ k]
+        outs[k][...] = slices[partner(k)]
 
 
 def weights_kernel(scale_gate, scale_up, scale_down, gate, up, down, gate_up, down_out, packed):
@@ -215,7 +234,7 @@
     dx = dx + mm(act[:, 3 * hid : 5 * hid], other[:depth, :], NT)
     count = chips * ROWS
     for k in range(groups):
-        out[lax.axis_index("dp") ^ k] = dx[k * count : (k + 1) * count].astype(BF16)
+        out[partner(k)] = dx[k * count : (k + 1) * count].astype(BF16)
 
 
 def share_kernel(groups, *refs):
@@ -325,7 +344,7 @@
         flops=4 * count * experts * ROWS * width,
         name="route",
     )
-    parts = [sent[0]] + [swap(sent[k], "dp", k) for k in range(1, groups)]
+    parts = [sent[0]] + [swap_slot(sent[k], k) for k in range(1, groups)]
     chunks = [chunk_of(parts, experts, member // HSH)]
     for c in range(1, chips):
         out = chunks[0] if experts == 1 else chunk_of(parts, experts, (member ^ (2 * c)) // HSH)
@@ -353,17 +372,17 @@
         name="partial",
     )
     other_rows = swap(own_rows, "expert", 1)
-    summands = [partial[0]] + [swap(partial[k], "dp", k) for k in range(1, groups)]
+    summands = [partial[0]] + [swap_slot(partial[k], k) for k in range(1, groups)]
     (act,) = call(
         functools.partial(act_kernel, groups, chips),
         [shape((chips * ROWS, 6 * hid))],
         (),
-        summands,
+        summands[:1] + summands[:0:-1],
         scratch=[pltpu.VMEM((chips, ROWS, 6 * hid), F32)],
         flops=40 * chips * ROWS * hid,
         name="activations",
     )
-    acts = [act] + [swap(act, "dp", k) for k in range(1, groups)]
+    acts = [act] + [swap_slot(act, k) for k in range(1, groups)]
     (act_out,) = call(
         functools.partial(share_kernel, groups),
         [shape((rows, 3 * hid))],

time: 55.7 us -> 55.8 us (level)
    ppermute x0 -> x9, starting transfers between devices: none -> 11.7 us  [swap_slot(): return lax.ppermute(x, ('dp', 'expert'), pairs)]
    ppermute x15 -> x6, starting transfers between devices: 16.2 us -> 4.6 us  [swap(): lax.ppermute(x, axis, [(i, i ^ k) for i in range(lax.axis_size(axis))])]
    ppermute x15 -> x6, waiting for transfers between devices: 20 us -> 8.61 us  [swap(): lax.ppermute(x, axis, [(i, i ^ k) for i in range(lax.axis_size(axis))])]
    ppermute x0 -> x9, waiting for transfers between devices: none -> 11.1 us  [swap_slot(): return lax.ppermute(x, ('dp', 'expert'), pairs)]
where the time goes in v7:
time: 55.8 us; the launch traced here: 55.5 us
  waiting for transfers between devices  25.2 us (45%)
  starting transfers between devices  21.3 us (38%)
  Pallas kernels  6.58 us (12%)
  between operations  2.27 us (4%)
    ppermute x9, starting transfers between devices, swap_slot(): return lax.ppermute(x, ('dp', 'expert'), pairs)  11.7 us
    ppermute x9, waiting for transfers between devices, swap_slot(): return lax.ppermute(x, ('dp', 'expert'), pairs)  11.1 us
    ppermute x6, waiting for transfers between devices, swap(): lax.ppermute(x, axis, [(i, i ^ k) for i in range(lax.axis_size(axis))])  8.61 us
    pallas_call x10, Pallas kernels, call(): pl.pallas_call(body, out_shape=outs, in_specs=[pl.BlockSpec(memory_space=...  6.58 us
    all_to_all x1, waiting for transfers between devices, on_device(): lax.all_to_all(dx, ('dp', 'expert'), split_axis=0, concat_axis=0, axis_in...  5.47 us
    all_to_all x1, starting transfers between devices, on_device(): lax.all_to_all(dx, ('dp', 'expert'), split_axis=0, concat_axis=0, axis_in...  5.05 us
    ppermute x6, starting transfers between devices, swap(): lax.ppermute(x, axis, [(i, i ^ k) for i in range(lax.axis_size(axis))])  4.6 us
  transfers between devices with their start and end apart: 16, of which 13 were waited for; matrix products, arithmetic and copies ran while one was open for 0% of the time, Pallas kernels for 7%

profile of v7, /device:TPU:0, one launch (start us, length us, event | category | flops | bytes accessed | tf_op | source)
XLA Modules:
  0.0 55.5 jit_solution(16782564715565102372)
XLA Ops:
  2.1 0.0 copy-start.2
  2.1 0.0 copy-start.3
  2.1 0.0 copy-start.4
  2.1 0.0 copy-start.7
  2.2 0.0 copy-start.8
  2.2 0.0 copy-start.9
  2.2 0.2 lists.1
  2.4 0.4 route.1
  2.8 3.0 %collective-permute-start = (bf16[16,896]{1,0:T(8,128)(2,1)S(1)}, bf16[16,896]{1,0:T(8,128)(2,1)S(1)}, u32[]{:S(2)}, u32[]{:S(2)}) collective-permute-start(bf16[16,896]{1,0:T(8,128)(2,1)S(1)} %get-tuple-element.25), channel_id=1, source_target_pairs={{0,8},{1,17},{2,10},{3,19},{4,12},{5,21},{6,14},{7,23},{8,0},{9,25... | collective-permute-start | bytes 86024 | tf_op jit(solution)/shard_map/ppermute | solution.py:83
  5.8 1.5 %collective-permute-start.1 = (bf16[16,896]{1,0:T(8,128)(2,1)S(1)}, bf16[16,896]{1,0:T(8,128)(2,1)S(1)}, u32[]{:S(2)}, u32[]{:S(2)}) collective-permute-start(bf16[16,896]{1,0:T(8,128)(2,1)S(1)} %get-tuple-element.26), channel_id=1, source_target_pairs={{0,16},{1,9},{2,18},{3,11},{4,20},{5,13},{6,22},{7,15},{8,24},{9,1... | collective-permute-start | bytes 86024 | tf_op jit(solution)/shard_map/ppermute | solution.py:83
  7.4 0.0 collective-permute-start.2
  7.4 0.3 collective-permute-done.refs_3_
  7.7 0.0 copy-done.7
  7.7 0.0 copy-done.8
  7.7 1.0 %weights.1 = (bf16[896,512]{1,0:T(8,128)(2,1)S(1)}, bf16[256,896]{1,0:T(8,128)(2,1)S(1)}, bf16[1408,512]{1,0:T(8,128)(2,1)S(1)}) custom-call(f32[2,28]{1,0:T(2,128)S(1)} %bitcast.7, f32[2,28]{1,0:T(2,128)S(1)} %bitcast.8, f32[2,28]{1,0:T(2,128)S(1)} %copy-done.9, bf16[16,896]{1,0:T(8,128)(2,1)S(1)} %collective-permute-done.refs_3_, ...), custom_call_target="tpu_custom_call" | custom-call | flops 1376256 | bytes 4194304 | tf_op jit(solution)/shard_map/weights/pallas_call | solution.py:37
  8.8 0.1 collective-permute-start.6
  8.9 0.8 %collective-permute-done.1 = bf16[16,896]{1,0:T(8,128)(2,1)S(1)} collective-permute-done((bf16[16,896]{1,0:T(8,128)(2,1)S(1)}, bf16[16,896]{1,0:T(8,128)(2,1)S(1)}, u32[]{:S(2)}, u32[]{:S(2)}) %collective-permute-start.1) | collective-permute-done | bytes 28704 | tf_op jit(solution)/shard_map/ppermute | solution.py:83
  9.7 2.4 %collective-permute-done.2 = bf16[16,896]{1,0:T(8,128)(2,1)S(1)} collective-permute-done((bf16[16,896]{1,0:T(8,128)(2,1)S(1)}, bf16[16,896]{1,0:T(8,128)(2,1)S(1)}, u32[]{:S(2)}, u32[]{:S(2)}) %collective-permute-start.2) | collective-permute-done | bytes 28704 | tf_op jit(solution)/shard_map/ppermute | solution.py:83
  12.2 3.7 %collective-permute-start.5 = (bf16[64,896]{1,0:T(8,128)(2,1)S(1)}, bf16[64,896]{1,0:T(8,128)(2,1)S(1)}, u32[]{:S(2)}, u32[]{:S(2)}) collective-permute-start(bf16[64,896]{1,0:T(8,128)(2,1)S(1)} %constant_dynamic-update-slice_fusion.refs_0_), channel_id=1, source_target_pairs={{0,6},{1,7},{2,4},{3,5},{4,2},{5,3},{6,0},{7,1},{8,14},{9,15},{10,... | collective-permute-start | bytes 344072 | tf_op jit(solution)/shard_map/ppermute | solution.py:64
  15.8 0.0 collective-permute-start.4
  15.8 0.8 %collective-permute-start.3 = (bf16[64,896]{1,0:T(8,128)(2,1)S(1)}, bf16[64,896]{1,0:T(8,128)(2,1)S(1)}, u32[]{:S(2)}, u32[]{:S(2)}) collective-permute-start(bf16[64,896]{1,0:T(8,128)(2,1)S(1)} %constant_dynamic-update-slice_fusion.refs_0_), channel_id=1, source_target_pairs={{0,2},{1,3},{2,0},{3,1},{4,6},{5,7},{6,4},{7,5},{8,10},{9,11},{10,... | collective-permute-start | bytes 344072 | tf_op jit(solution)/shard_map/ppermute | solution.py:64
  16.6 2.7 %collective-permute-done.5.refs_3_ = bf16[64,896]{1,0:T(8,128)(2,1)S(1)} collective-permute-done((bf16[64,896]{1,0:T(8,128)(2,1)S(1)}, bf16[64,896]{1,0:T(8,128)(2,1)S(1)}, u32[]{:S(2)}, u32[]{:S(2)}) %collective-permute-start.5) | collective-permute-done | bytes 114720 | tf_op jit(solution)/shard_map/ppermute | solution.py:64
  19.3 4.5 %collective-permute-done.4.refs_2_ = bf16[64,896]{1,0:T(8,128)(2,1)S(1)} collective-permute-done((bf16[64,896]{1,0:T(8,128)(2,1)S(1)}, bf16[64,896]{1,0:T(8,128)(2,1)S(1)}, u32[]{:S(2)}, u32[]{:S(2)}) %collective-permute-start.4) | collective-permute-done | bytes 114720 | tf_op jit(solution)/shard_map/ppermute | solution.py:64
  23.8 0.0 collective-permute-done.3.refs_1_
  23.8 0.0 collective-permute-done.6.refs_6_
  23.8 0.7 %partial.1 = (f32[32,1536]{1,0:T(8,128)S(1)}, bf16[32,1536]{1,0:T(8,128)(2,1)S(1)}, bf16[32,1536]{1,0:T(8,128)(2,1)S(1)}, bf16[32,1536]{1,0:T(8,128)(2,1)S(1)}, bf16[256,896]{1,0:T(8,128)(2,1)S(1)}) custom-call(bf16[64,896]{1,0:T(8,128)(2,1)S(1)} %constant_dynamic-update-slice_fusion.refs_0_, bf16[64,896]{1,0:T(8,128)(2,1)S(1)} %collective-permute-done.3.refs_1_, ...), custom_call_target="tpu_custom_call" | custom-call | flops 352321536 | bytes 4227072 | tf_op jit(solution)/shard_map/partial/pallas_call | solution.py:37
  24.5 2.2 %collective-permute-start.7 = (bf16[32,1536]{1,0:T(8,128)(2,1)S(1)}, bf16[32,1536]{1,0:T(8,128)(2,1)S(1)}, u32[]{:S(2)}, u32[]{:S(2)}) collective-permute-start(bf16[32,1536]{1,0:T(8,128)(2,1)S(1)} %get-tuple-element.32), channel_id=1, source_target_pairs={{0,24},{1,25},{2,26},{3,27},{4,28},{5,29},{6,30},{7,31},{8,16},{9,... | collective-permute-start | bytes 294920 | tf_op jit(solution)/shard_map/ppermute | solution.py:83
  26.7 0.7 %collective-permute-start.8 = (bf16[32,1536]{1,0:T(8,128)(2,1)S(1)}, bf16[32,1536]{1,0:T(8,128)(2,1)S(1)}, u32[]{:S(2)}, u32[]{:S(2)}) collective-permute-start(bf16[32,1536]{1,0:T(8,128)(2,1)S(1)} %get-tuple-element.33), channel_id=1, source_target_pairs={{0,16},{1,9},{2,18},{3,11},{4,20},{5,13},{6,22},{7,15},{8,24},{9,1... | collective-permute-start | bytes 294920 | tf_op jit(solution)/shard_map/ppermute | solution.py:83
  27.4 0.7 %collective-permute-start.9 = (bf16[32,1536]{1,0:T(8,128)(2,1)S(1)}, bf16[32,1536]{1,0:T(8,128)(2,1)S(1)}, u32[]{:S(2)}, u32[]{:S(2)}) collective-permute-start(bf16[32,1536]{1,0:T(8,128)(2,1)S(1)} %get-tuple-element.34), channel_id=1, source_target_pairs={{0,8},{1,17},{2,10},{3,19},{4,12},{5,21},{6,14},{7,23},{8,0},{9,25... | collective-permute-start | bytes 294920 | tf_op jit(solution)/shard_map/ppermute | solution.py:83
  28.1 2.4 %collective-permute-done.7.refs_1_ = bf16[32,1536]{1,0:T(8,128)(2,1)S(1)} collective-permute-done((bf16[32,1536]{1,0:T(8,128)(2,1)S(1)}, bf16[32,1536]{1,0:T(8,128)(2,1)S(1)}, u32[]{:S(2)}, u32[]{:S(2)}) %collective-permute-start.7) | collective-permute-done | bytes 98336 | tf_op jit(solution)/shard_map/ppermute | solution.py:83
  30.4 1.1 %collective-permute-done.8.refs_2_ = bf16[32,1536]{1,0:T(8,128)(2,1)S(1)} collective-permute-done((bf16[32,1536]{1,0:T(8,128)(2,1)S(1)}, bf16[32,1536]{1,0:T(8,128)(2,1)S(1)}, u32[]{:S(2)}, u32[]{:S(2)}) %collective-permute-start.8) | collective-permute-done | bytes 98336 | tf_op jit(solution)/shard_map/ppermute | solution.py:83
  31.5 0.5 collective-permute-done.9.refs_3_
  32.0 0.1 activations.1.refs_0_.refs_1_.refs_2_
  32.1 1.6 %collective-permute-start.12 = (bf16[32,1536]{1,0:T(8,128)(2,1)S(1)}, bf16[32,1536]{1,0:T(8,128)(2,1)S(1)}, u32[]{:S(2)}, u32[]{:S(2)}) collective-permute-start(bf16[32,1536]{1,0:T(8,128)(2,1)S(1)} %activations.1.refs_0_.refs_1_.refs_2_), channel_id=1, source_target_pairs={{0,24},{1,25},{2,26},{3,27},{4,28},{5,29},{6,30},{7,31},{8,16},{9,... | collective-permute-start | bytes 294920 | tf_op jit(solution)/shard_map/ppermute | solution.py:83
  33.7 1.0 %collective-permute-start.11 = (bf16[32,1536]{1,0:T(8,128)(2,1)S(1)}, bf16[32,1536]{1,0:T(8,128)(2,1)S(1)}, u32[]{:S(2)}, u32[]{:S(2)}) collective-permute-start(bf16[32,1536]{1,0:T(8,128)(2,1)S(1)} %activations.1.refs_0_.refs_1_.refs_2_), channel_id=1, source_target_pairs={{0,16},{1,9},{2,18},{3,11},{4,20},{5,13},{6,22},{7,15},{8,24},{9,1... | collective-permute-start | bytes 294920 | tf_op jit(solution)/shard_map/ppermute | solution.py:83
  34.7 1.0 %collective-permute-start.10 = (bf16[32,1536]{1,0:T(8,128)(2,1)S(1)}, bf16[32,1536]{1,0:T(8,128)(2,1)S(1)}, u32[]{:S(2)}, u32[]{:S(2)}) collective-permute-start(bf16[32,1536]{1,0:T(8,128)(2,1)S(1)} %activations.1.refs_0_.refs_1_.refs_2_), channel_id=1, source_target_pairs={{0,8},{1,17},{2,10},{3,19},{4,12},{5,21},{6,14},{7,23},{8,0},{9,25... | collective-permute-start | bytes 294920 | tf_op jit(solution)/shard_map/ppermute | solution.py:83
  35.7 0.0 collective-permute-start.13
  35.7 2.3 %collective-permute-done.12.refs_3_.refs_4_.refs_5_ = bf16[32,1536]{1,0:T(8,128)(2,1)S(1)} collective-permute-done((bf16[32,1536]{1,0:T(8,128)(2,1)S(1)}, bf16[32,1536]{1,0:T(8,128)(2,1)S(1)}, u32[]{:S(2)}, u32[]{:S(2)}) %collective-permute-start.12) | collective-permute-done | bytes 98336 | tf_op jit(solution)/shard_map/ppermute | solution.py:83
  38.0 1.0 %collective-permute-done.11.refs_2_.refs_3_.refs_4_ = bf16[32,1536]{1,0:T(8,128)(2,1)S(1)} collective-permute-done((bf16[32,1536]{1,0:T(8,128)(2,1)S(1)}, bf16[32,1536]{1,0:T(8,128)(2,1)S(1)}, u32[]{:S(2)}, u32[]{:S(2)}) %collective-permute-start.11) | collective-permute-done | bytes 98336 | tf_op jit(solution)/shard_map/ppermute | solution.py:83
  39.0 0.3 collective-permute-done.10.refs_1_.refs_2_.refs_3_
  39.3 1.4 %dx.1 = bf16[4,32,896]{2,1,0:T(8,128)(2,1)} custom-call(bf16[128,768]{1,0:T(8,128)(2,1)S(1)} %share.1.refs_0_, bf16[32,1536]{1,0:T(8,128)(2,1)S(1)} %activations.1.refs_0_.refs_1_.refs_2_, bf16[32,1536]{1,0:T(8,128)(2,1)S(1)} %collective-permute-done.10.refs_1_.refs_2_.refs_3_, bf16[32,1536]{1,0:T(8,128)(2,1)S(1)} %collective-permute-done.11.refs_2_.refs_3_.refs_4_, ...), custom_call_target="tpu_custom_call" | custom-call | flops 234881024 | bytes 2981888 | tf_op jit(solution)/shard_map/dx/pallas_call | solution.py:37
  40.7 5.0 %all-to-all-start = ((bf16[16,8,896]{2,1,0:T(8,128)(2,1)}), bf16[16,8,896]{2,1,0:T(8,128)(2,1)S(1)}, u32[]{:S(2)}, u32[]{:S(2)}) async-start(bf16[16,8,896]{2,1,0:T(8,128)(2,1)} %bitcast.4), calls=%async_computation | async-start | bytes 458752 | tf_op jit(solution)/shard_map/all_to_all | solution.py:407
  45.7 0.1 collective-permute-start.14
  45.8 1.4 %collective-permute-done.14.refs_6_ = bf16[128,768]{1,0:T(8,128)(2,1)S(1)} collective-permute-done((bf16[128,768]{1,0:T(8,128)(2,1)S(1)}, bf16[128,768]{1,0:T(8,128)(2,1)S(1)}, u32[]{:S(2)}, u32[]{:S(2)}) %collective-permute-start.14) | collective-permute-done | bytes 196640 | tf_op jit(solution)/shard_map/ppermute | solution.py:64
  47.2 0.0 collective-permute-done.13.refs_1_
  47.2 1.5 %gradients.1 = (bf16[896,256]{1,0:T(8,128)(2,1)}, bf16[896,256]{1,0:T(8,128)(2,1)}, bf16[256,896]{1,0:T(8,128)(2,1)}, f32[8,128]{1,0:T(8,128)S(1)}) custom-call(bf16[256,896]{1,0:T(8,128)(2,1)S(1)} %get-tuple-element.35.refs_0_, bf16[256,896]{1,0:T(8,128)(2,1)S(1)} %collective-permute-done.13.refs_1_, ...), custom_call_target="tpu_custom_call" | custom-call | flops 352321536 | bytes 2887680 | tf_op jit(solution)/shard_map/gradients/pallas_call | solution.py:37
  48.8 5.5 %all-to-all-done.refs_0_ = bf16[16,8,896]{2,1,0:T(8,128)(2,1)S(1)} async-done(((bf16[16,8,896]{2,1,0:T(8,128)(2,1)}), bf16[16,8,896]{2,1,0:T(8,128)(2,1)S(1)}, u32[]{:S(2)}, u32[]{:S(2)}) %all-to-all-start) | async-done | bytes 229408 | tf_op jit(solution)/shard_map/all_to_all | solution.py:407
  54.3 1.2 %place.1 = bf16[128,3584]{1,0:T(8,128)(2,1)} custom-call(bf16[16,8,896]{2,1,0:T(8,128)(2,1)S(1)} %all-to-all-done.refs_0_, f32[1,8,128]{2,1,0:T(8,128)S(1)} %get-tuple-element.22.refs_0_.refs_1_, f32[8,128]{1,0:T(8,128)S(1)} %get-tuple-element.36.refs_2_), custom_call_target="tpu_custom_call" | custom-call | flops 7340032 | bytes 1155072 | tf_op jit(solution)/shard_map/place/pallas_call | solution.py:37
  (22 shorter events, 0.1 us)
Async XLA Ops:
  0.6 1.6 %copy-start.5 = (s32[128,8]{0,1:T(8,128)S(1)}, s32[128,8]{0,1:T(8,128)}, u32[]{:S(2)}) copy-start(s32[128,8]{0,1:T(8,128)} %param.15) | copy-start | bytes 12292
  0.6 1.6 %copy-start.6 = (f32[128,8]{0,1:T(8,128)S(1)}, f32[128,8]{0,1:T(8,128)}, u32[]{:S(2)}) copy-start(f32[128,8]{0,1:T(8,128)} %param.14) | copy-start | bytes 12292
  0.7 1.8 %copy-start.1 = (bf16[128,3584]{1,0:T(8,128)(2,1)S(1)}, bf16[128,3584]{1,0:T(8,128)(2,1)}, u32[]{:S(2)}) copy-start(bf16[128,3584]{1,0:T(8,128)(2,1)} %refs_3_.1) | copy-start | bytes 2752516
  0.7 1.8 %copy-start = (bf16[128,3584]{1,0:T(8,128)(2,1)S(1)}, bf16[128,3584]{1,0:T(8,128)(2,1)}, u32[]{:S(2)}) copy-start(bf16[128,3584]{1,0:T(8,128)(2,1)} %refs_2_.2) | copy-start | bytes 2752516
  2.1 5.6 %copy-start.2 = (bf16[896,256]{1,0:T(8,128)(2,1)S(1)}, bf16[896,256]{1,0:T(8,128)(2,1)}, u32[]{:S(2)}) copy-start(bf16[896,256]{1,0:T(8,128)(2,1)} %refs_4_.1) | copy-start | bytes 1376260
  2.1 5.6 %copy-start.3 = (bf16[896,256]{1,0:T(8,128)(2,1)S(1)}, bf16[896,256]{1,0:T(8,128)(2,1)}, u32[]{:S(2)}) copy-start(bf16[896,256]{1,0:T(8,128)(2,1)} %refs_5_.1) | copy-start | bytes 1376260
  2.1 5.6 %copy-start.4 = (bf16[256,896]{1,0:T(8,128)(2,1)S(1)}, bf16[256,896]{1,0:T(8,128)(2,1)}, u32[]{:S(2)}) copy-start(bf16[256,896]{1,0:T(8,128)(2,1)} %refs_6_.1) | copy-start | bytes 1376260
  2.1 5.5 %copy-start.7 = (f32[28,2]{0,1:T(2,128)S(1)}, f32[28,2]{0,1:T(2,128)}, u32[]{:S(2)}) copy-start(f32[28,2]{0,1:T(2,128)} %param.21) | copy-start | bytes 676
  2.2 5.5 %copy-start.8 = (f32[28,2]{0,1:T(2,128)S(1)}, f32[28,2]{0,1:T(2,128)}, u32[]{:S(2)}) copy-start(f32[28,2]{0,1:T(2,128)} %param.22) | copy-start | bytes 676
  2.2 5.5 %copy-start.9 = (f32[2,28]{1,0:T(2,128)S(1)}, f32[2,28]{1,0:T(2,128)}, u32[]{:S(2)}) copy-start(f32[2,28]{1,0:T(2,128)} %refs_2_.3) | copy-start | bytes 676
  2.8 4.9 %collective-permute-start = (bf16[16,896]{1,0:T(8,128)(2,1)S(1)}, bf16[16,896]{1,0:T(8,128)(2,1)S(1)}, u32[]{:S(2)}, u32[]{:S(2)}) collective-permute-start(bf16[16,896]{1,0:T(8,128)(2,1)S(1)} %get-tuple-element.25), channel_id=1, source_target_pairs={{0,8},{1,17},{2,10},{3,19},{4,12},{5,21},{6,14},{7,23},{8,0},{9,25... | collective-permute-start | bytes 86024 | tf_op jit(solution)/shard_map/ppermute | solution.py:83
  5.8 3.9 %collective-permute-start.1 = (bf16[16,896]{1,0:T(8,128)(2,1)S(1)}, bf16[16,896]{1,0:T(8,128)(2,1)S(1)}, u32[]{:S(2)}, u32[]{:S(2)}) collective-permute-start(bf16[16,896]{1,0:T(8,128)(2,1)S(1)} %get-tuple-element.26), channel_id=1, source_target_pairs={{0,16},{1,9},{2,18},{3,11},{4,20},{5,13},{6,22},{7,15},{8,24},{9,1... | collective-permute-start | bytes 86024 | tf_op jit(solution)/shard_map/ppermute | solution.py:83
  7.4 4.8 %collective-permute-start.2 = (bf16[16,896]{1,0:T(8,128)(2,1)S(1)}, bf16[16,896]{1,0:T(8,128)(2,1)S(1)}, u32[]{:S(2)}, u32[]{:S(2)}) collective-permute-start(bf16[16,896]{1,0:T(8,128)(2,1)S(1)} %get-tuple-element.27), channel_id=1, source_target_pairs={{0,24},{1,25},{2,26},{3,27},{4,28},{5,29},{6,30},{7,31},{8,16},{9,... | collective-permute-start | bytes 86024 | tf_op jit(solution)/shard_map/ppermute | solution.py:83
  8.8 15.0 %collective-permute-start.6 = (bf16[1408,512]{1,0:T(8,128)(2,1)S(1)}, bf16[1408,512]{1,0:T(8,128)(2,1)S(1)}, u32[]{:S(2)}, u32[]{:S(2)}) collective-permute-start(bf16[1408,512]{1,0:T(8,128)(2,1)S(1)} %get-tuple-element.30), channel_id=1, source_target_pairs={{0,1},{1,0},{2,3},{3,2},{4,5},{5,4},{6,7},{7,6},{8,9},{9,8},{10,11... | collective-permute-start | bytes 4325384 | tf_op jit(solution)/shard_map/ppermute | solution.py:64
  12.2 7.2 %collective-permute-start.5 = (bf16[64,896]{1,0:T(8,128)(2,1)S(1)}, bf16[64,896]{1,0:T(8,128)(2,1)S(1)}, u32[]{:S(2)}, u32[]{:S(2)}) collective-permute-start(bf16[64,896]{1,0:T(8,128)(2,1)S(1)} %constant_dynamic-update-slice_fusion.refs_0_), channel_id=1, source_target_pairs={{0,6},{1,7},{2,4},{3,5},{4,2},{5,3},{6,0},{7,1},{8,14},{9,15},{10,... | collective-permute-start | bytes 344072 | tf_op jit(solution)/shard_map/ppermute | solution.py:64
  15.8 8.0 %collective-permute-start.4 = (bf16[64,896]{1,0:T(8,128)(2,1)S(1)}, bf16[64,896]{1,0:T(8,128)(2,1)S(1)}, u32[]{:S(2)}, u32[]{:S(2)}) collective-permute-start(bf16[64,896]{1,0:T(8,128)(2,1)S(1)} %constant_dynamic-update-slice_fusion.refs_0_), channel_id=1, source_target_pairs={{0,4},{1,5},{2,6},{3,7},{4,0},{5,1},{6,2},{7,3},{8,12},{9,13},{10,... | collective-permute-start | bytes 344072 | tf_op jit(solution)/shard_map/ppermute | solution.py:64
  15.8 8.0 %collective-permute-start.3 = (bf16[64,896]{1,0:T(8,128)(2,1)S(1)}, bf16[64,896]{1,0:T(8,128)(2,1)S(1)}, u32[]{:S(2)}, u32[]{:S(2)}) collective-permute-start(bf16[64,896]{1,0:T(8,128)(2,1)S(1)} %constant_dynamic-update-slice_fusion.refs_0_), channel_id=1, source_target_pairs={{0,2},{1,3},{2,0},{3,1},{4,6},{5,7},{6,4},{7,5},{8,10},{9,11},{10,... | collective-permute-start | bytes 344072 | tf_op jit(solution)/shard_map/ppermute | solution.py:64
  24.5 5.9 %collective-permute-start.7 = (bf16[32,1536]{1,0:T(8,128)(2,1)S(1)}, bf16[32,1536]{1,0:T(8,128)(2,1)S(1)}, u32[]{:S(2)}, u32[]{:S(2)}) collective-permute-start(bf16[32,1536]{1,0:T(8,128)(2,1)S(1)} %get-tuple-element.32), channel_id=1, source_target_pairs={{0,24},{1,25},{2,26},{3,27},{4,28},{5,29},{6,30},{7,31},{8,16},{9,... | collective-permute-start | bytes 294920 | tf_op jit(solution)/shard_map/ppermute | solution.py:83
  26.7 4.8 %collective-permute-start.8 = (bf16[32,1536]{1,0:T(8,128)(2,1)S(1)}, bf16[32,1536]{1,0:T(8,128)(2,1)S(1)}, u32[]{:S(2)}, u32[]{:S(2)}) collective-permute-start(bf16[32,1536]{1,0:T(8,128)(2,1)S(1)} %get-tuple-element.33), channel_id=1, source_target_pairs={{0,16},{1,9},{2,18},{3,11},{4,20},{5,13},{6,22},{7,15},{8,24},{9,1... | collective-permute-start | bytes 294920 | tf_op jit(solution)/shard_map/ppermute | solution.py:83
  27.4 4.6 %collective-permute-start.9 = (bf16[32,1536]{1,0:T(8,128)(2,1)S(1)}, bf16[32,1536]{1,0:T(8,128)(2,1)S(1)}, u32[]{:S(2)}, u32[]{:S(2)}) collective-permute-start(bf16[32,1536]{1,0:T(8,128)(2,1)S(1)} %get-tuple-element.34), channel_id=1, source_target_pairs={{0,8},{1,17},{2,10},{3,19},{4,12},{5,21},{6,14},{7,23},{8,0},{9,25... | collective-permute-start | bytes 294920 | tf_op jit(solution)/shard_map/ppermute | solution.py:83
  32.1 5.9 %collective-permute-start.12 = (bf16[32,1536]{1,0:T(8,128)(2,1)S(1)}, bf16[32,1536]{1,0:T(8,128)(2,1)S(1)}, u32[]{:S(2)}, u32[]{:S(2)}) collective-permute-start(bf16[32,1536]{1,0:T(8,128)(2,1)S(1)} %activations.1.refs_0_.refs_1_.refs_2_), channel_id=1, source_target_pairs={{0,24},{1,25},{2,26},{3,27},{4,28},{5,29},{6,30},{7,31},{8,16},{9,... | collective-permute-start | bytes 294920 | tf_op jit(solution)/shard_map/ppermute | solution.py:83
  33.7 5.3 %collective-permute-start.11 = (bf16[32,1536]{1,0:T(8,128)(2,1)S(1)}, bf16[32,1536]{1,0:T(8,128)(2,1)S(1)}, u32[]{:S(2)}, u32[]{:S(2)}) collective-permute-start(bf16[32,1536]{1,0:T(8,128)(2,1)S(1)} %activations.1.refs_0_.refs_1_.refs_2_), channel_id=1, source_target_pairs={{0,16},{1,9},{2,18},{3,11},{4,20},{5,13},{6,22},{7,15},{8,24},{9,1... | collective-permute-start | bytes 294920 | tf_op jit(solution)/shard_map/ppermute | solution.py:83
  34.7 4.6 %collective-permute-start.10 = (bf16[32,1536]{1,0:T(8,128)(2,1)S(1)}, bf16[32,1536]{1,0:T(8,128)(2,1)S(1)}, u32[]{:S(2)}, u32[]{:S(2)}) collective-permute-start(bf16[32,1536]{1,0:T(8,128)(2,1)S(1)} %activations.1.refs_0_.refs_1_.refs_2_), channel_id=1, source_target_pairs={{0,8},{1,17},{2,10},{3,19},{4,12},{5,21},{6,14},{7,23},{8,0},{9,25... | collective-permute-start | bytes 294920 | tf_op jit(solution)/shard_map/ppermute | solution.py:83
  35.7 11.6 %collective-permute-start.13 = (bf16[256,896]{1,0:T(8,128)(2,1)S(1)}, bf16[256,896]{1,0:T(8,128)(2,1)S(1)}, u32[]{:S(2)}, u32[]{:S(2)}) collective-permute-start(bf16[256,896]{1,0:T(8,128)(2,1)S(1)} %get-tuple-element.35.refs_0_), channel_id=1, source_target_pairs={{0,1},{1,0},{2,3},{3,2},{4,5},{5,4},{6,7},{7,6},{8,9},{9,8},{10,11... | collective-permute-start | bytes 1376264 | tf_op jit(solution)/shard_map/ppermute | solution.py:64
  40.7 13.6 %all-to-all-start = ((bf16[16,8,896]{2,1,0:T(8,128)(2,1)}), bf16[16,8,896]{2,1,0:T(8,128)(2,1)S(1)}, u32[]{:S(2)}, u32[]{:S(2)}) async-start(bf16[16,8,896]{2,1,0:T(8,128)(2,1)} %bitcast.4), calls=%async_computation | async-start | bytes 458752 | tf_op jit(solution)/shard_map/all_to_all | solution.py:407
  45.7 1.5 %collective-permute-start.14 = (bf16[128,768]{1,0:T(8,128)(2,1)S(1)}, bf16[128,768]{1,0:T(8,128)(2,1)S(1)}, u32[]{:S(2)}, u32[]{:S(2)}) collective-permute-start(bf16[128,768]{1,0:T(8,128)(2,1)S(1)} %share.1.refs_0_), channel_id=1, source_target_pairs={{0,1},{1,0},{2,3},{3,2},{4,5},{5,4},{6,7},{7,6},{8,9},{9,8},{10,11... | collective-permute-start | bytes 589832 | tf_op jit(solution)/shard_map/ppermute | solution.py:64

commit v8 on v7

--- a/solution.py
+++ b/solution.py
@@ -71,6 +71,16 @@
 def partner(k):
     other = jnp.where(lax.axis_index("expert") % 2 == 1, crossed(k), k)
     return lax.axis_index("dp") ^ (k if crossed(k) == k else other)
+
+
+def neighbour(c, turn=0):
+    other = jnp.where((lax.axis_index("expert") + turn) % 2 == 1, crossed(c), c)
+    return (lax.axis_index("expert") // 2) ^ (c if crossed(c) == c else other)
+
+
+def swap_chip(x, c):
+    pairs = [(m, m ^ (2 * (crossed(c) if m % 2 else c))) for m in range(lax.axis_size("expert"))]
+    return lax.ppermute(x, "expert", pairs)
 
 
 def swap_slot(x, k):
@@ -222,7 +232,7 @@
         for i, result in enumerate(results):
             cut = slice((3 * half + i) * hid, (3 * half + i + 1) * hid)
             for c in range(chips):
-                ordered[(lax.axis_index("expert") // 2) ^ c, :, cut] = rows_of(result, c * ROWS)
+                ordered[neighbour(c), :, cut] = rows_of(result, c * ROWS)
     out[...] = jnp.concatenate([ordered[c] for c in range(chips)], axis=0).astype(BF16)
 
 
@@ -277,7 +287,7 @@
             for c in range(chips):
                 blocks[i, k * chips + c] = rows_of(wide, c * ROWS)
     order = [
-        blocks[i, k * chips + ((lax.axis_index("expert") // 2) ^ c)]
+        blocks[i, k * chips + neighbour(c, i)]
         for i in range(2)
         for c in range(chips)
         for k in range(groups)
@@ -348,7 +358,7 @@
     chunks = [chunk_of(parts, experts, member // HSH)]
     for c in range(1, chips):
         out = chunks[0] if experts == 1 else chunk_of(parts, experts, (member ^ (2 * c)) // HSH)
-        chunks.append(swap(out, "expert", 2 * c))
+        chunks.append(swap_chip(out, c))
 
     tall = depth + hid * len(pieces(depth, 2 * hid))
     gate_up, down, packed = call(

time: 55.8 us -> 56.9 us (1.020)
  waiting for transfers between devices: 25.2 us -> 26.1 us
    ppermute x0 -> x3, waiting for transfers between devices: none -> 7.56 us  [swap_chip(): return lax.ppermute(x, 'expert', pairs)]
    ppermute x6 -> x3, waiting for transfers between devices: 8.61 us -> 1.43 us  [swap(): lax.ppermute(x, axis, [(i, i ^ k) for i in range(lax.axis_size(axis))])]
    ppermute x0 -> x3, starting transfers between devices: none -> 4.45 us  [swap_chip(): return lax.ppermute(x, 'expert', pairs)]
    ppermute x6 -> x3, starting transfers between devices: 4.6 us -> 0.14 us  [swap(): lax.ppermute(x, axis, [(i, i ^ k) for i in range(lax.axis_size(axis))])]
    all_to_all x1, waiting for transfers between devices: 5.47 us -> 6.27 us  [on_device(): lax.all_to_all(dx, ('dp', 'expert'), split_axis=0, concat_axis=0, axis_in...]
where the time goes in v8:
time: 56.9 us; the launch traced here: 56.7 us
  waiting for transfers between devices  26.1 us (46%)
  starting transfers between devices  21.6 us (38%)
  Pallas kernels  6.59 us (12%)
  between operations  2.27 us (4%)
    ppermute x9, starting transfers between devices, swap_slot(): return lax.ppermute(x, ('dp', 'expert'), pairs)  11.7 us
    ppermute x9, waiting for transfers between devices, swap_slot(): return lax.ppermute(x, ('dp', 'expert'), pairs)  10.8 us
    ppermute x3, waiting for transfers between devices, swap_chip(): return lax.ppermute(x, 'expert', pairs)  7.56 us
    pallas_call x10, Pallas kernels, call(): pl.pallas_call(body, out_shape=outs, in_specs=[pl.BlockSpec(memory_space=...  6.59 us
    all_to_all x1, waiting for transfers between devices, on_device(): lax.all_to_all(dx, ('dp', 'expert'), split_axis=0, concat_axis=0, axis_in...  6.27 us
    all_to_all x1, starting transfers between devices, on_device(): lax.all_to_all(dx, ('dp', 'expert'), split_axis=0, concat_axis=0, axis_in...  5.35 us
    ppermute x3, starting transfers between devices, swap_chip(): return lax.ppermute(x, 'expert', pairs)  4.45 us
    ppermute x3, waiting for transfers between devices, swap(): lax.ppermute(x, axis, [(i, i ^ k) for i in range(lax.axis_size(axis))])  1.43 us
  transfers between devices with their start and end apart: 16, of which 13 were waited for; matrix products, arithmetic and copies ran while one was open for 0% of the time, Pallas kernels for 7%

profile of v8, /device:TPU:0, one launch (start us, length us, event | category | flops | bytes accessed | tf_op | source)
XLA Modules:
  0.0 56.7 jit_solution(6835334114105683162)
XLA Ops:
  2.1 0.0 copy-start.2
  2.1 0.0 copy-start.3
  2.1 0.0 copy-start.4
  2.1 0.0 copy-start.7
  2.2 0.0 copy-start.8
  2.2 0.0 copy-start.9
  2.2 0.2 lists.1
  2.4 0.0 copy-done
  2.4 0.4 route.1
  2.8 3.0 %collective-permute-start = (bf16[16,896]{1,0:T(8,128)(2,1)S(1)}, bf16[16,896]{1,0:T(8,128)(2,1)S(1)}, u32[]{:S(2)}, u32[]{:S(2)}) collective-permute-start(bf16[16,896]{1,0:T(8,128)(2,1)S(1)} %get-tuple-element.25), channel_id=1, source_target_pairs={{0,8},{1,17},{2,10},{3,19},{4,12},{5,21},{6,14},{7,23},{8,0},{9,25... | collective-permute-start | bytes 86024 | tf_op jit(solution)/shard_map/ppermute | solution.py:93
  5.8 1.5 %collective-permute-start.1 = (bf16[16,896]{1,0:T(8,128)(2,1)S(1)}, bf16[16,896]{1,0:T(8,128)(2,1)S(1)}, u32[]{:S(2)}, u32[]{:S(2)}) collective-permute-start(bf16[16,896]{1,0:T(8,128)(2,1)S(1)} %get-tuple-element.26), channel_id=1, source_target_pairs={{0,16},{1,9},{2,18},{3,11},{4,20},{5,13},{6,22},{7,15},{8,24},{9,1... | collective-permute-start | bytes 86024 | tf_op jit(solution)/shard_map/ppermute | solution.py:93
  7.4 0.0 collective-permute-start.2
  7.4 0.3 collective-permute-done.refs_3_
  7.7 0.0 copy-done.4
  7.7 1.0 %weights.1 = (bf16[896,512]{1,0:T(8,128)(2,1)S(1)}, bf16[256,896]{1,0:T(8,128)(2,1)S(1)}, bf16[1408,512]{1,0:T(8,128)(2,1)S(1)}) custom-call(f32[2,28]{1,0:T(2,128)S(1)} %bitcast.7, f32[2,28]{1,0:T(2,128)S(1)} %bitcast.8, f32[2,28]{1,0:T(2,128)S(1)} %copy-done.9, bf16[16,896]{1,0:T(8,128)(2,1)S(1)} %collective-permute-done.refs_3_, ...), custom_call_target="tpu_custom_call" | custom-call | flops 1376256 | bytes 4194304 | tf_op jit(solution)/shard_map/weights/pallas_call | solution.py:37
  8.8 0.1 collective-permute-start.6
  8.9 0.8 %collective-permute-done.1 = bf16[16,896]{1,0:T(8,128)(2,1)S(1)} collective-permute-done((bf16[16,896]{1,0:T(8,128)(2,1)S(1)}, bf16[16,896]{1,0:T(8,128)(2,1)S(1)}, u32[]{:S(2)}, u32[]{:S(2)}) %collective-permute-start.1) | collective-permute-done | bytes 28704 | tf_op jit(solution)/shard_map/ppermute | solution.py:93
  9.7 2.4 %collective-permute-done.2 = bf16[16,896]{1,0:T(8,128)(2,1)S(1)} collective-permute-done((bf16[16,896]{1,0:T(8,128)(2,1)S(1)}, bf16[16,896]{1,0:T(8,128)(2,1)S(1)}, u32[]{:S(2)}, u32[]{:S(2)}) %collective-permute-start.2) | collective-permute-done | bytes 28704 | tf_op jit(solution)/shard_map/ppermute | solution.py:93
  12.2 3.7 %collective-permute-start.5 = (bf16[64,896]{1,0:T(8,128)(2,1)S(1)}, bf16[64,896]{1,0:T(8,128)(2,1)S(1)}, u32[]{:S(2)}, u32[]{:S(2)}) collective-permute-start(bf16[64,896]{1,0:T(8,128)(2,1)S(1)} %constant_dynamic-update-slice_fusion.refs_0_), channel_id=1, source_target_pairs={{0,6},{1,7},{2,4},{3,5},{4,2},{5,3},{6,0},{7,1},{8,14},{9,15},{10,... | collective-permute-start | bytes 344072 | tf_op jit(solution)/shard_map/ppermute | solution.py:83
  15.8 0.0 collective-permute-start.4
  15.8 0.8 %collective-permute-start.3 = (bf16[64,896]{1,0:T(8,128)(2,1)S(1)}, bf16[64,896]{1,0:T(8,128)(2,1)S(1)}, u32[]{:S(2)}, u32[]{:S(2)}) collective-permute-start(bf16[64,896]{1,0:T(8,128)(2,1)S(1)} %constant_dynamic-update-slice_fusion.refs_0_), channel_id=1, source_target_pairs={{0,2},{1,5},{2,0},{3,7},{4,6},{5,1},{6,4},{7,3},{8,10},{9,13},{10,... | collective-permute-start | bytes 344072 | tf_op jit(solution)/shard_map/ppermute | solution.py:83
  16.6 2.8 %collective-permute-done.5.refs_3_ = bf16[64,896]{1,0:T(8,128)(2,1)S(1)} collective-permute-done((bf16[64,896]{1,0:T(8,128)(2,1)S(1)}, bf16[64,896]{1,0:T(8,128)(2,1)S(1)}, u32[]{:S(2)}, u32[]{:S(2)}) %collective-permute-start.5) | collective-permute-done | bytes 114720 | tf_op jit(solution)/shard_map/ppermute | solution.py:83
  19.4 4.7 %collective-permute-done.4.refs_2_ = bf16[64,896]{1,0:T(8,128)(2,1)S(1)} collective-permute-done((bf16[64,896]{1,0:T(8,128)(2,1)S(1)}, bf16[64,896]{1,0:T(8,128)(2,1)S(1)}, u32[]{:S(2)}, u32[]{:S(2)}) %collective-permute-start.4) | collective-permute-done | bytes 114720 | tf_op jit(solution)/shard_map/ppermute | solution.py:83
  24.2 0.0 collective-permute-done.3.refs_1_
  24.2 0.0 collective-permute-done.6.refs_6_
  24.2 0.7 %partial.1 = (f32[32,1536]{1,0:T(8,128)S(1)}, bf16[32,1536]{1,0:T(8,128)(2,1)S(1)}, bf16[32,1536]{1,0:T(8,128)(2,1)S(1)}, bf16[32,1536]{1,0:T(8,128)(2,1)S(1)}, bf16[256,896]{1,0:T(8,128)(2,1)S(1)}) custom-call(bf16[64,896]{1,0:T(8,128)(2,1)S(1)} %constant_dynamic-update-slice_fusion.refs_0_, bf16[64,896]{1,0:T(8,128)(2,1)S(1)} %collective-permute-done.3.refs_1_, ...), custom_call_target="tpu_custom_call" | custom-call | flops 352321536 | bytes 4227072 | tf_op jit(solution)/shard_map/partial/pallas_call | solution.py:37
  24.9 1.8 %collective-permute-start.7 = (bf16[32,1536]{1,0:T(8,128)(2,1)S(1)}, bf16[32,1536]{1,0:T(8,128)(2,1)S(1)}, u32[]{:S(2)}, u32[]{:S(2)}) collective-permute-start(bf16[32,1536]{1,0:T(8,128)(2,1)S(1)} %get-tuple-element.32), channel_id=1, source_target_pairs={{0,24},{1,25},{2,26},{3,27},{4,28},{5,29},{6,30},{7,31},{8,16},{9,... | collective-permute-start | bytes 294920 | tf_op jit(solution)/shard_map/ppermute | solution.py:93
  26.7 0.7 %collective-permute-start.8 = (bf16[32,1536]{1,0:T(8,128)(2,1)S(1)}, bf16[32,1536]{1,0:T(8,128)(2,1)S(1)}, u32[]{:S(2)}, u32[]{:S(2)}) collective-permute-start(bf16[32,1536]{1,0:T(8,128)(2,1)S(1)} %get-tuple-element.33), channel_id=1, source_target_pairs={{0,16},{1,9},{2,18},{3,11},{4,20},{5,13},{6,22},{7,15},{8,24},{9,1... | collective-permute-start | bytes 294920 | tf_op jit(solution)/shard_map/ppermute | solution.py:93
  27.4 1.0 %collective-permute-start.9 = (bf16[32,1536]{1,0:T(8,128)(2,1)S(1)}, bf16[32,1536]{1,0:T(8,128)(2,1)S(1)}, u32[]{:S(2)}, u32[]{:S(2)}) collective-permute-start(bf16[32,1536]{1,0:T(8,128)(2,1)S(1)} %get-tuple-element.34), channel_id=1, source_target_pairs={{0,8},{1,17},{2,10},{3,19},{4,12},{5,21},{6,14},{7,23},{8,0},{9,25... | collective-permute-start | bytes 294920 | tf_op jit(solution)/shard_map/ppermute | solution.py:93
  28.4 2.4 %collective-permute-done.7.refs_1_ = bf16[32,1536]{1,0:T(8,128)(2,1)S(1)} collective-permute-done((bf16[32,1536]{1,0:T(8,128)(2,1)S(1)}, bf16[32,1536]{1,0:T(8,128)(2,1)S(1)}, u32[]{:S(2)}, u32[]{:S(2)}) %collective-permute-start.7) | collective-permute-done | bytes 98336 | tf_op jit(solution)/shard_map/ppermute | solution.py:93
  30.9 1.1 %collective-permute-done.8.refs_2_ = bf16[32,1536]{1,0:T(8,128)(2,1)S(1)} collective-permute-done((bf16[32,1536]{1,0:T(8,128)(2,1)S(1)}, bf16[32,1536]{1,0:T(8,128)(2,1)S(1)}, u32[]{:S(2)}, u32[]{:S(2)}) %collective-permute-start.8) | collective-permute-done | bytes 98336 | tf_op jit(solution)/shard_map/ppermute | solution.py:93
  32.0 0.1 collective-permute-done.9.refs_3_
  32.0 0.1 activations.1.refs_0_.refs_1_.refs_2_
  32.1 1.6 %collective-permute-start.12 = (bf16[32,1536]{1,0:T(8,128)(2,1)S(1)}, bf16[32,1536]{1,0:T(8,128)(2,1)S(1)}, u32[]{:S(2)}, u32[]{:S(2)}) collective-permute-start(bf16[32,1536]{1,0:T(8,128)(2,1)S(1)} %activations.1.refs_0_.refs_1_.refs_2_), channel_id=1, source_target_pairs={{0,24},{1,25},{2,26},{3,27},{4,28},{5,29},{6,30},{7,31},{8,16},{9,... | collective-permute-start | bytes 294920 | tf_op jit(solution)/shard_map/ppermute | solution.py:93
  33.7 1.0 %collective-permute-start.11 = (bf16[32,1536]{1,0:T(8,128)(2,1)S(1)}, bf16[32,1536]{1,0:T(8,128)(2,1)S(1)}, u32[]{:S(2)}, u32[]{:S(2)}) collective-permute-start(bf16[32,1536]{1,0:T(8,128)(2,1)S(1)} %activations.1.refs_0_.refs_1_.refs_2_), channel_id=1, source_target_pairs={{0,16},{1,9},{2,18},{3,11},{4,20},{5,13},{6,22},{7,15},{8,24},{9,1... | collective-permute-start | bytes 294920 | tf_op jit(solution)/shard_map/ppermute | solution.py:93
  34.7 0.9 %collective-permute-start.10 = (bf16[32,1536]{1,0:T(8,128)(2,1)S(1)}, bf16[32,1536]{1,0:T(8,128)(2,1)S(1)}, u32[]{:S(2)}, u32[]{:S(2)}) collective-permute-start(bf16[32,1536]{1,0:T(8,128)(2,1)S(1)} %activations.1.refs_0_.refs_1_.refs_2_), channel_id=1, source_target_pairs={{0,8},{1,17},{2,10},{3,19},{4,12},{5,21},{6,14},{7,23},{8,0},{9,25... | collective-permute-start | bytes 294920 | tf_op jit(solution)/shard_map/ppermute | solution.py:93
  35.7 0.0 collective-permute-start.13
  35.7 2.5 %collective-permute-done.12.refs_3_.refs_4_.refs_5_ = bf16[32,1536]{1,0:T(8,128)(2,1)S(1)} collective-permute-done((bf16[32,1536]{1,0:T(8,128)(2,1)S(1)}, bf16[32,1536]{1,0:T(8,128)(2,1)S(1)}, u32[]{:S(2)}, u32[]{:S(2)}) %collective-permute-start.12) | collective-permute-done | bytes 98336 | tf_op jit(solution)/shard_map/ppermute | solution.py:93
  38.1 1.0 %collective-permute-done.11.refs_2_.refs_3_.refs_4_ = bf16[32,1536]{1,0:T(8,128)(2,1)S(1)} collective-permute-done((bf16[32,1536]{1,0:T(8,128)(2,1)S(1)}, bf16[32,1536]{1,0:T(8,128)(2,1)S(1)}, u32[]{:S(2)}, u32[]{:S(2)}) %collective-permute-start.11) | collective-permute-done | bytes 98336 | tf_op jit(solution)/shard_map/ppermute | solution.py:93
  39.1 0.3 collective-permute-done.10.refs_1_.refs_2_.refs_3_
  39.4 1.4 %dx.1 = bf16[4,32,896]{2,1,0:T(8,128)(2,1)} custom-call(bf16[128,768]{1,0:T(8,128)(2,1)S(1)} %share.1.refs_0_, bf16[32,1536]{1,0:T(8,128)(2,1)S(1)} %activations.1.refs_0_.refs_1_.refs_2_, bf16[32,1536]{1,0:T(8,128)(2,1)S(1)} %collective-permute-done.10.refs_1_.refs_2_.refs_3_, bf16[32,1536]{1,0:T(8,128)(2,1)S(1)} %collective-permute-done.11.refs_2_.refs_3_.refs_4_, ...), custom_call_target="tpu_custom_call" | custom-call | flops 234881024 | bytes 2981888 | tf_op jit(solution)/shard_map/dx/pallas_call | solution.py:37
  40.8 5.3 %all-to-all-start = ((bf16[16,8,896]{2,1,0:T(8,128)(2,1)}), bf16[16,8,896]{2,1,0:T(8,128)(2,1)S(1)}, u32[]{:S(2)}, u32[]{:S(2)}) async-start(bf16[16,8,896]{2,1,0:T(8,128)(2,1)} %bitcast.4), calls=%async_computation | async-start | bytes 458752 | tf_op jit(solution)/shard_map/all_to_all | solution.py:417
  46.1 0.1 collective-permute-start.14
  46.2 1.4 %collective-permute-done.14.refs_6_ = bf16[128,768]{1,0:T(8,128)(2,1)S(1)} collective-permute-done((bf16[128,768]{1,0:T(8,128)(2,1)S(1)}, bf16[128,768]{1,0:T(8,128)(2,1)S(1)}, u32[]{:S(2)}, u32[]{:S(2)}) %collective-permute-start.14) | collective-permute-done | bytes 196640 | tf_op jit(solution)/shard_map/ppermute | solution.py:64
  47.6 0.0 collective-permute-done.13.refs_1_
  47.6 1.5 %gradients.1 = (bf16[896,256]{1,0:T(8,128)(2,1)}, bf16[896,256]{1,0:T(8,128)(2,1)}, bf16[256,896]{1,0:T(8,128)(2,1)}, f32[8,128]{1,0:T(8,128)S(1)}) custom-call(bf16[256,896]{1,0:T(8,128)(2,1)S(1)} %get-tuple-element.35.refs_0_, bf16[256,896]{1,0:T(8,128)(2,1)S(1)} %collective-permute-done.13.refs_1_, ...), custom_call_target="tpu_custom_call" | custom-call | flops 352321536 | bytes 2887680 | tf_op jit(solution)/shard_map/gradients/pallas_call | solution.py:37
  49.2 6.3 %all-to-all-done.refs_0_ = bf16[16,8,896]{2,1,0:T(8,128)(2,1)S(1)} async-done(((bf16[16,8,896]{2,1,0:T(8,128)(2,1)}), bf16[16,8,896]{2,1,0:T(8,128)(2,1)S(1)}, u32[]{:S(2)}, u32[]{:S(2)}) %all-to-all-start) | async-done | bytes 229408 | tf_op jit(solution)/shard_map/all_to_all | solution.py:417
  55.4 1.2 %place.1 = bf16[128,3584]{1,0:T(8,128)(2,1)} custom-call(bf16[16,8,896]{2,1,0:T(8,128)(2,1)S(1)} %all-to-all-done.refs_0_, f32[1,8,128]{2,1,0:T(8,128)S(1)} %get-tuple-element.22.refs_0_.refs_1_, f32[8,128]{1,0:T(8,128)S(1)} %get-tuple-element.36.refs_2_), custom_call_target="tpu_custom_call" | custom-call | flops 7340032 | bytes 1155072 | tf_op jit(solution)/shard_map/place/pallas_call | solution.py:37
  (22 shorter events, 0.1 us)
Async XLA Ops:
  0.6 1.6 %copy-start.5 = (s32[128,8]{0,1:T(8,128)S(1)}, s32[128,8]{0,1:T(8,128)}, u32[]{:S(2)}) copy-start(s32[128,8]{0,1:T(8,128)} %param.15) | copy-start | bytes 12292
  0.6 1.6 %copy-start.6 = (f32[128,8]{0,1:T(8,128)S(1)}, f32[128,8]{0,1:T(8,128)}, u32[]{:S(2)}) copy-start(f32[128,8]{0,1:T(8,128)} %param.14) | copy-start | bytes 12292
  0.7 1.8 %copy-start.1 = (bf16[128,3584]{1,0:T(8,128)(2,1)S(1)}, bf16[128,3584]{1,0:T(8,128)(2,1)}, u32[]{:S(2)}) copy-start(bf16[128,3584]{1,0:T(8,128)(2,1)} %refs_3_.1) | copy-start | bytes 2752516
  0.7 1.8 %copy-start = (bf16[128,3584]{1,0:T(8,128)(2,1)S(1)}, bf16[128,3584]{1,0:T(8,128)(2,1)}, u32[]{:S(2)}) copy-start(bf16[128,3584]{1,0:T(8,128)(2,1)} %refs_2_.2) | copy-start | bytes 2752516
  2.1 5.6 %copy-start.2 = (bf16[896,256]{1,0:T(8,128)(2,1)S(1)}, bf16[896,256]{1,0:T(8,128)(2,1)}, u32[]{:S(2)}) copy-start(bf16[896,256]{1,0:T(8,128)(2,1)} %refs_4_.1) | copy-start | bytes 1376260
  2.1 5.6 %copy-start.3 = (bf16[896,256]{1,0:T(8,128)(2,1)S(1)}, bf16[896,256]{1,0:T(8,128)(2,1)}, u32[]{:S(2)}) copy-start(bf16[896,256]{1,0:T(8,128)(2,1)} %refs_5_.1) | copy-start | bytes 1376260
  2.1 5.6 %copy-start.4 = (bf16[256,896]{1,0:T(8,128)(2,1)S(1)}, bf16[256,896]{1,0:T(8,128)(2,1)}, u32[]{:S(2)}) copy-start(bf16[256,896]{1,0:T(8,128)(2,1)} %refs_6_.1) | copy-start | bytes 1376260
  2.1 5.5 %copy-start.7 = (f32[28,2]{0,1:T(2,128)S(1)}, f32[28,2]{0,1:T(2,128)}, u32[]{:S(2)}) copy-start(f32[28,2]{0,1:T(2,128)} %param.21) | copy-start | bytes 676
  2.2 5.5 %copy-start.8 = (f32[28,2]{0,1:T(2,128)S(1)}, f32[28,2]{0,1:T(2,128)}, u32[]{:S(2)}) copy-start(f32[28,2]{0,1:T(2,128)} %param.22) | copy-start | bytes 676
  2.2 5.5 %copy-start.9 = (f32[2,28]{1,0:T(2,128)S(1)}, f32[2,28]{1,0:T(2,128)}, u32[]{:S(2)}) copy-start(f32[2,28]{1,0:T(2,128)} %refs_2_.3) | copy-start | bytes 676
  2.8 4.9 %collective-permute-start = (bf16[16,896]{1,0:T(8,128)(2,1)S(1)}, bf16[16,896]{1,0:T(8,128)(2,1)S(1)}, u32[]{:S(2)}, u32[]{:S(2)}) collective-permute-start(bf16[16,896]{1,0:T(8,128)(2,1)S(1)} %get-tuple-element.25), channel_id=1, source_target_pairs={{0,8},{1,17},{2,10},{3,19},{4,12},{5,21},{6,14},{7,23},{8,0},{9,25... | collective-permute-start | bytes 86024 | tf_op jit(solution)/shard_map/ppermute | solution.py:93
  5.8 3.9 %collective-permute-start.1 = (bf16[16,896]{1,0:T(8,128)(2,1)S(1)}, bf16[16,896]{1,0:T(8,128)(2,1)S(1)}, u32[]{:S(2)}, u32[]{:S(2)}) collective-permute-start(bf16[16,896]{1,0:T(8,128)(2,1)S(1)} %get-tuple-element.26), channel_id=1, source_target_pairs={{0,16},{1,9},{2,18},{3,11},{4,20},{5,13},{6,22},{7,15},{8,24},{9,1... | collective-permute-start | bytes 86024 | tf_op jit(solution)/shard_map/ppermute | solution.py:93
  7.4 4.8 %collective-permute-start.2 = (bf16[16,896]{1,0:T(8,128)(2,1)S(1)}, bf16[16,896]{1,0:T(8,128)(2,1)S(1)}, u32[]{:S(2)}, u32[]{:S(2)}) collective-permute-start(bf16[16,896]{1,0:T(8,128)(2,1)S(1)} %get-tuple-element.27), channel_id=1, source_target_pairs={{0,24},{1,25},{2,26},{3,27},{4,28},{5,29},{6,30},{7,31},{8,16},{9,... | collective-permute-start | bytes 86024 | tf_op jit(solution)/shard_map/ppermute | solution.py:93
  8.8 15.4 %collective-permute-start.6 = (bf16[1408,512]{1,0:T(8,128)(2,1)S(1)}, bf16[1408,512]{1,0:T(8,128)(2,1)S(1)}, u32[]{:S(2)}, u32[]{:S(2)}) collective-permute-start(bf16[1408,512]{1,0:T(8,128)(2,1)S(1)} %get-tuple-element.30), channel_id=1, source_target_pairs={{0,1},{1,0},{2,3},{3,2},{4,5},{5,4},{6,7},{7,6},{8,9},{9,8},{10,11... | collective-permute-start | bytes 4325384 | tf_op jit(solution)/shard_map/ppermute | solution.py:64
  12.2 7.3 %collective-permute-start.5 = (bf16[64,896]{1,0:T(8,128)(2,1)S(1)}, bf16[64,896]{1,0:T(8,128)(2,1)S(1)}, u32[]{:S(2)}, u32[]{:S(2)}) collective-permute-start(bf16[64,896]{1,0:T(8,128)(2,1)S(1)} %constant_dynamic-update-slice_fusion.refs_0_), channel_id=1, source_target_pairs={{0,6},{1,7},{2,4},{3,5},{4,2},{5,3},{6,0},{7,1},{8,14},{9,15},{10,... | collective-permute-start | bytes 344072 | tf_op jit(solution)/shard_map/ppermute | solution.py:83
  15.8 8.3 %collective-permute-start.4 = (bf16[64,896]{1,0:T(8,128)(2,1)S(1)}, bf16[64,896]{1,0:T(8,128)(2,1)S(1)}, u32[]{:S(2)}, u32[]{:S(2)}) collective-permute-start(bf16[64,896]{1,0:T(8,128)(2,1)S(1)} %constant_dynamic-update-slice_fusion.refs_0_), channel_id=1, source_target_pairs={{0,4},{1,3},{2,6},{3,1},{4,0},{5,7},{6,2},{7,5},{8,12},{9,11},{10,... | collective-permute-start | bytes 344072 | tf_op jit(solution)/shard_map/ppermute | solution.py:83
  15.8 8.3 %collective-permute-start.3 = (bf16[64,896]{1,0:T(8,128)(2,1)S(1)}, bf16[64,896]{1,0:T(8,128)(2,1)S(1)}, u32[]{:S(2)}, u32[]{:S(2)}) collective-permute-start(bf16[64,896]{1,0:T(8,128)(2,1)S(1)} %constant_dynamic-update-slice_fusion.refs_0_), channel_id=1, source_target_pairs={{0,2},{1,5},{2,0},{3,7},{4,6},{5,1},{6,4},{7,3},{8,10},{9,13},{10,... | collective-permute-start | bytes 344072 | tf_op jit(solution)/shard_map/ppermute | solution.py:83
  24.9 6.0 %collective-permute-start.7 = (bf16[32,1536]{1,0:T(8,128)(2,1)S(1)}, bf16[32,1536]{1,0:T(8,128)(2,1)S(1)}, u32[]{:S(2)}, u32[]{:S(2)}) collective-permute-start(bf16[32,1536]{1,0:T(8,128)(2,1)S(1)} %get-tuple-element.32), channel_id=1, source_target_pairs={{0,24},{1,25},{2,26},{3,27},{4,28},{5,29},{6,30},{7,31},{8,16},{9,... | collective-permute-start | bytes 294920 | tf_op jit(solution)/shard_map/ppermute | solution.py:93
  26.7 5.3 %collective-permute-start.8 = (bf16[32,1536]{1,0:T(8,128)(2,1)S(1)}, bf16[32,1536]{1,0:T(8,128)(2,1)S(1)}, u32[]{:S(2)}, u32[]{:S(2)}) collective-permute-start(bf16[32,1536]{1,0:T(8,128)(2,1)S(1)} %get-tuple-element.33), channel_id=1, source_target_pairs={{0,16},{1,9},{2,18},{3,11},{4,20},{5,13},{6,22},{7,15},{8,24},{9,1... | collective-permute-start | bytes 294920 | tf_op jit(solution)/shard_map/ppermute | solution.py:93
  27.4 4.6 %collective-permute-start.9 = (bf16[32,1536]{1,0:T(8,128)(2,1)S(1)}, bf16[32,1536]{1,0:T(8,128)(2,1)S(1)}, u32[]{:S(2)}, u32[]{:S(2)}) collective-permute-start(bf16[32,1536]{1,0:T(8,128)(2,1)S(1)} %get-tuple-element.34), channel_id=1, source_target_pairs={{0,8},{1,17},{2,10},{3,19},{4,12},{5,21},{6,14},{7,23},{8,0},{9,25... | collective-permute-start | bytes 294920 | tf_op jit(solution)/shard_map/ppermute | solution.py:93
  32.1 6.0 %collective-permute-start.12 = (bf16[32,1536]{1,0:T(8,128)(2,1)S(1)}, bf16[32,1536]{1,0:T(8,128)(2,1)S(1)}, u32[]{:S(2)}, u32[]{:S(2)}) collective-permute-start(bf16[32,1536]{1,0:T(8,128)(2,1)S(1)} %activations.1.refs_0_.refs_1_.refs_2_), channel_id=1, source_target_pairs={{0,24},{1,25},{2,26},{3,27},{4,28},{5,29},{6,30},{7,31},{8,16},{9,... | collective-permute-start | bytes 294920 | tf_op jit(solution)/shard_map/ppermute | solution.py:93
  33.7 5.4 %collective-permute-start.11 = (bf16[32,1536]{1,0:T(8,128)(2,1)S(1)}, bf16[32,1536]{1,0:T(8,128)(2,1)S(1)}, u32[]{:S(2)}, u32[]{:S(2)}) collective-permute-start(bf16[32,1536]{1,0:T(8,128)(2,1)S(1)} %activations.1.refs_0_.refs_1_.refs_2_), channel_id=1, source_target_pairs={{0,16},{1,9},{2,18},{3,11},{4,20},{5,13},{6,22},{7,15},{8,24},{9,1... | collective-permute-start | bytes 294920 | tf_op jit(solution)/shard_map/ppermute | solution.py:93
  34.7 4.6 %collective-permute-start.10 = (bf16[32,1536]{1,0:T(8,128)(2,1)S(1)}, bf16[32,1536]{1,0:T(8,128)(2,1)S(1)}, u32[]{:S(2)}, u32[]{:S(2)}) collective-permute-start(bf16[32,1536]{1,0:T(8,128)(2,1)S(1)} %activations.1.refs_0_.refs_1_.refs_2_), channel_id=1, source_target_pairs={{0,8},{1,17},{2,10},{3,19},{4,12},{5,21},{6,14},{7,23},{8,0},{9,25... | collective-permute-start | bytes 294920 | tf_op jit(solution)/shard_map/ppermute | solution.py:93
  35.7 12.0 %collective-permute-start.13 = (bf16[256,896]{1,0:T(8,128)(2,1)S(1)}, bf16[256,896]{1,0:T(8,128)(2,1)S(1)}, u32[]{:S(2)}, u32[]{:S(2)}) collective-permute-start(bf16[256,896]{1,0:T(8,128)(2,1)S(1)} %get-tuple-element.35.refs_0_), channel_id=1, source_target_pairs={{0,1},{1,0},{2,3},{3,2},{4,5},{5,4},{6,7},{7,6},{8,9},{9,8},{10,11... | collective-permute-start | bytes 1376264 | tf_op jit(solution)/shard_map/ppermute | solution.py:64
  40.8 14.7 %all-to-all-start = ((bf16[16,8,896]{2,1,0:T(8,128)(2,1)}), bf16[16,8,896]{2,1,0:T(8,128)(2,1)S(1)}, u32[]{:S(2)}, u32[]{:S(2)}) async-start(bf16[16,8,896]{2,1,0:T(8,128)(2,1)} %bitcast.4), calls=%async_computation | async-start | bytes 458752 | tf_op jit(solution)/shard_map/all_to_all | solution.py:417
  46.1 1.5 %collective-permute-start.14 = (bf16[128,768]{1,0:T(8,128)(2,1)S(1)}, bf16[128,768]{1,0:T(8,128)(2,1)S(1)}, u32[]{:S(2)}, u32[]{:S(2)}) collective-permute-start(bf16[128,768]{1,0:T(8,128)(2,1)S(1)} %share.1.refs_0_), channel_id=1, source_target_pairs={{0,1},{1,0},{2,3},{3,2},{4,5},{5,4},{6,7},{7,6},{8,9},{9,8},{10,11... | collective-permute-start | bytes 589832 | tf_op jit(solution)/shard_map/ppermute | solution.py:64
